TPU v7x, 32 devices: a whole 2x2x4 slice. The times are simulated.
32 devices in a mesh: xy: 4 (over y, core), gz: 8 (over z, x).
Axes of the slice: x: 2, y: 2, z: 4, core: 2. Of those that a mesh axis runs over, the one named last changes fastest.
Arguments:
- concentration: float32 [256, 64, 2048], P('gz', None, 'xy'), may hold values from -1 to 1
- geometry: float32 [2, 2048], P(None, 'xy'), may hold values from 0.5 to 2
- nbr_elem: int32 [4, 2048], P(None, 'xy'), may hold values from -1 to 2047, as said below
- nbr_edge: int32 [4, 2048], P(None, 'xy'), may hold values from 0 to 7, as said below
- wall_flags: int32 [256], P('gz'), may hold values 0 or 1
Outputs:
- modes: float32 [256, 64, 2048], P('gz', None, 'xy')
Inputs may be any that keep to these rules, and one draw needn't show every extreme that they name: `nbr_elem`: entry [a, e] is the global number of the element across local edge a of element e, or -1 where that edge lies on a wall of the slab; the pairing is mutual. The neighbour is held by the same index of xy or by the index just before or after it, wrapping around; an element with a neighbour on the index before is among the first 64 elements of its device, one with a neighbour on the index after is among the last 64. No element has more than one edge whose neighbour is held by another index of xy. `nbr_edge`: the neighbour's local edge, plus 4 where the two elements number the shared nodes in opposite orders; 0 at walls; the same pairing read from both sides.
All inputs are finite; a program needn't handle non-finite values. No bound on the sum of `wall_flags` on one device may be relied on, other than what follows from the above.
Results may differ from a plain program's by a relative error of at most 0.0001.
Values sent between devices are 32-bit elements; how exact they have to be, the bound alone decides.
No kernel may reach another device: no remote copies, remote signals or barrier semaphores. Data moves between devices by JAX's collectives and lax.ppermute only.
A program may use at most 128 MiB of HBM per device.

v0:
```python
import jax
import jax.numpy as jnp
import numpy as np
from jax import lax
from jax.sharding import PartitionSpec as P

ROWS = 64
ITERS = 2


time_step = 0.2
axial_stiffness = 0.002
plane_stiffness = 1.0
edge_penalty = 4.0
axial_mobility = 0.002
mobility_floor = 0.05
highest = lax.Precision.HIGHEST


def padded(x, sides, width):
    for axis, dim in sides:
        size, length = (lax.axis_size(axis), x.shape[dim])
        up = [(i, (i + 1) % size) for i in range(size)]
        down = [(j, i) for i, j in up]
        last = lax.slice_in_dim(x, length - width, length, axis=dim)
        initial = lax.slice_in_dim(x, 0, width, axis=dim)
        before = lax.ppermute(last, axis, up)
        after = lax.ppermute(initial, axis, down)
        x = jnp.concatenate([before, x, after], axis=dim)
    return x


def point_tables():
    degree = 7
    points = np.arange(degree + 1)
    theta = np.pi * points / degree
    nodes_x = np.cos(theta)
    signs = np.where((points == 0) | (points == degree), 2.0, 1.0) * (-1.0) ** points
    differ = nodes_x[:, None] - nodes_x[None, :]
    deriv = np.outer(signs, 1.0 / signs) / (differ + np.eye(degree + 1))
    deriv = deriv - np.eye(degree + 1) * deriv.sum(axis=1)[:, None]
    inner = np.ones(degree - 1)
    for number in range(1, (degree - 1) // 2 + 1):
        inner = inner - 2.0 * np.cos(2 * number * theta[1:degree]) / (4 * number * number - 1)
    weights = np.zeros(degree + 1)
    weights[1:degree] = 2.0 * inner / degree
    weights[0] = 1.0 / degree**2
    weights[degree] = 1.0 / degree**2
    return (deriv, weights)


def make_tables():
    deriv, weights = point_tables()
    grad_x = np.kron(np.eye(8), deriv)
    grad_y = np.kron(deriv, np.eye(8))
    mass_w = np.kron(weights, weights)
    return (
        jnp.asarray(grad_x, jnp.float32),
        jnp.asarray(grad_y, jnp.float32),
        jnp.asarray(mass_w, jnp.float32),
        jnp.asarray(weights, jnp.float32),
    )


def fourier_table(length):
    planes = np.arange(length)
    wave_no = (planes + 1) // 2
    phase = np.outer(wave_no, planes) % length * (2.0 * np.pi / length)
    table = np.where((planes % 2 == 1)[:, None], np.cos(phase), np.sin(phase)) * np.sqrt(
        2.0 / length
    )
    table[0] = 1.0 / np.sqrt(length)
    table[length - 1] = np.cos(phase[length - 1]) / np.sqrt(length)
    return table


def weak_flux(field, mobility, tables, jacobian, scale_x, scale_y):
    grad_x, grad_y, mass_w, edge_w = tables
    along_x = jnp.einsum("nm,ame->ane", grad_x, field, precision=highest)
    along_y = jnp.einsum("nm,ame->ane", grad_y, field, precision=highest)
    flux_x = mass_w[:, None] * mobility * along_x * (jacobian * scale_x * scale_x)
    flux_y = mass_w[:, None] * mobility * along_y * (jacobian * scale_y * scale_y)
    return jnp.einsum("mn,ame->ane", grad_x, flux_x, precision=highest) + jnp.einsum(
        "mn,ame->ane", grad_y, flux_y, precision=highest
    )


def plane_terms(field, tables, scale_x, scale_y):
    mass_w = tables[2]
    jacobian = 1.0 / (scale_x * scale_y)
    chem = field * field * field - field
    mobility = jnp.maximum(1.0 - field * field, mobility_floor)
    explicit = jacobian * mass_w[:, None] * field / time_step - weak_flux(
        chem, mobility, tables, jacobian, scale_x, scale_y
    )
    bulk = jacobian * mass_w[:, None] * chem
    return (explicit, bulk)


def edge_traces(field):
    grid = field.reshape(field.shape[0], 8, 8, field.shape[2])
    return jnp.stack(
        [grid[:, 0, :, :], grid[:, :, 7, :], grid[:, 7, :, :], grid[:, :, 0, :]], axis=2
    )


def add_edges(field, penalty):
    grid = field.reshape(field.shape[0], 8, 8, field.shape[2])
    grid = grid.at[:, 0, :, :].add(penalty[:, :, 0])
    grid = grid.at[:, :, 7, :].add(penalty[:, :, 1])
    grid = grid.at[:, 7, :, :].add(penalty[:, :, 2])
    grid = grid.at[:, :, 0, :].add(penalty[:, :, 3])
    return grid.reshape(field.shape)


def squares_sum(resid):
    return lax.psum(jnp.sum(resid * resid, axis=(1, 2)), "xy")


def per_device(concentration, geometry, nbr_elem, nbr_edge, wall_flags):
    tables = make_tables()
    mass_w = tables[2]
    edge_w = tables[3]
    elems = concentration.shape[2]
    scale_x = geometry[0]
    scale_y = geometry[1]
    jacobian = 1.0 / (scale_x * scale_y)
    total_planes = concentration.shape[0] * lax.axis_size("gz")
    fourier = jnp.asarray(fourier_table(total_planes), jnp.float32)
    wave_all = ((jnp.arange(total_planes, dtype=jnp.int32) + 1) // 2).astype(jnp.float32)
    explicit, bulk = plane_terms(concentration, tables, scale_x, scale_y)
    explicit_hat = jnp.einsum(
        "kp,pne->kne",
        fourier,
        lax.all_to_all(explicit, "gz", split_axis=2, concat_axis=0, tiled=True),
        precision=highest,
    )
    bulk_hat = jnp.einsum(
        "kp,pne->kne",
        fourier,
        lax.all_to_all(bulk, "gz", split_axis=2, concat_axis=0, tiled=True),
        precision=highest,
    )
    right_side = lax.all_to_all(
        explicit_hat - axial_mobility * (wave_all * wave_all)[:, None, None] * bulk_hat,
        "gz",
        split_axis=0,
        concat_axis=2,
        tiled=True,
    )
    modes_dev = right_side.shape[0]
    mode_ids = lax.axis_index("gz") * modes_dev + jnp.arange(modes_dev, dtype=jnp.int32)
    wave = ((mode_ids + 1) // 2).astype(jnp.float32)
    mass_coef = 1.0 / time_step + axial_stiffness * wave * wave
    flag_f = wall_flags.astype(jnp.float32)
    me_xy = lax.axis_index("xy")
    wall = nbr_elem < 0
    safe_ids = jnp.maximum(nbr_elem, 0)
    owner = safe_ids // elems
    local_id = safe_ids % elems
    reverse = nbr_edge >= 4
    window_id = jnp.where(
        owner == me_xy,
        ROWS + local_id,
        jnp.where(local_id < ROWS, ROWS + elems + local_id, local_id - (elems - ROWS)),
    )
    width = elems + 2 * ROWS
    position = (nbr_edge % 4 * width + window_id).reshape(-1)
    solution = jnp.zeros_like(right_side)
    residual = right_side
    direction = right_side
    norm_now = squares_sum(residual)
    for sweep in range(ITERS):
        result = jacobian * mass_w[:, None] * mass_coef[:, None, None] * direction
        result = result + plane_stiffness * weak_flux(
            direction, 1.0, tables, jacobian, scale_x, scale_y
        )
        helm_traces = edge_traces(direction)
        window = padded(helm_traces, (("xy", 3),), ROWS)
        flat = window.reshape(modes_dev, 8, 4 * width)
        values = jnp.take(flat, position, axis=2).reshape(modes_dev, 8, 4, elems)
        values = jnp.where(reverse[None, None], values[:, ::-1], values)
        jump = jnp.where(
            wall[None, None], flag_f[:, None, None, None] * helm_traces, helm_traces - values
        )
        penalty = edge_penalty * edge_w[None, :, None, None] * jump
        image = add_edges(result, penalty)
        alpha = norm_now / lax.psum(jnp.sum(direction * image, axis=(1, 2)), "xy")
        solution = solution + alpha[:, None, None] * direction
        residual = residual - alpha[:, None, None] * image
        if sweep + 1 < ITERS:
            norm_next = squares_sum(residual)
            direction = residual + (norm_next / norm_now)[:, None, None] * direction
            norm_now = norm_next
    return solution


def solution(mesh):
    return jax.shard_map(
        per_device,
        mesh=mesh,
        in_specs=(P("gz", None, "xy"), P(None, "xy"), P(None, "xy"), P(None, "xy"), P("gz")),
        out_specs=P("gz", None, "xy"),
        check_vma=False,
    )
```

profile of v0, /device:TPU:8, one launch (start us, length us, event | category | flops | bytes accessed | tf_op | source)
XLA Modules:
  0.0 794.4 jit_solution(11346135174734293699)
XLA Ops:
  15.6 9.8 %reshape.471 = f32[8,1,131072]{2,1,0:T(1,128)} reshape(f32[512,32,64]{2,1,0:T(8,128)} %bitcast.138) | data formatting | bytes 8388608
  66.2 9.8 %reshape.473 = f32[8,1,131072]{2,1,0:T(1,128)} reshape(f32[512,32,64]{2,1,0:T(8,128)} %bitcast.139) | data formatting | bytes 8388608
  76.0 47.0 %all-to-all-done.1 = f32[8,1,131072]{2,1,0:T(1,128)} async-done(((f32[8,1,131072]{2,1,0:T(1,128)}), f32[8,1,131072]{2,1,0:T(1,128)}, u32[]{:S(2)}, u32[]{:S(2)}) %all-to-all-start.1) | async-done | bytes 4194336 | tf_op jit(solution)/shard_map/all_to_all | solution.py:141
  130.6 13.7 %reduce.20 = f32[8,131072]{1,0:T(8,128)} reduce(f32[8,1,131072]{2,1,0:T(1,128)} %all-to-all-done.1, f32[]{:T(128)} %broadcast.345), dimensions={1}, to_apply=%all_to_all.43.reduce_sub_computation | reduce | bytes 8388612 | tf_op jit(solution)/shard_map/all_to_all | solution.py:141
  153.0 9.6 %copy.84 = f32[32,64,8,64]{3,1,0,2:T(8,128)} copy(f32[32,64,8,64]{1,0,3,2:T(8,128)} %bitcast.143) | data formatting | bytes 8388608 | tf_op jit(solution)/shard_map/all_to_all | solution.py:141
  162.6 57.5 %all-to-all-done = f32[8,1,131072]{2,1,0:T(1,128)} async-done(((f32[8,1,131072]{2,1,0:T(1,128)}), f32[8,1,131072]{2,1,0:T(1,128)}, u32[]{:S(2)}, u32[]{:S(2)}) %all-to-all-start) | async-done | bytes 4194336 | tf_op jit(solution)/shard_map/all_to_all | solution.py:135
  220.2 13.7 %reduce.21 = f32[8,131072]{1,0:T(8,128)} reduce(f32[8,1,131072]{2,1,0:T(1,128)} %all-to-all-done, f32[]{:T(128)} %broadcast.345), dimensions={1}, to_apply=%all_to_all.39.reduce_sub_computation | reduce | bytes 8388612 | tf_op jit(solution)/shard_map/all_to_all | solution.py:135
  242.6 9.6 %copy.81 = f32[32,64,8,64]{3,1,0,2:T(8,128)} copy(f32[32,64,8,64]{1,0,3,2:T(8,128)} %bitcast.144) | data formatting | bytes 8388608 | tf_op jit(solution)/shard_map/all_to_all | solution.py:135
  252.2 20.8 %fusion = f32[64,64,256]{2,1,0:T(8,128)S(1)} fusion(f32[256,256,1]{1,0,2:T(8,128)S(1)} %copy-done.17, f32[256,64,64]{2,1,0:T(8,128)} %bitcast.141), kind=kOutput, calls=%fused_computation.2 | convolution fusion | flops 3221225472 | bytes 8650752 | tf_op jit(solution)/shard_map/kp,pne->kne/dot_general | solution.py:138
  273.0 21.6 %subtract_bitcast_fusion = f32[256,64,64]{0,2,1:T(8,128)} fusion(f32[64,64,256]{2,1,0:T(8,128)S(1)} %fusion, f32[256,256,1]{1,0,2:T(8,128)S(1)} %copy-done.17, f32[256,64,64]{2,1,0:T(8,128)S(1)} %bitcast.142, f32[256]{0:T(256)S(1)} %multiply_multiply_fusion.4), kind=kOutput, calls=%fused_computation.50 | convolution fusion | flops 3223322624 | bytes 12846080 | tf_op jit(solution)/shard_map/kp,pne->kne/dot_general | solution.py:132
  294.6 9.2 %copy.86 = f32[256,64,64]{2,1,0:T(8,128)} copy(f32[256,64,64]{0,2,1:T(8,128)} %subtract_bitcast_fusion) | data formatting | bytes 8388608 | tf_op jit(solution)/shard_map/sub | solution.py:145
  303.8 9.8 %reshape.475 = f32[8,1,131072]{2,1,0:T(1,128)} reshape(f32[256,64,64]{2,1,0:T(8,128)} %copy.86) | data formatting | bytes 8388608
  320.9 89.9 %all-to-all-done.2 = f32[8,1,131072]{2,1,0:T(1,128)} async-done(((f32[8,1,131072]{2,1,0:T(1,128)}), f32[8,1,131072]{2,1,0:T(1,128)}, u32[]{:S(2)}, u32[]{:S(2)}) %all-to-all-start.2) | async-done | bytes 4194336 | tf_op jit(solution)/shard_map/all_to_all | solution.py:144
  410.8 14.1 %reduce.22 = f32[8,131072]{1,0:T(8,128)} reduce(f32[8,1,131072]{2,1,0:T(1,128)} %all-to-all-done.2, f32[]{:T(128)} %broadcast.345), dimensions={1}, to_apply=%all_to_all.47.reduce_sub_computation | reduce | bytes 8388612 | tf_op jit(solution)/shard_map/all_to_all | solution.py:144
  433.8 14.3 %copy.87 = f32[32,64,8,64]{3,2,1,0:T(8,128)} copy(f32[32,64,8,64]{3,1,0,2:T(8,128)} %bitcast.134) | data formatting | bytes 8388608 | tf_op jit(solution)/shard_map/all_to_all | solution.py:144
  511.6 19.9 %gather_fusion = f32[2048,32,8]{1,2,0:T(8,128)} fusion(f32[32,8,2560]{0,1,2:T(8,128)} %bitcast.146, s32[2048]{0:T(1024)S(1)} %fusion.80), kind=kCustom, calls=%fused_computation.clone | custom fusion | bytes 4202496 | tf_op jit(solution)/shard_map/jit(_take)/gather | solution.py:181
  531.5 12.5 %broadcast_select_fusion.1 = f32[2048,32,8]{1,2,0:T(8,128)} fusion(f32[2048,32,8]{1,2,0:T(8,128)} %gather_fusion, pred[2048]{0:T(1024)(128)(4,1)S(1)} %compare_and_fusion), kind=kLoop, calls=%fused_computation.38 | loop fusion | flops 524288 | bytes 4196352 | tf_op jit(solution)/shard_map/jit(_take)/select_n | solution.py:181
  562.3 11.4 %scatter-add.29 = f32[32,8,8,512]{3,2,1,0:T(8,128)} dynamic-update-slice(f32[32,8,8,512]{3,2,1,0:T(8,128)} %fusion.73, f32[32,8,1,512]{3,2,1,0:T(1,128)S(1)} %slice_add_fusion.4, s32[]{:T(128)} %constant.288.clone.1, s32[]{:T(128)} %constant.288.clone.1, s32[]{:T(128)} %constant.305.clone.1, s32[]{:T(128)} %constant.288.clone.1) | dynamic-update-slice | bytes 1048580 | tf_op jit(solution)/shard_map/scatter-add | solution.py:110
  578.6 11.4 %scatter-add.31 = f32[32,8,8,512]{3,2,1,0:T(8,128)} dynamic-update-slice(f32[32,8,8,512]{3,2,1,0:T(8,128)} %fusion.72, f32[32,8,1,512]{3,2,1,0:T(1,128)S(1)} %slice_add_fusion.2, s32[]{:T(128)} %constant.288.clone.1, s32[]{:T(128)} %constant.288.clone.1, s32[]{:T(128)} %constant.288.clone.1, s32[]{:T(128)} %constant.288.clone.1) | dynamic-update-slice | bytes 1048580 | tf_op jit(solution)/shard_map/scatter-add | solution.py:112
  680.8 19.8 %gather_fusion.1 = f32[2048,32,8]{1,2,0:T(8,128)} fusion(f32[32,8,2560]{0,1,2:T(8,128)} %bitcast.145, s32[2048]{0:T(1024)S(1)} %fusion.80), kind=kCustom, calls=%fused_computation.1.clone | custom fusion | bytes 4202496 | tf_op jit(solution)/shard_map/jit(_take)/gather | solution.py:181
  700.6 12.5 %broadcast_select_fusion = f32[2048,32,8]{1,2,0:T(8,128)} fusion(f32[2048,32,8]{1,2,0:T(8,128)} %gather_fusion.1, pred[2048]{0:T(1024)(128)(4,1)S(1)} %compare_and_fusion), kind=kLoop, calls=%fused_computation.37 | loop fusion | flops 524288 | bytes 4196352 | tf_op jit(solution)/shard_map/jit(_take)/select_n | solution.py:181
  728.2 11.4 %scatter-add.34 = f32[32,8,8,512]{3,1,2,0:T(8,128)} dynamic-update-slice(f32[32,8,8,512]{3,1,2,0:T(8,128)} %copy.108, f32[32,1,8,512]{3,1,2,0:T(1,128)S(1)} %fusion.71, s32[]{:T(128)} %constant.288.clone.1, s32[]{:T(128)} %constant.288.clone.1, s32[]{:T(128)} %constant.288.clone.1, s32[]{:T(128)} %constant.288.clone.1) | dynamic-update-slice | bytes 1048580 | tf_op jit(solution)/shard_map/scatter-add | solution.py:109
  744.6 11.6 %scatter-add.36 = f32[32,8,8,512]{3,1,2,0:T(8,128)} dynamic-update-slice(f32[32,8,8,512]{3,1,2,0:T(8,128)} %fusion.70, f32[32,1,8,512]{3,1,2,0:T(1,128)S(1)} %fusion.69, s32[]{:T(128)} %constant.288.clone.1, s32[]{:T(128)} %constant.305.clone.1, s32[]{:T(128)} %constant.288.clone.1, s32[]{:T(128)} %constant.288.clone.1) | dynamic-update-slice | bytes 1048580 | tf_op jit(solution)/shard_map/scatter-add | solution.py:111
  766.1 11.3 %scatter-add.39 = f32[32,8,8,512]{3,2,1,0:T(8,128)} dynamic-update-slice(f32[32,8,8,512]{3,2,1,0:T(8,128)} %copy.111, f32[32,8,1,512]{3,2,1,0:T(1,128)S(1)} %slice_add_fusion, s32[]{:T(128)} %constant.288.clone.1, s32[]{:T(128)} %constant.288.clone.1, s32[]{:T(128)} %constant.288.clone.1, s32[]{:T(128)} %constant.288.clone.1) | dynamic-update-slice | bytes 1048580 | tf_op jit(solution)/shard_map/scatter-add | solution.py:112
  (134 shorter events, 321.3 us)
Async XLA Ops:
  25.4 7.0 copy-start.15
  25.4 97.6 %all-to-all-start.1 = ((f32[8,1,131072]{2,1,0:T(1,128)}), f32[8,1,131072]{2,1,0:T(1,128)}, u32[]{:S(2)}, u32[]{:S(2)}) async-start(f32[8,1,131072]{2,1,0:T(1,128)} %reshape.471), calls=%async_computation.1 | async-start | bytes 8388608 | tf_op jit(solution)/shard_map/all_to_all | solution.py:141
  32.4 6.5 copy-start.3
  123.0 97.1 %all-to-all-start = ((f32[8,1,131072]{2,1,0:T(1,128)}), f32[8,1,131072]{2,1,0:T(1,128)}, u32[]{:S(2)}, u32[]{:S(2)}) async-start(f32[8,1,131072]{2,1,0:T(1,128)} %reshape.473), calls=%async_computation | async-start | bytes 8388608 | tf_op jit(solution)/shard_map/all_to_all | solution.py:135
  242.6 9.6 %copy-start.17 = (f32[256,256,1]{1,0,2:T(8,128)S(1)}, f32[256,256,1]{1,0,2:T(8,128)}, u32[]{:S(2)}) copy-start(f32[256,256,1]{1,0,2:T(8,128)} %constant.314) | copy-start | bytes 786436
  252.2 20.8 %copy-start.5 = (f32[32,64,8,64]{3,1,0,2:T(8,128)S(1)}, f32[32,64,8,64]{3,1,0,2:T(8,128)}, u32[]{:S(2)}) copy-start(f32[32,64,8,64]{3,1,0,2:T(8,128)} %copy.81) | copy-start | bytes 12582916
  313.6 7.2 copy-start.22
  313.6 7.2 copy-start.18
  313.6 7.2 copy-start.19
  313.6 97.2 %all-to-all-start.2 = ((f32[8,1,131072]{2,1,0:T(1,128)}), f32[8,1,131072]{2,1,0:T(1,128)}, u32[]{:S(2)}, u32[]{:S(2)}) async-start(f32[8,1,131072]{2,1,0:T(1,128)} %reshape.475), calls=%async_computation.2 | async-start | bytes 8388608 | tf_op jit(solution)/shard_map/all_to_all | solution.py:144
  467.9 29.8 %copy-start.11 = (f32[32,8,1,512]{3,2,1,0:T(1,128)}, f32[32,8,1,512]{3,2,1,0:T(1,128)S(1)}, u32[]{:S(2)}) copy-start(f32[32,8,1,512]{3,2,1,0:T(1,128)S(1)} %get-tuple-element.113) | copy-start | bytes 1572868
  481.0 16.7 %copy-start.13 = (f32[32,8,1,512]{3,2,1,0:T(1,128)}, f32[32,8,1,512]{3,2,1,0:T(1,128)S(1)}, u32[]{:S(2)}) copy-start(f32[32,8,1,512]{3,2,1,0:T(1,128)S(1)} %get-tuple-element.125) | copy-start | bytes 1572868
  481.0 16.7 %copy-start.14 = (f32[32,8,1,512]{3,2,1,0:T(1,128)}, f32[32,8,1,512]{3,2,1,0:T(1,128)S(1)}, u32[]{:S(2)}) copy-start(f32[32,8,1,512]{3,2,1,0:T(1,128)S(1)} %get-tuple-element.126) | copy-start | bytes 1572868
  483.5 14.1 %collective-permute-start = (f32[32,8,4,64]{3,2,1,0:T(4,128)S(1)}, f32[32,8,4,64]{3,2,1,0:T(4,128)S(1)}, u32[]{:S(2)}, u32[]{:S(2)}) collective-permute-start(f32[32,8,4,64]{3,2,1,0:T(4,128)S(1)} %get-tuple-element.118), channel_id=1, source_target_pairs={{0,8},{8,16},{16,24},{24,0},{1,9},{9,17},{17,25},{25,1},{2,10},{10... | collective-permute-start | bytes 786440 | tf_op jit(solution)/shard_map/ppermute | solution.py:27
  483.7 13.9 %collective-permute-start.1 = (f32[32,8,4,64]{3,2,1,0:T(4,128)S(1)}, f32[32,8,4,64]{3,2,1,0:T(4,128)S(1)}, u32[]{:S(2)}, u32[]{:S(2)}) collective-permute-start(f32[32,8,4,64]{3,2,1,0:T(4,128)S(1)} %get-tuple-element.119), channel_id=1, source_target_pairs={{8,0},{16,8},{24,16},{0,24},{9,1},{17,9},{25,17},{1,25},{10,2},{18... | collective-permute-start | bytes 786440 | tf_op jit(solution)/shard_map/ppermute | solution.py:28
  544.0 6.7 copy-start.12
  544.0 6.7 copy-start.21
  632.7 21.6 %copy-start.2 = (f32[32,64,512]{2,1,0:T(8,128)}, f32[32,64,512]{2,1,0:T(8,128)S(1)}, u32[]{:S(2)}) copy-start(f32[32,64,512]{2,1,0:T(8,128)S(1)} %fusion.15) | copy-start | bytes 12582916
  634.0 32.8 %copy-start.9 = (f32[32,8,1,512]{3,2,1,0:T(1,128)}, f32[32,8,1,512]{3,2,1,0:T(1,128)S(1)}, u32[]{:S(2)}) copy-start(f32[32,8,1,512]{3,2,1,0:T(1,128)S(1)} %get-tuple-element.108) | copy-start | bytes 1572868
  634.0 32.8 %copy-start.10 = (f32[32,8,1,512]{3,2,1,0:T(1,128)}, f32[32,8,1,512]{3,2,1,0:T(1,128)S(1)}, u32[]{:S(2)}) copy-start(f32[32,8,1,512]{3,2,1,0:T(1,128)S(1)} %get-tuple-element.109) | copy-start | bytes 1572868
  645.0 21.8 %copy-start.7 = (f32[32,1,8,512]{3,1,2,0:T(1,128)}, f32[32,1,8,512]{3,1,2,0:T(1,128)S(1)}, u32[]{:S(2)}) copy-start(f32[32,1,8,512]{3,1,2,0:T(1,128)S(1)} %copy.152) | copy-start | bytes 1572868
  647.5 19.3 %collective-permute-start.2 = (f32[32,8,4,64]{3,2,1,0:T(4,128)S(1)}, f32[32,8,4,64]{3,2,1,0:T(4,128)S(1)}, u32[]{:S(2)}, u32[]{:S(2)}) collective-permute-start(f32[32,8,4,64]{3,2,1,0:T(4,128)S(1)} %get-tuple-element.114), channel_id=1, source_target_pairs={{0,8},{8,16},{16,24},{24,0},{1,9},{9,17},{17,25},{25,1},{2,10},{10... | collective-permute-start | bytes 786440 | tf_op jit(solution)/shard_map/ppermute | solution.py:27
  647.6 19.2 %collective-permute-start.3 = (f32[32,8,4,64]{3,2,1,0:T(4,128)S(1)}, f32[32,8,4,64]{3,2,1,0:T(4,128)S(1)}, u32[]{:S(2)}, u32[]{:S(2)}) collective-permute-start(f32[32,8,4,64]{3,2,1,0:T(4,128)S(1)} %get-tuple-element.115), channel_id=1, source_target_pairs={{8,0},{16,8},{24,16},{0,24},{9,1},{17,9},{25,17},{1,25},{10,2},{18... | collective-permute-start | bytes 786440 | tf_op jit(solution)/shard_map/ppermute | solution.py:28
  713.1 6.7 copy-start.8
  (6 other events, 30.9 us)
where the time goes:
time: 805 us; the launch traced here: 794 us
  local copies, waits for them, and re-layouts  291 us (36%)
  waiting for transfers between devices  195 us (24%)
  other arithmetic  155 us (19%)
  matrix products  110 us (14%)
  starting transfers between devices  24.9 us (3%)
  blocking collectives  18.6 us (2%)
    all_to_all x1, waiting for transfers between devices, per_device(): lax.all_to_all(explicit_hat - axial_mobility * (wave_all * wave_all)[:, N...  89.9 us
    unnamed x55, local copies, waits for them, and re-layouts  58.4 us
    all_to_all x1, waiting for transfers between devices, per_device(): lax.all_to_all(explicit, 'gz', split_axis=2, concat_axis=0, tiled=True)  57.5 us
    all_to_all x1, waiting for transfers between devices, per_device(): lax.all_to_all(bulk, 'gz', split_axis=2, concat_axis=0, tiled=True)  47 us
    gather x2, local copies, waits for them, and re-layouts, per_device(): values = jnp.take(flat, position, axis=2).reshape(modes_dev, 8, 4, elems)  39.7 us
    select_n x2, other arithmetic, per_device(): values = jnp.take(flat, position, axis=2).reshape(modes_dev, 8, 4, elems)  25 us
    scatter-add x2, local copies, waits for them, and re-layouts, add_edges(): grid = grid.at[:, :, 0, :].add(penalty[:, :, 3])  22.7 us
    all_to_all x2, local copies, waits for them, and re-layouts, per_device(): lax.all_to_all(explicit_hat - axial_mobility * (wave_all * wave_all)[:, N...  21.9 us
  transfers between devices with their start and end apart: 7, of which 3 were waited for; matrix products, arithmetic and copies ran while one was open for 13% of the time, Pallas kernels for 0%

commit v1 on v0

v1 whole, which is shorter than its diff:
```python
import functools

import jax
import jax.numpy as jnp
import ml_dtypes
import numpy as np
from jax import lax
from jax.experimental import pallas as pl
from jax.experimental.pallas import tpu as pltpu
from jax.sharding import PartitionSpec as P

ROWS = 64
LANES = 128
MIB = 1024 * 1024

time_step = 0.2
axial_stiffness = 0.002
plane_stiffness = 1.0
edge_penalty = 4.0
axial_mobility = 0.002
mobility_floor = 0.05


def point_tables():
    degree = 7
    points = np.arange(degree + 1)
    theta = np.pi * points / degree
    nodes_x = np.cos(theta)
    signs = np.where((points == 0) | (points == degree), 2.0, 1.0) * (-1.0) ** points
    differ = nodes_x[:, None] - nodes_x[None, :]
    deriv = np.outer(signs, 1.0 / signs) / (differ + np.eye(degree + 1))
    deriv = deriv - np.eye(degree + 1) * deriv.sum(axis=1)[:, None]
    inner = np.ones(degree - 1)
    for number in range(1, (degree - 1) // 2 + 1):
        inner = inner - 2.0 * np.cos(2 * number * theta[1:degree]) / (4 * number * number - 1)
    weights = np.zeros(degree + 1)
    weights[1:degree] = 2.0 * inner / degree
    weights[0] = 1.0 / degree**2
    weights[degree] = 1.0 / degree**2
    return (deriv, weights)


def fourier_table(length):
    planes = np.arange(length)
    wave_no = (planes + 1) // 2
    phase = np.outer(wave_no, planes) % length * (2.0 * np.pi / length)
    table = np.where((planes % 2 == 1)[:, None], np.cos(phase), np.sin(phase)) * np.sqrt(
        2.0 / length
    )
    table[0] = 1.0 / np.sqrt(length)
    table[length - 1] = np.cos(phase[length - 1]) / np.sqrt(length)
    return table


DERIV, WEIGHTS = point_tables()
BACK = DERIV.T * WEIGHTS[None, :]
STIFF = BACK @ DERIV


def two_parts(table):
    upper = table.astype(np.float32).astype(ml_dtypes.bfloat16)
    lower = (table - upper.astype(np.float64)).astype(np.float32).astype(ml_dtypes.bfloat16)
    return upper, lower


def split(value):
    upper = value.astype(jnp.bfloat16)
    lower = (value - upper.astype(jnp.float32)).astype(jnp.bfloat16)
    return upper, lower


class Fold:
    def __init__(self, width):
        self.width = width
        self.parts = LANES // width
        self.fold_j = 2 if self.parts >= 2 else 1
        self.fold_i = 2 if self.parts >= 4 else 1
        self.count_j = 8 // self.fold_j
        self.count_i = 8 // self.fold_i
        self.slots = self.count_j * self.count_i

    def slot(self, jp, ip):
        return jp * self.count_i + ip

    def node(self, jp, ip, part):
        half_j, half_i = part // self.fold_i, part % self.fold_i
        j = 7 - jp if half_j else jp
        i = 7 - ip if half_i else ip
        return 8 * j + i

    def place(self, node):
        j, i = node // 8, node % 8
        half_j = 1 if j >= self.count_j else 0
        half_i = 1 if i >= self.count_i else 0
        jp = 7 - j if half_j else j
        ip = 7 - i if half_i else i
        return self.slot(jp, ip), half_j * self.fold_i + half_i


def lane_of(shape):
    return lax.broadcasted_iota(jnp.int32, shape, len(shape) - 1)


def rolled(value, lanes):
    lanes = lanes % LANES
    return value if lanes == 0 else pltpu.roll(value, lanes, value.ndim - 1)


def by_part(values, lane, width):
    out = values[0]
    for r in range(1, len(values)):
        out = jnp.where(lane >= r * width, values[r], out)
    return out


def mirrored(value, lane, shift):
    if 2 * shift == LANES:
        return rolled(value, shift)
    return jnp.where((lane & shift) == 0, rolled(value, -shift), rolled(value, shift))


def combine(coefs, values):
    total = None
    for c, v in zip(coefs, values):
        term = v * np.float32(c)
        total = term if total is None else total + term
    return total


def line_apply(matrix, values, sign):
    even = [values[k] + values[7 - k] for k in range(4)]
    odd = [values[k] - values[7 - k] for k in range(4)]
    out = [None] * 8
    for a in range(4):
        from_even = combine([(matrix[a, b] + matrix[a, 7 - b]) / 2 for b in range(4)], even)
        from_odd = combine([(matrix[a, b] - matrix[a, 7 - b]) / 2 for b in range(4)], odd)
        out[a] = from_even + from_odd
        out[7 - a] = from_even - from_odd if sign > 0 else from_odd - from_even
    return out


def derivative_line(matrix, values, back, swap):
    if swap is None:
        return line_apply(matrix, values, -1)
    other = [swap(v) for v in values]
    sign = -1.0 if back else 1.0
    out = []
    for a in range(4):
        coefs = [matrix[a, b] for b in range(4)] + [sign * matrix[a, 7 - b] for b in range(4)]
        out.append(combine(coefs, list(values) + other))
    return out


EDGE_NODES = [
    [t for t in range(8)],
    [8 * t + 7 for t in range(8)],
    [56 + t for t in range(8)],
    [8 * t for t in range(8)],
]


def pack_kernel(fold, c_ref, out_ref):
    lane = lane_of((c_ref.shape[0], LANES))
    for jp in range(fold.count_j):
        for ip in range(fold.count_i):
            loads = [c_ref[:, fold.node(jp, ip, q), :] for q in range(fold.parts)]
            for r in range(fold.parts):
                parts = [rolled(loads[q], (q - r) * fold.width) for q in range(fold.parts)]
                out_ref[r, fold.slot(jp, ip)] = by_part(parts, lane, fold.width)


def pack(conc, fold, groups):
    planes, nodes, elems = conc.shape
    blocks = elems // LANES
    return pl.pallas_call(
        functools.partial(pack_kernel, fold),
        grid=(blocks,),
        in_specs=[pl.BlockSpec((planes, nodes, LANES), lambda b: (0, 0, b))],
        out_specs=pl.BlockSpec((fold.parts, fold.slots, planes, LANES), lambda b: (b, 0, 0, 0)),
        out_shape=jax.ShapeDtypeStruct((groups, fold.slots, planes, LANES), jnp.float32),
        compiler_params=pltpu.CompilerParams(vmem_limit_bytes=24 * MIB),
        cost_estimate=pl.CostEstimate(
            flops=conc.size, bytes_accessed=8 * conc.size, transcendentals=0
        ),
    )(conc)


def rhs_kernel(fold, groups, planes, first_ref, second_ref, y_ref, geo_ref, out_ref, x_ref, acc_ref):
    step = pl.program_id(0)
    total = groups * planes

    @pl.when(step < groups)
    def _():
        def chunk(part, _):
            base = pl.multiple_of(part * 16, 16)
            lane = lane_of((16, LANES))
            jac = jnp.broadcast_to(geo_ref[0:1, :], (16, LANES))
            ratio_x = jnp.broadcast_to(geo_ref[1:2, :], (16, LANES))
            ratio_y = jnp.broadcast_to(geo_ref[2:3, :], (16, LANES))

            def conc(jp, ip):
                return y_ref[0, fold.slot(jp, ip), pl.ds(base, 16), :]

            def potential(c):
                square = c * c
                return square * c - c, jnp.maximum(1.0 - square, mobility_floor)

            def flux(fields, swap):
                pairs = [potential(c) for c in fields]
                slope = derivative_line(DERIV, [p[0] for p in pairs], False, swap)
                scaled = [s * p[1] for s, p in zip(slope, pairs)]
                return derivative_line(BACK, scaled, True, swap), pairs

            swap_i = None
            if fold.fold_i == 2:
                swap_i = lambda v: mirrored(v, lane, fold.width)
            swap_j = None
            if fold.fold_j == 2:
                swap_j = lambda v: mirrored(v, lane, fold.width * fold.fold_i)
            for jp in range(fold.count_j):
                fields = [conc(jp, ip) for ip in range(fold.count_i)]
                result, _unused = flux(fields, swap_i)
                scale = ratio_x * np.float32(WEIGHTS[jp])
                for ip in range(fold.count_i):
                    acc_ref[fold.slot(jp, ip)] = result[ip] * scale
            row = pl.multiple_of(step * planes + base, 16)
            for ip in range(fold.count_i):
                fields = [conc(jp, ip) for jp in range(fold.count_j)]
                result, pairs = flux(fields, swap_j)
                scale = ratio_y * np.float32(WEIGHTS[ip])
                for jp in range(fold.count_j):
                    slot = fold.slot(jp, ip)
                    mass = jac * np.float32(WEIGHTS[jp] * WEIGHTS[ip])
                    explicit = (
                        mass * (fields[jp] * np.float32(1.0 / time_step))
                        - acc_ref[slot]
                        - result[jp] * scale
                    )
                    bulk = mass * pairs[jp][0]
                    where = pl.ds((slot % 2) * LANES, LANES)
                    upper, lower = split(explicit)
                    x_ref[slot // 2, pl.ds(row, 16), where] = upper
                    x_ref[slot // 2, pl.ds(2 * total + row, 16), where] = lower
                    upper, lower = split(bulk)
                    x_ref[slot // 2, pl.ds(total + row, 16), where] = upper
                    x_ref[slot // 2, pl.ds(3 * total + row, 16), where] = lower
            return 0

        lax.fori_loop(0, planes // 16, chunk, 0)

    @pl.when(step >= groups)
    def _():
        pair = step - groups
        data = x_ref[pair]
        result = jnp.dot(first_ref[...], data, preferred_element_type=jnp.float32)
        result = result + jnp.dot(
            second_ref[...], data[: 2 * total], preferred_element_type=jnp.float32
        )
        for h in range(groups):
            rows = result[h * planes : (h + 1) * planes]
            out_ref[h, 0] = rows[:, :LANES]
            out_ref[h, 1] = rows[:, LANES:]


def right_hand_side(field, geo, fold, total):
    groups, slots, planes, _ = field.shape
    table = fourier_table(total).astype(np.float32).astype(np.float64)
    wave = ((np.arange(total) + 1) // 2).astype(np.float64)
    upper, lower = two_parts(table)
    upper_b, lower_b = two_parts(-axial_mobility * (wave * wave)[:, None] * table)
    first = jnp.asarray(np.concatenate([upper, upper_b, upper, upper_b], axis=1))
    second = jnp.asarray(np.concatenate([lower, lower_b], axis=1))
    pairs = slots // 2
    return pl.pallas_call(
        functools.partial(rhs_kernel, fold, groups, planes),
        grid=(groups + pairs,),
        in_specs=[
            pl.BlockSpec((total, 4 * total), lambda s: (0, 0)),
            pl.BlockSpec((total, 2 * total), lambda s: (0, 0)),
            pl.BlockSpec(
                (1, slots, planes, LANES), lambda s: (jnp.minimum(s, groups - 1), 0, 0, 0)
            ),
            pl.BlockSpec((8, LANES), lambda s: (0, 0)),
        ],
        out_specs=pl.BlockSpec(
            (groups, 2, planes, LANES), lambda s: (0, jnp.maximum(s - groups, 0), 0, 0)
        ),
        out_shape=jax.ShapeDtypeStruct((groups, slots, planes, LANES), jnp.float32),
        scratch_shapes=[
            pltpu.VMEM((pairs, 4 * total, 2 * LANES), jnp.bfloat16),
            pltpu.VMEM((slots, 16, LANES), jnp.float32),
        ],
        compiler_params=pltpu.CompilerParams(vmem_limit_bytes=40 * MIB),
        cost_estimate=pl.CostEstimate(
            flops=12 * total * field.size, bytes_accessed=8 * field.size, transcendentals=0
        ),
    )(first, second, field, geo)


def edge_send(mask_ref, edge, out_ref):
    for t in range(8):
        total = None
        for a in range(4):
            term = edge(a, t) * mask_ref[a : a + 1, :]
            total = term if total is None else total + term
        out_ref[t] = total


def first_send_kernel(fold, rhs_ref, mask_ref, out_ref):
    half = rhs_ref.shape[0] // 2
    lane = lane_of(out_ref.shape[1:])

    def edge(a, t):
        slot, part = fold.place(EDGE_NODES[a][t])
        parts = []
        for r in range(2 * half):
            parts.append(rolled(rhs_ref[r, slot], (r - part) * fold.width))
        return by_part(parts, lane, fold.width)

    edge_send(mask_ref, edge, out_ref)


def first_send(rhs, mask, fold):
    groups, slots, modes, _ = rhs.shape
    half = ROWS // fold.width
    ends = jnp.concatenate([rhs[:half], rhs[groups - half :]], axis=0)
    return pl.pallas_call(
        functools.partial(first_send_kernel, fold),
        out_shape=jax.ShapeDtypeStruct((8, modes, LANES), jnp.float32),
        compiler_params=pltpu.CompilerParams(vmem_limit_bytes=16 * MIB),
    )(ends, mask)


def unpack(fold, r_ref, out_ref, rows, lanes):
    lane = lane_of((8, LANES))
    for jp in range(fold.count_j):
        for ip in range(fold.count_i):
            loads = [r_ref[r, fold.slot(jp, ip), rows, :] for r in range(fold.parts)]
            for q in range(fold.parts):
                parts = [rolled(loads[r], (r - q) * fold.width) for r in range(fold.parts)]
                out_ref[fold.node(jp, ip, q), rows, lanes] = by_part(parts, lane, fold.width)


def volume(field, acc_ref, geo_ref, mass_ref, rows, lanes, visit):
    jac = geo_ref[0:1, :] * mass_ref[rows, :]
    ratio_x = jnp.broadcast_to(geo_ref[1:2, :], (8, LANES))
    ratio_y = jnp.broadcast_to(geo_ref[2:3, :], (8, LANES))
    for j in range(8):
        result = line_apply(plane_stiffness * STIFF, [field(8 * j + i) for i in range(8)], 1)
        scale = ratio_x * np.float32(WEIGHTS[j])
        for i in range(8):
            acc_ref[8 * j + i] = result[i] * scale
    for i in range(8):
        values = [field(8 * j + i) for j in range(8)]
        result = line_apply(plane_stiffness * STIFF, values, 1)
        scale = ratio_y * np.float32(WEIGHTS[i])
        for j in range(8):
            mass = jac * np.float32(WEIGHTS[j] * WEIGHTS[i])
            visit(8 * j + i, values[j], acc_ref[8 * j + i] + result[j] * scale + mass * values[j])


def fill_traces(field_ref, trace_ref):
    modes, elems = field_ref.shape[1:]
    for a in range(4):
        for t in range(8):
            upper, lower = split(field_ref[EDGE_NODES[a][t]])
            where = pl.ds(a * elems, elems)
            trace_ref[pl.ds(t * modes, modes), where] = upper
            trace_ref[pl.ds((8 + t) * modes, modes), where] = lower


def fill_halo(halo_ref, parts_ref):
    modes = halo_ref.shape[2]
    lane = lane_of((modes, LANES))
    for t in range(8):
        upper, lower = split(jnp.where(lane < ROWS, halo_ref[0, t], halo_ref[1, t]))
        parts_ref[pl.ds(t * modes, modes), :] = upper
        parts_ref[pl.ds((8 + t) * modes, modes), :] = lower


def gathered(trace_ref, parts_ref, local_ref, far_ref, val_ref):
    modes, elems = val_ref.shape[1:]
    rows = 8 * modes
    value = jnp.dot(trace_ref[...], local_ref[...], preferred_element_type=jnp.float32)
    val_ref[...] = (value[:rows] + value[rows:]).reshape(8, modes, elems)
    value = jnp.dot(parts_ref[...], far_ref[...], preferred_element_type=jnp.float32)
    far = (value[:rows] + value[rows:]).reshape(8, modes, LANES)
    lane = lane_of(far.shape)
    val_ref[:, :, :LANES] += jnp.where(lane < ROWS, far, 0.0)
    val_ref[:, :, elems - LANES :] += jnp.where(lane < ROWS, 0.0, far)


def penalties(edge, field_ref, val_ref, edges_ref, flag_ref, visit):
    modes, elems = val_ref.shape[1:]
    for block in range(elems // LANES):
        lanes = pl.ds(block * LANES, LANES)
        wall = edges_ref[0:1, lanes]
        reverse = jnp.broadcast_to(edges_ref[1:2, lanes], (modes, LANES)) > 0.5
        coef = 1.0 - wall * (1.0 - flag_ref[...])
        for t in range(8):
            node = EDGE_NODES[edge][t]
            mine = field_ref[node, :, lanes]
            other = jnp.where(reverse, val_ref[7 - t, :, lanes], val_ref[t, :, lanes])
            weight = np.float32(edge_penalty * WEIGHTS[t])
            visit(node, lanes, mine, weight * (coef * mine - other))


def first_apply_kernel(
    fold,
    blocks,
    r_ref,
    geo_ref,
    mass_ref,
    flag_ref,
    mask_ref,
    halo_ref,
    far_ref,
    local_ref,
    edges_ref,
    r0_ref,
    q0_ref,
    send_ref,
    sums_ref,
    trace_ref,
    parts_ref,
    val_ref,
    acc_ref,
):
    step = pl.program_id(0)
    modes, elems = val_ref.shape[1:]

    @pl.when(step == 0)
    def _():
        sums_ref[...] = jnp.zeros_like(sums_ref)

    @pl.when(step < blocks)
    def _():
        lanes = pl.ds(pl.multiple_of(step * LANES, LANES), LANES)

        def tile(part, _):
            rows = pl.ds(pl.multiple_of(part * 8, 8), 8)
            unpack(fold, r_ref, r0_ref, rows, lanes)
            totals = [None, None]

            def visit(node, value, image):
                q0_ref[node, rows, lanes] = image
                for k, term in enumerate((value * value, value * image)):
                    totals[k] = term if totals[k] is None else totals[k] + term

            volume(
                lambda node: r0_ref[node, rows, lanes],
                acc_ref,
                geo_ref,
                mass_ref,
                rows,
                lanes,
                visit,
            )
            for k in range(2):
                sums_ref[k, rows, :] += totals[k]
            return 0

        lax.fori_loop(0, modes // 8, tile, 0)

    @pl.when(step == blocks)
    def _():
        fill_traces(r0_ref, trace_ref)
        fill_halo(halo_ref, parts_ref)

    for edge in range(4):

        @pl.when(step == blocks + edge)
        def _():
            gathered(trace_ref, parts_ref, local_ref, far_ref, val_ref)
            totals = [None]

            def visit(node, lanes, mine, term):
                q0_ref[node, :, lanes] += term
                product = mine * term
                totals[0] = product if totals[0] is None else totals[0] + product

            penalties(edge, r0_ref, val_ref, edges_ref, flag_ref, visit)
            sums_ref[1] += totals[0]

    @pl.when(step == blocks + 3)
    def _():
        lane = lane_of((modes, LANES))

        def edge_value(a, t):
            node = EDGE_NODES[a][t]
            return jnp.where(
                lane < ROWS, q0_ref[node, :, :LANES], q0_ref[node, :, elems - LANES :]
            )

        edge_send(mask_ref, edge_value, send_ref)


def edge_specs(blocks, elems):
    def at(step):
        return jnp.maximum(step - blocks, 0)

    far = pl.BlockSpec((LANES, LANES), lambda s: (0, at(s)))
    local = pl.BlockSpec((4 * elems, elems), lambda s: (0, at(s)))
    flags = pl.BlockSpec((8, elems), lambda s: (at(s), 0))
    return far, local, flags


def whole(shape):
    return pl.BlockSpec(shape, lambda s: (0,) * len(shape))


def edge_scratch(modes, elems):
    return [
        pltpu.VMEM((16 * modes, 4 * elems), jnp.bfloat16),
        pltpu.VMEM((16 * modes, LANES), jnp.bfloat16),
        pltpu.VMEM((8, modes, elems), jnp.float32),
        pltpu.VMEM((64, 8, LANES), jnp.float32),
    ]


def first_apply(rhs, geo, mass, flag, mask, halo, far, local, edges, fold):
    groups, slots, modes, _ = rhs.shape
    blocks = groups // fold.parts
    elems = blocks * LANES
    block_of = lambda s: jnp.minimum(s, blocks - 1)
    far_spec, local_spec, edges_spec = edge_specs(blocks, elems)
    field = jax.ShapeDtypeStruct((64, modes, elems), jnp.float32)
    return pl.pallas_call(
        functools.partial(first_apply_kernel, fold, blocks),
        grid=(blocks + 4,),
        in_specs=[
            pl.BlockSpec((fold.parts, slots, modes, LANES), lambda s: (block_of(s), 0, 0, 0)),
            pl.BlockSpec((8, LANES), lambda s: (0, block_of(s))),
            whole((modes, LANES)),
            whole((modes, LANES)),
            whole((8, LANES)),
            whole((2, 8, modes, LANES)),
            far_spec,
            local_spec,
            edges_spec,
        ],
        out_specs=[
            whole((64, modes, elems)),
            whole((64, modes, elems)),
            whole((8, modes, LANES)),
            whole((2, modes, LANES)),
        ],
        out_shape=[
            field,
            field,
            jax.ShapeDtypeStruct((8, modes, LANES), jnp.float32),
            jax.ShapeDtypeStruct((2, modes, LANES), jnp.float32),
        ],
        scratch_shapes=edge_scratch(modes, elems),
        compiler_params=pltpu.CompilerParams(vmem_limit_bytes=48 * MIB),
        cost_estimate=pl.CostEstimate(
            flops=256 * modes * elems * elems, bytes_accessed=24 * MIB, transcendentals=0
        ),
    )(rhs, geo, mass, flag, mask, halo, far, local, edges)


def second_apply_kernel(
    blocks,
    q0_ref,
    geo_ref,
    mass_ref,
    flag_ref,
    halo_ref,
    far_ref,
    local_ref,
    edges_ref,
    sums_ref,
    out_ref,
    trace_ref,
    parts_ref,
    val_ref,
    acc_ref,
    more_ref,
):
    step = pl.program_id(0)
    modes, elems = val_ref.shape[1:]

    @pl.when(step == 0)
    def _():
        more_ref[...] = jnp.zeros_like(more_ref)

    @pl.when(step < blocks)
    def _():
        lanes = pl.ds(pl.multiple_of(step * LANES, LANES), LANES)

        def tile(part, _):
            rows = pl.ds(pl.multiple_of(part * 8, 8), 8)
            totals = [None, None]

            def visit(node, value, image):
                for k, term in enumerate((value * value, value * image)):
                    totals[k] = term if totals[k] is None else totals[k] + term

            volume(
                lambda node: q0_ref[node, rows, lanes],
                acc_ref,
                geo_ref,
                mass_ref,
                rows,
                lanes,
                visit,
            )
            for k in range(2):
                more_ref[k, rows, :] += totals[k]
            return 0

        lax.fori_loop(0, modes // 8, tile, 0)

    @pl.when(step == blocks)
    def _():
        fill_traces(q0_ref, trace_ref)
        fill_halo(halo_ref, parts_ref)

    for edge in range(4):

        @pl.when(step == blocks + edge)
        def _():
            gathered(trace_ref, parts_ref, local_ref, far_ref, val_ref)
            totals = [None]

            def visit(node, lanes, mine, term):
                product = mine * term
                totals[0] = product if totals[0] is None else totals[0] + product

            penalties(edge, q0_ref, val_ref, edges_ref, flag_ref, visit)
            more_ref[1] += totals[0]

    @pl.when(step == blocks + 3)
    def _():
        lane = lane_of((modes, LANES))
        sums = [sums_ref[0], sums_ref[1], more_ref[0], more_ref[1]]
        packed = jnp.zeros((modes, LANES), jnp.float32)
        for k, value in enumerate(sums):
            packed = jnp.where(lane == k, jnp.sum(value, axis=1, keepdims=True), packed)
        out_ref[...] = packed


def second_apply(q0, geo, mass, flag, halo, far, local, edges, sums):
    _, modes, elems = q0.shape
    blocks = elems // LANES
    block_of = lambda s: jnp.minimum(s, blocks - 1)
    far_spec, local_spec, edges_spec = edge_specs(blocks, elems)
    return pl.pallas_call(
        functools.partial(second_apply_kernel, blocks),
        grid=(blocks + 4,),
        in_specs=[
            whole((64, modes, elems)),
            pl.BlockSpec((8, LANES), lambda s: (0, block_of(s))),
            whole((modes, LANES)),
            whole((modes, LANES)),
            whole((2, 8, modes, LANES)),
            far_spec,
            local_spec,
            edges_spec,
            whole((2, modes, LANES)),
        ],
        out_specs=whole((modes, LANES)),
        out_shape=jax.ShapeDtypeStruct((modes, LANES), jnp.float32),
        scratch_shapes=edge_scratch(modes, elems) + [pltpu.VMEM((2, modes, LANES), jnp.float32)],
        compiler_params=pltpu.CompilerParams(vmem_limit_bytes=48 * MIB),
        cost_estimate=pl.CostEstimate(
            flops=256 * modes * elems * elems, bytes_accessed=12 * MIB, transcendentals=0
        ),
    )(q0, geo, mass, flag, halo, far, local, edges, sums)


def finish_kernel(r0_ref, q0_ref, sums_ref, out_ref):
    modes = out_ref.shape[0]
    total = sums_ref[0]
    for k in range(1, sums_ref.shape[0]):
        total = total + sums_ref[k]
    m0, m1, m2, m3 = [total[:, k : k + 1] for k in range(4)]
    alpha = m0 / m1
    norm = alpha * (alpha * m2) - 2.0 * (alpha * m1) + m0
    energy = m1 - 2.0 * (alpha * m2) + alpha * (alpha * m3)
    beta = norm / m0
    second = norm / (energy - beta * (norm / alpha))
    on_r = jnp.broadcast_to(alpha + second * (1.0 + beta), (modes, LANES))
    on_q = jnp.broadcast_to(second * alpha, (modes, LANES))
    for node in range(64):
        out_ref[:, node, :] = on_r * r0_ref[node] - on_q * q0_ref[node]


def finish(r0, q0, sums):
    _, modes, elems = r0.shape
    field = pl.BlockSpec((64, modes, LANES), lambda b: (0, 0, b))
    return pl.pallas_call(
        finish_kernel,
        grid=(elems // LANES,),
        in_specs=[field, field, whole(sums.shape)],
        out_specs=pl.BlockSpec((modes, 64, LANES), lambda b: (0, 0, b)),
        out_shape=jax.ShapeDtypeStruct((modes, 64, elems), jnp.float32),
        compiler_params=pltpu.CompilerParams(vmem_limit_bytes=24 * MIB),
    )(r0, q0, sums)


def shifted(value, axis, steps):
    size = lax.axis_size(axis)
    return lax.ppermute(value, axis, [(i, (i + steps) % size) for i in range(size)])


def both_sides(send):
    return jnp.stack([shifted(send, "xy", -1), shifted(send, "xy", 1)])


def pad_rows(values, rows=8):
    return jnp.pad(values, ((0, rows - values.shape[0]), (0, 0)))


def edge_tables(nbr_elem, nbr_edge):
    elems = nbr_elem.shape[1]
    me, size = lax.axis_index("xy"), lax.axis_size("xy")
    wall = nbr_elem < 0
    ids = jnp.maximum(nbr_elem, 0)
    owner, local_id = ids // elems, ids % elems
    here = (owner == me) & ~wall
    after = (owner == (me + 1) % size) & ~wall & ~here
    before = ~wall & ~here & ~after
    place = jnp.where(here, nbr_edge % 4 * elems + local_id, -1).reshape(-1)
    source = jnp.arange(4 * elems, dtype=jnp.int32)[:, None]
    local = (source == place[None, :]).astype(jnp.bfloat16)
    first = jnp.arange(LANES) < ROWS

    def ends(table):
        return jnp.where(first[None, :], table[:, :LANES], table[:, elems - LANES :])

    send = jnp.where(first[None, :], before[:, :LANES], after[:, elems - LANES :])
    slot = jnp.where(after, local_id, local_id - (elems - ROWS) + ROWS)
    slot = jnp.where(send, ends(slot), -1).reshape(-1)
    far = (jnp.arange(LANES, dtype=jnp.int32)[:, None] == slot[None, :]).astype(jnp.bfloat16)
    flags = jnp.stack([wall, nbr_edge >= 4], axis=1).astype(jnp.float32)
    flags = jnp.pad(flags, ((0, 0), (0, 6), (0, 0))).reshape(32, elems)
    return local, far, pad_rows(send.astype(jnp.float32)), flags


def per_device(concentration, geometry, nbr_elem, nbr_edge, wall_flags):
    planes, _, elems = concentration.shape
    groups = lax.axis_size("gz")
    me = lax.axis_index("gz")
    total = planes * groups
    fold = Fold(elems // groups)
    scale_x, scale_y = geometry[0], geometry[1]
    jacobian = 1.0 / (scale_x * scale_y)
    geo = pad_rows(
        jnp.stack([jacobian, jacobian * scale_x * scale_x, jacobian * scale_y * scale_y])
    )
    mine = lax.dynamic_slice_in_dim(geo, me * fold.width, fold.width, axis=1)
    sent = pack(concentration, fold, groups)
    field = lax.all_to_all(sent, "gz", split_axis=0, concat_axis=0, tiled=True)
    modes_of = right_hand_side(field, jnp.tile(mine, (1, fold.parts)), fold, total)
    rhs = lax.all_to_all(modes_of, "gz", split_axis=0, concat_axis=0, tiled=True)

    mode_ids = me * planes + jnp.arange(planes, dtype=jnp.int32)
    wave = ((mode_ids + 1) // 2).astype(jnp.float32)
    mass = jnp.broadcast_to(
        (1.0 / time_step + axial_stiffness * wave * wave)[:, None], (planes, LANES)
    )
    flag = jnp.broadcast_to(wall_flags.astype(jnp.float32)[:, None], (planes, LANES))
    local, far, mask, edges = edge_tables(nbr_elem, nbr_edge)
    halo = both_sides(first_send(rhs, mask, fold))
    r0, q0, send, sums = first_apply(rhs, geo, mass, flag, mask, halo, far, local, edges, fold)
    packed = second_apply(q0, geo, mass, flag, both_sides(send), far, local, edges, sums)
    size = lax.axis_size("xy")
    packs = jnp.stack([packed] + [shifted(packed, "xy", k) for k in range(1, size)])
    return finish(r0, q0, packs)


def solution(mesh):
    return jax.shard_map(
        per_device,
        mesh=mesh,
        in_specs=(P("gz", None, "xy"), P(None, "xy"), P(None, "xy"), P(None, "xy"), P("gz")),
        out_specs=P("gz", None, "xy"),
        check_vma=False,
    )
```

time: 805 us -> 284 us (0.35)
  local copies, waits for them, and re-layouts: 291 us -> 10 us
  other arithmetic: 155 us -> 7.76 us
  matrix products: 110 us -> 0 us
  Pallas kernels: 0 us -> 59.5 us
  blocking collectives: 18.6 us -> 0 us
  waiting for transfers between devices: 195 us -> 182 us
    dot_general x14 -> x0, matrix products: 110 us -> none  [the longest x1 21.6 us: per_device(): jnp.einsum('kp,pne->kne', fourier, lax.all_to_all(explicit, 'gz', split_a...]
    scatter-add x6 -> x0, local copies, waits for them, and re-layouts: 64.9 us -> none  [the longest x2 22.7 us: add_edges(): grid = grid.at[:, :, 0, :].add(penalty[:, :, 3])]
    pallas_call x0 -> x6, Pallas kernels: none -> 59.5 us  [the longest x1 19.4 us: right_hand_side(): pl.pallas_call(functools.partial(rhs_kernel, fold, groups, planes), grid=...]
    unnamed x55 -> x21, local copies, waits for them, and re-layouts: 58.4 us -> 8.41 us
    all_to_all x3 -> x0, other arithmetic: 41.6 us -> none  [the longest x1 14.1 us: per_device(): lax.all_to_all(explicit_hat - axial_mobility * (wave_all * wave_all)[:, N...]
    all_to_all x5 -> x0, local copies, waits for them, and re-layouts: 41.6 us -> none  [the longest x2 21.9 us: per_device(): lax.all_to_all(explicit_hat - axial_mobility * (wave_all * wave_all)[:, N...]
    gather x2 -> x0, local copies, waits for them, and re-layouts: 39.7 us -> none  [per_device(): values = jnp.take(flat, position, axis=2).reshape(modes_dev, 8, 4, elems)]
    reshape x5 -> x1, local copies, waits for them, and re-layouts: 34 us -> 0.02 us  [edge_tables(): flags = jnp.pad(flags, ((0, 0), (0, 6), (0, 0))).reshape(32, elems)]
  transfers between devices with their start and end apart: 7 -> 9, of which waited for: 3 -> 9; matrix products, arithmetic and copies ran while one was open for 13% -> 3% of each run, Pallas kernels for 0% -> 0%
where the time goes in v1:
time: 284 us; the launch traced here: 280 us
  waiting for transfers between devices  182 us (64%)
  Pallas kernels  59.5 us (21%)
  starting transfers between devices  20.1 us (7%)
  local copies, waits for them, and re-layouts  10 us (4%)
  other arithmetic  7.76 us (3%)
    all_to_all x1, waiting for transfers between devices, per_device(): field = lax.all_to_all(sent, 'gz', split_axis=0, concat_axis=0, tiled=True)  90.5 us
    all_to_all x1, waiting for transfers between devices, per_device(): lax.all_to_all(modes_of, 'gz', split_axis=0, concat_axis=0, tiled=True)  82.3 us
    pallas_call x1, Pallas kernels, right_hand_side(): pl.pallas_call(functools.partial(rhs_kernel, fold, groups, planes), grid=...  19.4 us
    pallas_call x1, Pallas kernels, first_apply(): pl.pallas_call(functools.partial(first_apply_kernel, fold, blocks), grid=...  16.4 us
    pallas_call x1, Pallas kernels, second_apply(): pl.pallas_call(functools.partial(second_apply_kernel, blocks), grid=(bloc...  12.3 us
    ppermute x7, waiting for transfers between devices, shifted(): lax.ppermute(value, axis, [(i, (i + steps) % size) for i in range(size)])  9.27 us
    unnamed x21, local copies, waits for them, and re-layouts  8.41 us
    pallas_call x1, Pallas kernels, finish(): pl.pallas_call(finish_kernel, grid=(elems // LANES,), in_specs=[field, fi...  7.6 us
  transfers between devices with their start and end apart: 9, of which 9 were waited for; matrix products, arithmetic and copies ran while one was open for 3% of the time, Pallas kernels for 0%

profile of v1, /device:TPU:8, one launch (start us, length us, event | category | flops | bytes accessed | tf_op | source)
XLA Modules:
  0.0 279.7 jit_solution(4572296215331114506)
XLA Ops:
  0.0 2.2 copy-done.2
  2.2 3.6 %shard_map.73 = f32[8,32,32,128]{3,2,1,0:T(8,128)S(1)} custom-call(f32[32,64,512]{2,1,0:T(8,128)S(1)} %copy-done.2), custom_call_target="tpu_custom_call" | custom-call | flops 1048576 | bytes 8388608 | tf_op jit(solution)/shard_map/pallas_call | solution.py:175
  5.9 2.0 copy-done.1
  7.9 6.4 %all-to-all-start = ((f32[8,32,32,128]{3,2,1,0:T(8,128)}), f32[8,32,32,128]{3,2,1,0:T(8,128)}, u32[]{:S(2)}, u32[]{:S(2)}) async-start(f32[8,32,32,128]{3,2,1,0:T(8,128)} %copy-done.1), calls=%async_computation | async-start | bytes 8388608 | tf_op jit(solution)/shard_map/all_to_all | solution.py:754
  14.5 90.5 %all-to-all-done.y_ref = f32[8,32,32,128]{3,2,1,0:T(8,128)} async-done(((f32[8,32,32,128]{3,2,1,0:T(8,128)}), f32[8,32,32,128]{3,2,1,0:T(8,128)}, u32[]{:S(2)}, u32[]{:S(2)}) %all-to-all-start) | async-done | bytes 4194336 | tf_op jit(solution)/shard_map/all_to_all | solution.py:754
  105.0 19.4 %shard_map.74 = f32[8,32,32,128]{3,2,1,0:T(8,128)S(1)} custom-call(bf16[256,1024]{1,0:T(8,128)(2,1)S(1)} %copy-done.4, bf16[256,512]{1,0:T(8,128)(2,1)S(1)} %copy-done.5, f32[8,32,32,128]{3,2,1,0:T(8,128)} %all-to-all-done.y_ref, f32[8,128]{1,0:T(8,128)S(1)} %tile.10.geo_ref), custom_call_target="tpu_custom_call" | custom-call | flops 3221225472 | bytes 8388608 | tf_op jit(solution)/shard_map/pallas_call | solution.py:274
  124.4 2.0 copy-done.3
  126.4 7.2 %all-to-all-start.1 = ((f32[8,32,32,128]{3,2,1,0:T(8,128)}), f32[8,32,32,128]{3,2,1,0:T(8,128)}, u32[]{:S(2)}, u32[]{:S(2)}) async-start(f32[8,32,32,128]{3,2,1,0:T(8,128)} %copy-done.3), calls=%async_computation.1 | async-start | bytes 8388608 | tf_op jit(solution)/shard_map/all_to_all | solution.py:756
  133.8 7.4 %fusion.local_ref = bf16[2048,2048]{1,0:T(8,128)(2,1)} fusion(s32[2048]{0:T(1024)S(1)} %bitcast.27), kind=kLoop, calls=%fused_computation.1 | loop fusion | flops 8388608 | bytes 8396800 | tf_op jit(solution)/shard_map/convert_element_type | solution.py:726
  141.3 82.3 %all-to-all-done.1.r_ref = f32[8,32,32,128]{3,2,1,0:T(8,128)} async-done(((f32[8,32,32,128]{3,2,1,0:T(8,128)}), f32[8,32,32,128]{3,2,1,0:T(8,128)}, u32[]{:S(2)}, u32[]{:S(2)}) %all-to-all-start.1) | async-done | bytes 4194336 | tf_op jit(solution)/shard_map/all_to_all | solution.py:756
  223.6 1.3 fusion.14
  225.2 1.7 collective-permute-start
  227.1 2.6 collective-permute-done.1
  230.2 16.4 %shard_map.76 = (f32[64,32,512]{2,1,0:T(8,128)S(1)}, f32[64,32,512]{2,1,0:T(8,128)}, f32[8,32,128]{2,1,0:T(8,128)S(1)}, f32[2,32,128]{2,1,0:T(8,128)S(1)}) custom-call(f32[8,32,32,128]{3,2,1,0:T(8,128)} %all-to-all-done.1.r_ref, f32[8,512]{1,0:T(8,128)S(1)} %select_maximum_fusion.geo_ref, f32[32,128]{1,0:T(8,128)S(1)} %broadcast_in_dim.25.mass_ref, ...), custom_call_target="tpu_custom_call" | custom-call | flops 2147483648 | bytes 25165824 | tf_op jit(solution)/shard_map/pallas_call | solution.py:528
  246.6 1.2 collective-permute-start.3
  247.8 0.7 collective-permute-start.2
  248.5 2.6 collective-permute-done.3
  251.6 2.2 copy-done
  253.8 12.3 %shard_map.77 = f32[32,128]{1,0:T(8,128)S(1)} custom-call(f32[64,32,512]{2,1,0:T(8,128)S(1)} %copy-done, f32[8,512]{1,0:T(8,128)S(1)} %select_maximum_fusion.geo_ref, f32[32,128]{1,0:T(8,128)S(1)} %broadcast_in_dim.25.mass_ref, f32[32,128]{1,0:T(8,128)S(1)} %broadcast_in_dim.27.flag_ref, f32[2,8,32,128]{3,2,1,0:T(8,128)S(1)} %pad_maximum_fusion.2.halo_ref, ...), custom_call_target="tpu_custom_call" | custom-call | flops 2147483648 | bytes 12582912 | tf_op jit(solution)/shard_map/pallas_call | solution.py:648
  266.1 1.9 collective-permute-start.6
  268.0 0.9 collective-permute-start.5
  269.0 0.5 collective-permute-done.6
  269.5 2.3 collective-permute-done.5
  272.1 7.6 %shard_map.78 = f32[32,64,512]{2,1,0:T(8,128)} custom-call(f32[64,32,512]{2,1,0:T(8,128)S(1)} %get-tuple-element.9.r0_ref, f32[64,32,512]{2,1,0:T(8,128)S(1)} %copy-done, f32[4,32,128]{2,1,0:T(8,128)S(1)} %pad_maximum_fusion.3.sums_ref), custom_call_target="tpu_custom_call" | custom-call | tf_op jit(solution)/shard_map/pallas_call | solution.py:692
  (49 shorter events, 2.2 us)
Async XLA Ops:
  0.0 2.2 copy-start.2
  5.8 2.0 copy-start.1
  7.9 6.4 %copy-start.8 = (f32[2,512]{1,0:T(2,128)S(1)}, f32[2,512]{1,0:T(2,128)}, u32[]{:S(2)}) copy-start(f32[2,512]{1,0:T(2,128)} %param.8) | copy-start | bytes 12292
  7.9 97.1 %copy-start.4 = (bf16[256,1024]{1,0:T(8,128)(2,1)S(1)}, bf16[256,1024]{1,0:T(8,128)(2,1)}, u32[]{:S(2)}) copy-start(bf16[256,1024]{1,0:T(8,128)(2,1)} %constant.98.clone.first_ref) | copy-start | bytes 1572868
  7.9 97.1 %copy-start.5 = (bf16[256,512]{1,0:T(8,128)(2,1)S(1)}, bf16[256,512]{1,0:T(8,128)(2,1)}, u32[]{:S(2)}) copy-start(bf16[256,512]{1,0:T(8,128)(2,1)} %constant.99.clone.second_ref) | copy-start | bytes 786436
  7.9 97.1 %all-to-all-start = ((f32[8,32,32,128]{3,2,1,0:T(8,128)}), f32[8,32,32,128]{3,2,1,0:T(8,128)}, u32[]{:S(2)}, u32[]{:S(2)}) async-start(f32[8,32,32,128]{3,2,1,0:T(8,128)} %copy-done.1), calls=%async_computation | async-start | bytes 8388608 | tf_op jit(solution)/shard_map/all_to_all | solution.py:754
  124.4 2.0 copy-start.3
  126.4 7.2 %copy-start.6 = (s32[4,512]{1,0:T(4,128)S(1)}, s32[4,512]{1,0:T(4,128)}, u32[]{:S(2)}) copy-start(s32[4,512]{1,0:T(4,128)} %param.9) | copy-start | bytes 24580
  126.4 7.2 %copy-start.7 = (s32[4,512]{1,0:T(4,128)S(1)}, s32[4,512]{1,0:T(4,128)}, u32[]{:S(2)}) copy-start(s32[4,512]{1,0:T(4,128)} %param.10) | copy-start | bytes 24580
  126.4 97.2 %all-to-all-start.1 = ((f32[8,32,32,128]{3,2,1,0:T(8,128)}), f32[8,32,32,128]{3,2,1,0:T(8,128)}, u32[]{:S(2)}, u32[]{:S(2)}) async-start(f32[8,32,32,128]{3,2,1,0:T(8,128)} %copy-done.3), calls=%async_computation.1 | async-start | bytes 8388608 | tf_op jit(solution)/shard_map/all_to_all | solution.py:756
  141.3 85.7 %copy-start.9 = (s32[32]{0:T(128)S(1)}, s32[32]{0:T(128)}, u32[]{:S(2)}) copy-start(s32[32]{0:T(128)} %param.11) | copy-start | bytes 388
  225.2 4.4 %collective-permute-start.1 = (f32[8,32,128]{2,1,0:T(8,128)S(1)}, f32[8,32,128]{2,1,0:T(8,128)S(1)}, u32[]{:S(2)}, u32[]{:S(2)}) collective-permute-start(f32[8,32,128]{2,1,0:T(8,128)S(1)} %shard_map.75), channel_id=1, source_target_pairs={{0,8},{8,16},{16,24},{24,0},{1,9},{9,17},{17,25},{25,1},{2,10},{10... | collective-permute-start | bytes 393224 | tf_op jit(solution)/shard_map/ppermute | solution.py:704
  225.2 4.8 %collective-permute-start = (f32[8,32,128]{2,1,0:T(8,128)S(1)}, f32[8,32,128]{2,1,0:T(8,128)S(1)}, u32[]{:S(2)}, u32[]{:S(2)}) collective-permute-start(f32[8,32,128]{2,1,0:T(8,128)S(1)} %shard_map.75), channel_id=1, source_target_pairs={{0,24},{8,0},{16,8},{24,16},{1,25},{9,1},{17,9},{25,17},{2,26},{10... | collective-permute-start | bytes 393224 | tf_op jit(solution)/shard_map/ppermute | solution.py:704
  246.6 4.6 %collective-permute-start.3 = (f32[8,32,128]{2,1,0:T(8,128)S(1)}, f32[8,32,128]{2,1,0:T(8,128)S(1)}, u32[]{:S(2)}, u32[]{:S(2)}) collective-permute-start(f32[8,32,128]{2,1,0:T(8,128)S(1)} %get-tuple-element.11), channel_id=1, source_target_pairs={{0,8},{8,16},{16,24},{24,0},{1,9},{9,17},{17,25},{25,1},{2,10},{10... | collective-permute-start | bytes 393224 | tf_op jit(solution)/shard_map/ppermute | solution.py:704
  247.8 3.8 %collective-permute-start.2 = (f32[8,32,128]{2,1,0:T(8,128)S(1)}, f32[8,32,128]{2,1,0:T(8,128)S(1)}, u32[]{:S(2)}, u32[]{:S(2)}) collective-permute-start(f32[8,32,128]{2,1,0:T(8,128)S(1)} %get-tuple-element.11), channel_id=1, source_target_pairs={{0,24},{8,0},{16,8},{24,16},{1,25},{9,1},{17,9},{25,17},{2,26},{10... | collective-permute-start | bytes 393224 | tf_op jit(solution)/shard_map/ppermute | solution.py:704
  251.6 2.2 copy-start
  266.1 3.4 %collective-permute-start.6 = (f32[32,128]{1,0:T(8,128)S(1)}, f32[32,128]{1,0:T(8,128)S(1)}, u32[]{:S(2)}, u32[]{:S(2)}) collective-permute-start(f32[32,128]{1,0:T(8,128)S(1)} %shard_map.77), channel_id=1, source_target_pairs={{0,24},{8,0},{16,8},{24,16},{1,25},{9,1},{17,9},{25,17},{2,26},{10... | collective-permute-start | bytes 49160 | tf_op jit(solution)/shard_map/ppermute | solution.py:704
  268.0 3.7 %collective-permute-start.5 = (f32[32,128]{1,0:T(8,128)S(1)}, f32[32,128]{1,0:T(8,128)S(1)}, u32[]{:S(2)}, u32[]{:S(2)}) collective-permute-start(f32[32,128]{1,0:T(8,128)S(1)} %shard_map.77), channel_id=1, source_target_pairs={{0,16},{8,24},{16,0},{24,8},{1,17},{9,25},{17,1},{25,9},{2,18},{10... | collective-permute-start | bytes 49160 | tf_op jit(solution)/shard_map/ppermute | solution.py:704
  269.0 3.2 %collective-permute-start.4 = (f32[32,128]{1,0:T(8,128)S(1)}, f32[32,128]{1,0:T(8,128)S(1)}, u32[]{:S(2)}, u32[]{:S(2)}) collective-permute-start(f32[32,128]{1,0:T(8,128)S(1)} %shard_map.77), channel_id=1, source_target_pairs={{0,8},{8,16},{16,24},{24,0},{1,9},{9,17},{17,25},{25,1},{2,10},{10... | collective-permute-start | bytes 49160 | tf_op jit(solution)/shard_map/ppermute | solution.py:704

commit v2 on v0

v2 whole, which is shorter than its diff:
```python
import functools

import jax
import jax.numpy as jnp
import ml_dtypes
import numpy as np
from jax import lax
from jax.experimental import pallas as pl
from jax.experimental.pallas import tpu as pltpu
from jax.sharding import PartitionSpec as P

ROWS = 64
LANES = 128
MIB = 1024 * 1024

time_step = 0.2
axial_stiffness = 0.002
plane_stiffness = 1.0
edge_penalty = 4.0
axial_mobility = 0.002
mobility_floor = 0.05


def point_tables():
    degree = 7
    points = np.arange(degree + 1)
    theta = np.pi * points / degree
    nodes_x = np.cos(theta)
    signs = np.where((points == 0) | (points == degree), 2.0, 1.0) * (-1.0) ** points
    differ = nodes_x[:, None] - nodes_x[None, :]
    deriv = np.outer(signs, 1.0 / signs) / (differ + np.eye(degree + 1))
    deriv = deriv - np.eye(degree + 1) * deriv.sum(axis=1)[:, None]
    inner = np.ones(degree - 1)
    for number in range(1, (degree - 1) // 2 + 1):
        inner = inner - 2.0 * np.cos(2 * number * theta[1:degree]) / (4 * number * number - 1)
    weights = np.zeros(degree + 1)
    weights[1:degree] = 2.0 * inner / degree
    weights[0] = 1.0 / degree**2
    weights[degree] = 1.0 / degree**2
    return (deriv, weights)


def fourier_table(length):
    planes = np.arange(length)
    wave_no = (planes + 1) // 2
    phase = np.outer(wave_no, planes) % length * (2.0 * np.pi / length)
    table = np.where((planes % 2 == 1)[:, None], np.cos(phase), np.sin(phase)) * np.sqrt(
        2.0 / length
    )
    table[0] = 1.0 / np.sqrt(length)
    table[length - 1] = np.cos(phase[length - 1]) / np.sqrt(length)
    return table


DERIV, WEIGHTS = point_tables()
BACK = DERIV.T * WEIGHTS[None, :]
STIFF = BACK @ DERIV
BACK_SCALED = BACK / WEIGHTS[:, None]


def two_parts(table):
    upper = table.astype(np.float32).astype(ml_dtypes.bfloat16)
    lower = (table - upper.astype(np.float64)).astype(np.float32).astype(ml_dtypes.bfloat16)
    return upper, lower


def split(value):
    upper = value.astype(jnp.bfloat16)
    lower = (value - upper.astype(jnp.float32)).astype(jnp.bfloat16)
    return upper, lower


class Fold:
    def __init__(self, width):
        self.width = width
        self.parts = LANES // width
        self.fold_j = 2 if self.parts >= 2 else 1
        self.fold_i = 2 if self.parts >= 4 else 1
        self.count_j = 8 // self.fold_j
        self.count_i = 8 // self.fold_i
        self.slots = self.count_j * self.count_i

    def slot(self, jp, ip):
        return jp * self.count_i + ip

    def node(self, jp, ip, part):
        half_j, half_i = part // self.fold_i, part % self.fold_i
        j = 7 - jp if half_j else jp
        i = 7 - ip if half_i else ip
        return 8 * j + i

    def place(self, node):
        j, i = node // 8, node % 8
        half_j = 1 if j >= self.count_j else 0
        half_i = 1 if i >= self.count_i else 0
        jp = 7 - j if half_j else j
        ip = 7 - i if half_i else i
        return self.slot(jp, ip), half_j * self.fold_i + half_i


def lane_of(shape):
    return lax.broadcasted_iota(jnp.int32, shape, len(shape) - 1)


def rolled(value, lanes):
    lanes = lanes % LANES
    return value if lanes == 0 else pltpu.roll(value, lanes, value.ndim - 1)


def by_part(values, lane, width):
    out = values[0]
    for r in range(1, len(values)):
        out = jnp.where(lane >= r * width, values[r], out)
    return out


def mirrored(value, lane, shift):
    if 2 * shift == LANES:
        return rolled(value, shift)
    return jnp.where((lane & shift) == 0, rolled(value, -shift), rolled(value, shift))


def combine(coefs, values):
    total = None
    for c, v in zip(coefs, values):
        term = v * np.float32(c)
        total = term if total is None else total + term
    return total


def line_apply(matrix, values, sign):
    even = [values[k] + values[7 - k] for k in range(4)]
    odd = [values[k] - values[7 - k] for k in range(4)]
    out = [None] * 8
    for a in range(4):
        from_even = combine([(matrix[a, b] + matrix[a, 7 - b]) / 2 for b in range(4)], even)
        from_odd = combine([(matrix[a, b] - matrix[a, 7 - b]) / 2 for b in range(4)], odd)
        out[a] = from_even + from_odd
        out[7 - a] = from_even - from_odd if sign > 0 else from_odd - from_even
    return out


def derivative_line(matrix, values, back, swap):
    if swap is None:
        return line_apply(matrix, values, -1)
    other = [swap(v) for v in values]
    sign = -1.0 if back else 1.0
    out = []
    for a in range(4):
        coefs = [matrix[a, b] for b in range(4)] + [sign * matrix[a, 7 - b] for b in range(4)]
        out.append(combine(coefs, list(values) + other))
    return out


EDGE_NODES = [
    [t for t in range(8)],
    [8 * t + 7 for t in range(8)],
    [56 + t for t in range(8)],
    [8 * t for t in range(8)],
]


def swapped(me, values):
    bit = 1
    while bit < len(values):
        flip = (me & bit) != 0
        values = [jnp.where(flip, values[r ^ bit], values[r]) for r in range(len(values))]
        bit *= 2
    return values


def pack_kernel(fold, me_ref, c_ref, *out_refs):
    lane = lane_of((c_ref.shape[0], LANES))
    me = me_ref[0]
    for step in range(len(out_refs) // fold.parts):

        @pl.when(pl.program_id(0) == step)
        def _():
            for jp in range(fold.count_j):
                for ip in range(fold.count_i):
                    loads = [c_ref[:, fold.node(jp, ip, q), :] for q in range(fold.parts)]
                    made = []
                    for r in range(fold.parts):
                        parts = [rolled(loads[q], (q - r) * fold.width) for q in range(fold.parts)]
                        made.append(by_part(parts, lane, fold.width))
                    for p, value in enumerate(swapped(me, made)):
                        out_refs[step * fold.parts + p][fold.slot(jp, ip)] = value


def pack(me, conc, fold, groups, first):
    planes, nodes, elems = conc.shape
    count = groups // 2
    offset = first // fold.parts

    def block(step, me_ref):
        return (0, 0, (step + offset) ^ (me_ref[0] // fold.parts))

    slot = jax.ShapeDtypeStruct((fold.slots, planes, LANES), jnp.float32)
    return pl.pallas_call(
        functools.partial(pack_kernel, fold),
        grid_spec=pltpu.PrefetchScalarGridSpec(
            num_scalar_prefetch=1,
            grid=(count // fold.parts,),
            in_specs=[pl.BlockSpec((planes, nodes, LANES), block)],
            out_specs=[pl.BlockSpec(slot.shape, lambda s, me_ref: (0, 0, 0))] * count,
        ),
        out_shape=[slot] * count,
        compiler_params=pltpu.CompilerParams(vmem_limit_bytes=60 * MIB),
        cost_estimate=pl.CostEstimate(
            flops=conc.size, bytes_accessed=4 * conc.size, transcendentals=0
        ),
    )(me, conc)


def plane_terms(fold, y_ref, geo_ref, x_ref, acc_ref, row, base, half):
    lane = lane_of((16, LANES))
    square_x = jnp.broadcast_to(geo_ref[1:2, :], (16, LANES))
    square_y = jnp.broadcast_to(geo_ref[2:3, :], (16, LANES))

    def conc(jp, ip):
        return y_ref[fold.slot(jp, ip), pl.ds(base, 16), :]

    def potential(c):
        square = c * c
        return square * c - c, jnp.maximum(1.0 - square, mobility_floor)

    def flux(fields, swap):
        pairs = [potential(c) for c in fields]
        slope = derivative_line(DERIV, [p[0] for p in pairs], False, swap)
        scaled = [s * p[1] for s, p in zip(slope, pairs)]
        return derivative_line(BACK_SCALED, scaled, True, swap), pairs

    swap_i = None
    if fold.fold_i == 2:
        swap_i = lambda v: mirrored(v, lane, fold.width)
    swap_j = None
    if fold.fold_j == 2:
        swap_j = lambda v: mirrored(v, lane, fold.width * fold.fold_i)
    for jp in range(fold.count_j):
        fields = [conc(jp, ip) for ip in range(fold.count_i)]
        result, _unused = flux(fields, swap_i)
        for ip in range(fold.count_i):
            acc_ref[fold.slot(jp, ip)] = (
                fields[ip] * np.float32(1.0 / time_step) - result[ip] * square_x
            )
    for ip in range(fold.count_i):
        fields = [conc(jp, ip) for jp in range(fold.count_j)]
        result, pairs = flux(fields, swap_j)
        for jp in range(fold.count_j):
            slot = fold.slot(jp, ip)
            explicit = acc_ref[slot] - result[jp] * square_y
            where = pl.ds((slot % 2) * LANES, LANES)
            for kind, value in enumerate((explicit, pairs[jp][0])):
                upper, lower = split(value)
                x_ref[slot // 2, pl.ds(kind * half + row, 16), where] = upper
                x_ref[slot // 2, pl.ds((2 + kind) * half + row, 16), where] = lower


def half_terms(fold, me, first, y_refs, geo_ref, x_ref, acc_ref):
    planes = y_refs[0].shape[1]
    half = len(y_refs) * planes
    for number, y_ref in enumerate(y_refs):
        place = (me ^ (first + number)) % len(y_refs)

        def chunk(part, _, y_ref=y_ref, place=place):
            base = pl.multiple_of(part * 16, 16)
            row = pl.multiple_of(place * planes + base, 16)
            plane_terms(fold, y_ref, geo_ref, x_ref, acc_ref, row, base, half)
            return 0

        lax.fori_loop(0, planes // 16, chunk, 0)


def near_kernel(fold, count, me_ref, geo_ref, *refs):
    y_refs, (x_ref, acc_ref) = refs[:count], refs[count:]
    half_terms(fold, me_ref[0], 0, y_refs, geo_ref, x_ref, acc_ref)


def far_kernel(fold, count, me_ref, geo_ref, table_ref, near_ref, *refs):
    y_refs, out_refs = refs[:count], refs[count : 3 * count]
    x_ref, acc_ref, result_ref = refs[3 * count :]
    planes = y_refs[0].shape[1]
    half = count * planes
    me = me_ref[0]
    half_terms(fold, me, count, y_refs, geo_ref, x_ref, acc_ref)
    mine = me // count
    jac = jnp.broadcast_to(geo_ref[0:1, :], (planes, LANES))

    def product(which, data):
        table = table_ref[which]
        return jnp.dot(
            table[:, : 4 * half], data, preferred_element_type=jnp.float32
        ) + jnp.dot(table[:, 4 * half :], data[: 2 * half], preferred_element_type=jnp.float32)

    for pair in range(fold.slots // 2):
        result_ref[...] = product(mine, near_ref[pair]) + product(1 - mine, x_ref[pair])
        for number, out_ref in enumerate(out_refs):
            rows = pl.ds(pl.multiple_of((me ^ number) * planes, 16), planes)
            for k in range(2):
                slot = 2 * pair + k
                jp, ip = slot // fold.count_i, slot % fold.count_i
                scale = jac * np.float32(WEIGHTS[jp] * WEIGHTS[ip])
                out_ref[slot] = result_ref[rows, k * LANES : (k + 1) * LANES] * scale


def smem():
    return pl.BlockSpec(memory_space=pltpu.SMEM)


def vmem(count):
    return [pl.BlockSpec(memory_space=pltpu.VMEM)] * count


def near_terms(me, geo, fields, fold):
    slots, planes, _ = fields[0].shape
    count = len(fields)
    size = count * fields[0].size
    return pl.pallas_call(
        functools.partial(near_kernel, fold, count),
        in_specs=[smem()] + vmem(1 + count),
        out_specs=vmem(1)[0],
        out_shape=jax.ShapeDtypeStruct(
            (slots // 2, 4 * count * planes, 2 * LANES), jnp.bfloat16
        ),
        scratch_shapes=[pltpu.VMEM((slots, 16, LANES), jnp.float32)],
        compiler_params=pltpu.CompilerParams(vmem_limit_bytes=16 * MIB),
        cost_estimate=pl.CostEstimate(
            flops=80 * size, bytes_accessed=12 * size, transcendentals=0
        ),
    )(me, geo, *fields)


def right_hand_side(me, geo, near, fields, fold):
    slots, planes, _ = fields[0].shape
    count = len(fields)
    total = 2 * count * planes
    half = total // 2
    size = count * fields[0].size
    table = fourier_table(total).astype(np.float32).astype(np.float64)
    wave = ((np.arange(total) + 1) // 2).astype(np.float64)
    upper, lower = two_parts(table)
    upper_b, lower_b = two_parts(-axial_mobility * (wave * wave)[:, None] * table)
    kinds = [upper, upper_b, upper, upper_b, lower, lower_b]
    tables = np.stack(
        [np.concatenate([k[:, h * half : (h + 1) * half] for k in kinds], axis=1) for h in (0, 1)]
    )
    slot = jax.ShapeDtypeStruct((slots, planes, LANES), jnp.float32)
    return pl.pallas_call(
        functools.partial(far_kernel, fold, count),
        in_specs=[smem()] + vmem(3 + count),
        out_specs=vmem(2 * count),
        out_shape=[slot] * (2 * count),
        scratch_shapes=[
            pltpu.VMEM(near.shape, jnp.bfloat16),
            pltpu.VMEM((slots, 16, LANES), jnp.float32),
            pltpu.VMEM((total, 2 * LANES), jnp.float32),
        ],
        compiler_params=pltpu.CompilerParams(vmem_limit_bytes=24 * MIB),
        cost_estimate=pl.CostEstimate(
            flops=12 * total * 2 * size, bytes_accessed=8 * size, transcendentals=0
        ),
    )(me, geo, jnp.asarray(tables), near, *fields)


def edge_send(mask_ref, edge, out_ref):
    for t in range(8):
        total = None
        for a in range(4):
            term = edge(a, t) * mask_ref[a : a + 1, :]
            total = term if total is None else total + term
        out_ref[t] = total


def send_from(field_ref, mask_ref, out_ref):
    modes, elems = field_ref.shape[1:]
    lane = lane_of((modes, LANES))

    def edge(a, t):
        node = EDGE_NODES[a][t]
        ends = field_ref[node, :, :LANES], field_ref[node, :, elems - LANES :]
        return jnp.where(lane < ROWS, ends[0], ends[1])

    edge_send(mask_ref, edge, out_ref)


def unpack_kernel(fold, groups, me_ref, mask_ref, *refs):
    parts, (r0_ref, send_ref) = refs[:groups], refs[groups:]
    modes = r0_ref.shape[1]
    me = me_ref[0]

    def tile(part, _):
        rows = pl.ds(pl.multiple_of(part * 8, 8), 8)
        lane = lane_of((8, LANES))
        for k in range(groups // fold.parts):
            block = k ^ (me // fold.parts)
            lanes = pl.ds(pl.multiple_of(block * LANES, LANES), LANES)
            mine = parts[k * fold.parts : (k + 1) * fold.parts]
            for jp in range(fold.count_j):
                for ip in range(fold.count_i):
                    loads = swapped(me, [ref[fold.slot(jp, ip), rows, :] for ref in mine])
                    for q in range(fold.parts):
                        shifts = [
                            rolled(loads[r], (r - q) * fold.width) for r in range(fold.parts)
                        ]
                        value = by_part(shifts, lane, fold.width)
                        r0_ref[fold.node(jp, ip, q), rows, lanes] = value
        return 0

    lax.fori_loop(0, modes // 8, tile, 0)
    send_from(r0_ref, mask_ref, send_ref)


def unpack(me, mask, parts, fold):
    slots, modes, _ = parts[0].shape
    groups = len(parts)
    elems = groups * fold.width
    size = groups * parts[0].size
    return pl.pallas_call(
        functools.partial(unpack_kernel, fold, groups),
        in_specs=[smem()] + vmem(1 + groups),
        out_specs=vmem(2),
        out_shape=[
            jax.ShapeDtypeStruct((64, modes, elems), jnp.float32),
            jax.ShapeDtypeStruct((8, modes, LANES), jnp.float32),
        ],
        compiler_params=pltpu.CompilerParams(vmem_limit_bytes=4 * MIB),
        cost_estimate=pl.CostEstimate(flops=8 * size, bytes_accessed=8 * size, transcendentals=0),
    )(me, mask, *parts)


def volume_kernel(want_image, field_ref, geo_ref, mass_ref, *refs):
    if want_image:
        image_ref, sums_ref, acc_ref = refs
    else:
        sums_ref, acc_ref = refs
    modes, elems = field_ref.shape[1:]
    sums_ref[...] = jnp.zeros_like(sums_ref)
    tiles = modes // 8

    def tile(number, _):
        rows = pl.ds(pl.multiple_of(number % tiles * 8, 8), 8)
        lanes = pl.ds(pl.multiple_of(number // tiles * LANES, LANES), LANES)
        jac = geo_ref[0:1, lanes] * mass_ref[rows, :]
        square_x = jnp.broadcast_to(geo_ref[0:1, lanes] * geo_ref[1:2, lanes], (8, LANES))
        square_y = jnp.broadcast_to(geo_ref[0:1, lanes] * geo_ref[2:3, lanes], (8, LANES))
        stiff = plane_stiffness * STIFF
        for j in range(8):
            values = [field_ref[8 * j + i, rows, lanes] for i in range(8)]
            result = line_apply(stiff, values, 1)
            scale = square_x * np.float32(WEIGHTS[j])
            mass = jac * np.float32(WEIGHTS[j])
            for i in range(8):
                acc_ref[8 * j + i] = result[i] * scale + (mass * np.float32(WEIGHTS[i])) * values[i]
        totals = [None, None]
        for i in range(8):
            values = [field_ref[8 * j + i, rows, lanes] for j in range(8)]
            result = line_apply(stiff, values, 1)
            scale = square_y * np.float32(WEIGHTS[i])
            for j in range(8):
                image = acc_ref[8 * j + i] + result[j] * scale
                if want_image:
                    image_ref[8 * j + i, rows, lanes] = image
                for k, term in enumerate((values[j] * values[j], values[j] * image)):
                    totals[k] = term if totals[k] is None else totals[k] + term
        for k in range(2):
            sums_ref[k, rows, :] += totals[k]
        return 0

    lax.fori_loop(0, tiles * (elems // LANES), tile, 0)


def volume(field, geo, mass, want_image):
    _, modes, elems = field.shape
    sums = jax.ShapeDtypeStruct((2, modes, LANES), jnp.float32)
    shapes = [jax.ShapeDtypeStruct(field.shape, jnp.float32), sums] if want_image else [sums]
    return pl.pallas_call(
        functools.partial(volume_kernel, want_image),
        in_specs=vmem(3),
        out_specs=vmem(len(shapes)),
        out_shape=shapes,
        scratch_shapes=[pltpu.VMEM((64, 8, LANES), jnp.float32)],
        compiler_params=pltpu.CompilerParams(vmem_limit_bytes=4 * MIB),
        cost_estimate=pl.CostEstimate(
            flops=40 * field.size, bytes_accessed=8 * field.size, transcendentals=0
        ),
    )(field, geo, mass)


def gather_edges(
    field_ref, flag_ref, after_ref, before_ref, far_ref, local_ref, edges_ref, scratch, visit
):
    trace_ref, parts_ref, val_ref = scratch
    modes, elems = field_ref.shape[1:]
    rows = 8 * modes
    lane = lane_of((modes, LANES))
    for a in range(4):
        for t in range(8):
            upper, lower = split(field_ref[EDGE_NODES[a][t]])
            where = pl.ds(a * elems, elems)
            trace_ref[pl.ds(t * modes, modes), where] = upper
            trace_ref[pl.ds((8 + t) * modes, modes), where] = lower
    for t in range(8):
        upper, lower = split(jnp.where(lane < ROWS, after_ref[t], before_ref[t]))
        parts_ref[pl.ds(t * modes, modes), :] = upper
        parts_ref[pl.ds((8 + t) * modes, modes), :] = lower
    for edge in range(4):
        mine = slice(edge * elems, (edge + 1) * elems)
        value = jnp.dot(trace_ref[...], local_ref[:, mine], preferred_element_type=jnp.float32)
        val_ref[...] = (value[:rows] + value[rows:]).reshape(8, modes, elems)
        mine = slice(edge * LANES, (edge + 1) * LANES)
        value = jnp.dot(parts_ref[...], far_ref[:, mine], preferred_element_type=jnp.float32)
        far = (value[:rows] + value[rows:]).reshape(8, modes, LANES)
        wide = lane_of(far.shape)
        val_ref[:, :, :LANES] += jnp.where(wide < ROWS, far, 0.0)
        val_ref[:, :, elems - LANES :] += jnp.where(wide < ROWS, 0.0, far)
        for block in range(elems // LANES):
            lanes = pl.ds(block * LANES, LANES)
            wall = edges_ref[8 * edge : 8 * edge + 1, lanes]
            turned = edges_ref[8 * edge + 1 : 8 * edge + 2, lanes]
            turned = jnp.broadcast_to(turned, (modes, LANES)) > 0.5
            coef = 1.0 - wall * (1.0 - flag_ref[...])
            for t in range(8):
                node = EDGE_NODES[edge][t]
                value = field_ref[node, :, lanes]
                other = jnp.where(turned, val_ref[7 - t, :, lanes], val_ref[t, :, lanes])
                weight = np.float32(edge_penalty * WEIGHTS[t])
                visit(node, lanes, value, weight * (coef * value - other))


def gather_scratch(modes, elems):
    return [
        pltpu.VMEM((16 * modes, 4 * elems), jnp.bfloat16),
        pltpu.VMEM((16 * modes, LANES), jnp.bfloat16),
        pltpu.VMEM((8, modes, elems), jnp.float32),
    ]


def first_edges_kernel(
    q_ref,
    sums_ref,
    mask_ref,
    r0_ref,
    flag_ref,
    after_ref,
    before_ref,
    far_ref,
    local_ref,
    edges_ref,
    q0_ref,
    send_ref,
    out_ref,
    *scratch,
):
    totals = [sums_ref[1]]
    q0_ref[...] = q_ref[...]

    def visit(node, lanes, value, term):
        q0_ref[node, :, lanes] += term
        totals[0] = totals[0] + value * term

    gather_edges(
        r0_ref, flag_ref, after_ref, before_ref, far_ref, local_ref, edges_ref, scratch, visit
    )
    out_ref[0] = sums_ref[0]
    out_ref[1] = totals[0]
    send_from(q0_ref, mask_ref, send_ref)


def second_edges_kernel(
    first_ref,
    second_ref,
    q0_ref,
    flag_ref,
    after_ref,
    before_ref,
    far_ref,
    local_ref,
    edges_ref,
    out_ref,
    *scratch,
):
    totals = [second_ref[1]]

    def visit(node, lanes, value, term):
        totals[0] = totals[0] + value * term

    gather_edges(
        q0_ref, flag_ref, after_ref, before_ref, far_ref, local_ref, edges_ref, scratch, visit
    )
    modes = q0_ref.shape[1]
    lane = lane_of((modes, LANES))
    sums = [first_ref[0], first_ref[1], second_ref[0], totals[0]]
    packed = jnp.zeros((modes, LANES), jnp.float32)
    for k, value in enumerate(sums):
        packed = jnp.where(lane == k, jnp.sum(value, axis=1, keepdims=True), packed)
    out_ref[...] = packed


def edges_cost(modes, elems):
    return pl.CostEstimate(
        flops=256 * modes * elems * elems,
        bytes_accessed=8 * elems * elems * 4,
        transcendentals=0,
    )


def first_edges(image, sums, mask, field, rest):
    _, modes, elems = field.shape
    return pl.pallas_call(
        first_edges_kernel,
        in_specs=vmem(4 + len(rest)),
        out_specs=vmem(3),
        out_shape=[
            jax.ShapeDtypeStruct(field.shape, jnp.float32),
            jax.ShapeDtypeStruct((8, modes, LANES), jnp.float32),
            jax.ShapeDtypeStruct((2, modes, LANES), jnp.float32),
        ],
        scratch_shapes=gather_scratch(modes, elems),
        input_output_aliases={0: 0},
        compiler_params=pltpu.CompilerParams(vmem_limit_bytes=16 * MIB),
        cost_estimate=edges_cost(modes, elems),
    )(image, sums, mask, field, *rest)


def second_edges(first, second, field, rest):
    _, modes, elems = field.shape
    return pl.pallas_call(
        second_edges_kernel,
        in_specs=vmem(3 + len(rest)),
        out_specs=vmem(1)[0],
        out_shape=jax.ShapeDtypeStruct((modes, LANES), jnp.float32),
        scratch_shapes=gather_scratch(modes, elems),
        compiler_params=pltpu.CompilerParams(vmem_limit_bytes=16 * MIB),
        cost_estimate=edges_cost(modes, elems),
    )(first, second, field, *rest)


def finish_kernel(count, r0_ref, q0_ref, *refs):
    sum_refs, out_ref = refs[:count], refs[count]
    modes = out_ref.shape[0]
    total = sum_refs[0][...]
    for ref in sum_refs[1:]:
        total = total + ref[...]
    m0, m1, m2, m3 = [total[:, k : k + 1] for k in range(4)]
    alpha = m0 / m1
    norm = alpha * (alpha * m2) - 2.0 * (alpha * m1) + m0
    energy = m1 - 2.0 * (alpha * m2) + alpha * (alpha * m3)
    beta = norm / m0
    second = norm / (energy - beta * (norm / alpha))
    on_r = jnp.broadcast_to(alpha + second * (1.0 + beta), (modes, LANES))
    on_q = jnp.broadcast_to(second * alpha, (modes, LANES))
    for j in range(8):
        rows = slice(8 * j, 8 * j + 8)
        value = on_r * r0_ref[rows] - on_q * q0_ref[rows]
        out_ref[:, rows, :] = jnp.swapaxes(value, 0, 1)


def finish(r0, q0, sums):
    _, modes, elems = r0.shape
    field = pl.BlockSpec((64, modes, LANES), lambda b: (0, 0, b))
    small = pl.BlockSpec((modes, LANES), lambda b: (0, 0))
    return pl.pallas_call(
        functools.partial(finish_kernel, len(sums)),
        grid=(elems // LANES,),
        in_specs=[field, field] + [small] * len(sums),
        out_specs=pl.BlockSpec((modes, 64, LANES), lambda b: (0, 0, b)),
        out_shape=jax.ShapeDtypeStruct((modes, 64, elems), jnp.float32),
        compiler_params=pltpu.CompilerParams(vmem_limit_bytes=16 * MIB),
    )(r0, q0, *sums)


def shifted(value, axis, steps):
    size = lax.axis_size(axis)
    return lax.ppermute(value, axis, [(i, (i + steps) % size) for i in range(size)])


def exchanged(slots, first=0):
    size = lax.axis_size("gz")
    out = []
    for number, value in enumerate(slots):
        d = first + number
        out.append(lax.ppermute(value, "gz", [(i, i ^ d) for i in range(size)]) if d else value)
    return out


def both_sides(send):
    return [shifted(send, "xy", -1), shifted(send, "xy", 1)]


def pad_rows(values, rows=8):
    return jnp.pad(values, ((0, rows - values.shape[0]), (0, 0)))


def edge_tables(nbr_elem, nbr_edge):
    elems = nbr_elem.shape[1]
    me, size = lax.axis_index("xy"), lax.axis_size("xy")
    wall = nbr_elem < 0
    ids = jnp.maximum(nbr_elem, 0)
    owner, local_id = ids // elems, ids % elems
    here = (owner == me) & ~wall
    after = (owner == (me + 1) % size) & ~wall & ~here
    before = ~wall & ~here & ~after
    place = jnp.where(here, nbr_edge % 4 * elems + local_id, -1).reshape(-1)
    source = jnp.arange(4 * elems, dtype=jnp.int32)[:, None]
    local = (source == place[None, :]).astype(jnp.bfloat16)
    first = jnp.arange(LANES) < ROWS

    def ends(table):
        return jnp.where(first[None, :], table[:, :LANES], table[:, elems - LANES :])

    send = jnp.where(first[None, :], before[:, :LANES], after[:, elems - LANES :])
    slot = jnp.where(after, local_id, local_id - (elems - ROWS) + ROWS)
    slot = jnp.where(send, ends(slot), -1).reshape(-1)
    far = (jnp.arange(LANES, dtype=jnp.int32)[:, None] == slot[None, :]).astype(jnp.bfloat16)
    flags = jnp.stack([wall, nbr_edge >= 4], axis=1).astype(jnp.float32)
    flags = jnp.pad(flags, ((0, 0), (0, 6), (0, 0))).reshape(32, elems)
    return local, far, pad_rows(send.astype(jnp.float32)), flags


def per_device(concentration, geometry, nbr_elem, nbr_edge, wall_flags):
    planes, _, elems = concentration.shape
    groups = lax.axis_size("gz")
    me = lax.axis_index("gz")
    fold = Fold(elems // groups)
    scale_x, scale_y = geometry[0], geometry[1]
    geo = pad_rows(jnp.stack([1.0 / (scale_x * scale_y), scale_x * scale_x, scale_y * scale_y]))
    mine = lax.dynamic_slice_in_dim(geo, me * fold.width, fold.width, axis=1)
    mine = jnp.tile(mine, (1, fold.parts))
    index = me.astype(jnp.int32).reshape(1)
    near_sent = pack(index, concentration, fold, groups, 0)
    far_sent = pack(index, concentration, fold, groups, groups // 2)
    near_field = exchanged(near_sent)
    far_field = exchanged(far_sent, groups // 2)
    near = near_terms(index, mine, near_field, fold)
    parts = exchanged(right_hand_side(index, mine, near, far_field, fold))

    mode_ids = me * planes + jnp.arange(planes, dtype=jnp.int32)
    wave = ((mode_ids + 1) // 2).astype(jnp.float32)
    mass = jnp.broadcast_to(
        (1.0 / time_step + axial_stiffness * wave * wave)[:, None], (planes, LANES)
    )
    flag = jnp.broadcast_to(wall_flags.astype(jnp.float32)[:, None], (planes, LANES))
    local, far, mask, edges = edge_tables(nbr_elem, nbr_edge)
    r0, send = unpack(index, mask, parts, fold)
    image, sums = volume(r0, geo, mass, True)
    halo = both_sides(send)
    q0, send, sums = first_edges(image, sums, mask, r0, [flag, *halo, far, local, edges])
    (more,) = volume(q0, geo, mass, False)
    halo = both_sides(send)
    packed = second_edges(sums, more, q0, [flag, *halo, far, local, edges])
    size = lax.axis_size("xy")
    packs = [packed] + [shifted(packed, "xy", k) for k in range(1, size)]
    return finish(r0, q0, packs)


def solution(mesh):
    return jax.shard_map(
        per_device,
        mesh=mesh,
        in_specs=(P("gz", None, "xy"), P(None, "xy"), P(None, "xy"), P(None, "xy"), P("gz")),
        out_specs=P("gz", None, "xy"),
        check_vma=False,
    )
```

time: 805 us -> 250 us (0.31); the launches traced: 794 us -> 250 us
  local copies, waits for them, and re-layouts: 291 us -> 11.3 us
  other arithmetic: 155 us -> 7.66 us
  matrix products: 110 us -> 0 us
  Pallas kernels: 0 us -> 50.1 us
  waiting for transfers between devices: 195 us -> 155 us
  blocking collectives: 18.6 us -> 0 us
    all_to_all x3 -> x0, waiting for transfers between devices: 195 us -> none  [the longest x1 89.9 us: per_device(): lax.all_to_all(explicit_hat - axial_mobility * (wave_all * wave_all)[:, N...]
    ppermute x4 -> x21, waiting for transfers between devices: 0.01 us -> 155 us  [the longest x14 152 us: exchanged(): lax.ppermute(value, 'gz', [(i, i ^ d) for i in range(size)])]
    dot_general x14 -> x0, matrix products: 110 us -> none  [the longest x1 21.6 us: per_device(): jnp.einsum('kp,pne->kne', fourier, lax.all_to_all(explicit, 'gz', split_a...]
    scatter-add x6 -> x0, local copies, waits for them, and re-layouts: 64.9 us -> none  [the longest x2 22.7 us: add_edges(): grid = grid.at[:, :, 0, :].add(penalty[:, :, 3])]
    pallas_call x0 -> x10, Pallas kernels: none -> 50.1 us  [the longest x1 10.5 us: right_hand_side(): pl.pallas_call(functools.partial(far_kernel, fold, count), in_specs=[smem...]
    unnamed x55 -> x23, local copies, waits for them, and re-layouts: 58.4 us -> 11 us
    all_to_all x3 -> x0, other arithmetic: 41.6 us -> none  [the longest x1 14.1 us: per_device(): lax.all_to_all(explicit_hat - axial_mobility * (wave_all * wave_all)[:, N...]
    all_to_all x5 -> x0, local copies, waits for them, and re-layouts: 41.6 us -> none  [the longest x2 21.9 us: per_device(): lax.all_to_all(explicit_hat - axial_mobility * (wave_all * wave_all)[:, N...]
  transfers between devices with their start and end apart: 7 -> 21, of which waited for: 3 -> 13; matrix products, arithmetic and copies ran while one was open for 13% -> 3% of each run, Pallas kernels for 0% -> 7%
where the time goes in v2:
time: 250 us
  waiting for transfers between devices  155 us (62%)
  Pallas kernels  50.1 us (20%)
  starting transfers between devices  25.4 us (10%)
  local copies, waits for them, and re-layouts  11.3 us (5%)
  other arithmetic  7.66 us (3%)
    ppermute x14, waiting for transfers between devices, exchanged(): lax.ppermute(value, 'gz', [(i, i ^ d) for i in range(size)])  152 us
    ppermute x14, starting transfers between devices, exchanged(): lax.ppermute(value, 'gz', [(i, i ^ d) for i in range(size)])  20.1 us
    unnamed x23, local copies, waits for them, and re-layouts  11 us
    pallas_call x1, Pallas kernels, right_hand_side(): pl.pallas_call(functools.partial(far_kernel, fold, count), in_specs=[smem...  10.5 us
    pallas_call x2, Pallas kernels, volume(): pl.pallas_call(functools.partial(volume_kernel, want_image), in_specs=vme...  8.85 us
    pallas_call x2, Pallas kernels, pack(): pl.pallas_call(functools.partial(pack_kernel, fold), grid_spec=pltpu.Pref...  8.51 us
    convert_element_type x1, other arithmetic, edge_tables(): local = (source == place[None, :]).astype(jnp.bfloat16)  7.46 us
    pallas_call x1, Pallas kernels, first_edges(): pl.pallas_call(first_edges_kernel, in_specs=vmem(4 + len(rest)), out_spec...  5.72 us
  transfers between devices with their start and end apart: 21, of which 13 were waited for; matrix products, arithmetic and copies ran while one was open for 3% of the time, Pallas kernels for 7%

profile of v2, /device:TPU:8, one launch (start us, length us, event | category | flops | bytes accessed | tf_op | source)
XLA Modules:
  0.0 249.8 jit_solution(13362763232674024101)
XLA Ops:
  0.0 4.3 %shard_map.66 = (f32[32,32,128]{2,1,0:T(8,128)}, f32[32,32,128]{2,1,0:T(8,128)}, f32[32,32,128]{2,1,0:T(8,128)}, f32[32,32,128]{2,1,0:T(8,128)}) custom-call(s32[1]{0:T(128)} %bitcast.me_ref, f32[32,64,512]{2,1,0:T(8,128)} %c_ref.3), custom_call_target="tpu_custom_call" | custom-call | flops 1048576 | bytes 4194304 | tf_op jit(solution)/shard_map/pallas_call | solution.py:199
  4.3 2.6 %collective-permute-start.3 = (f32[32,32,128]{2,1,0:T(8,128)}, f32[32,32,128]{2,1,0:T(8,128)S(1)}, u32[]{:S(2)}, u32[]{:S(2)}) collective-permute-start(f32[32,32,128]{2,1,0:T(8,128)} %get-tuple-element.32), channel_id=1, source_target_pairs={{0,4},{1,5},{2,6},{3,7},{4,0},{5,1},{6,2},{7,3},{8,12},{9,13},{10,... | collective-permute-start | bytes 1572872 | tf_op jit(solution)/shard_map/ppermute | solution.py:682
  9.7 4.2 %shard_map.64 = (f32[32,32,128]{2,1,0:T(8,128)}, f32[32,32,128]{2,1,0:T(8,128)}, f32[32,32,128]{2,1,0:T(8,128)}, f32[32,32,128]{2,1,0:T(8,128)}) custom-call(s32[1]{0:T(128)} %bitcast.me_ref, f32[32,64,512]{2,1,0:T(8,128)} %c_ref.3), custom_call_target="tpu_custom_call" | custom-call | flops 1048576 | bytes 4194304 | tf_op jit(solution)/shard_map/pallas_call | solution.py:199
  17.0 7.5 %fusion.local_ref = bf16[2048,2048]{1,0:T(8,128)(2,1)} fusion(s32[2048]{0:T(1024)S(1)} %bitcast.15), kind=kLoop, calls=%fused_computation.1 | loop fusion | flops 8388608 | bytes 8396800 | tf_op jit(solution)/shard_map/convert_element_type | solution.py:705
  24.5 13.7 %collective-permute-done.refs_1_ = f32[32,32,128]{2,1,0:T(8,128)S(1)} collective-permute-done((f32[32,32,128]{2,1,0:T(8,128)}, f32[32,32,128]{2,1,0:T(8,128)S(1)}, u32[]{:S(2)}, u32[]{:S(2)}) %collective-permute-start) | collective-permute-done | bytes 524320 | tf_op jit(solution)/shard_map/ppermute | solution.py:682
  38.6 15.5 %collective-permute-done.1.refs_2_ = f32[32,32,128]{2,1,0:T(8,128)S(1)} collective-permute-done((f32[32,32,128]{2,1,0:T(8,128)}, f32[32,32,128]{2,1,0:T(8,128)S(1)}, u32[]{:S(2)}, u32[]{:S(2)}) %collective-permute-start.1) | collective-permute-done | bytes 524320 | tf_op jit(solution)/shard_map/ppermute | solution.py:682
  54.9 29.6 %collective-permute-done.2.refs_3_ = f32[32,32,128]{2,1,0:T(8,128)S(1)} collective-permute-done((f32[32,32,128]{2,1,0:T(8,128)}, f32[32,32,128]{2,1,0:T(8,128)S(1)}, u32[]{:S(2)}, u32[]{:S(2)}) %collective-permute-start.2) | collective-permute-done | bytes 524320 | tf_op jit(solution)/shard_map/ppermute | solution.py:682
  84.5 5.3 %shard_map.65.near_ref = bf16[16,512,256]{2,1,0:T(8,128)(2,1)S(1)} custom-call(s32[1]{0:T(128)} %bitcast.me_ref, f32[8,128]{1,0:T(8,128)S(1)} %tile.10.geo_ref, f32[32,32,128]{2,1,0:T(8,128)S(1)} %copy-done.5, f32[32,32,128]{2,1,0:T(8,128)S(1)} %collective-permute-done.refs_1_, f32[32,32,128]{2,1,0:T(8,128)S(1)} %collective-permute-done.1.refs_2_, ...), custom_call_target="tpu_custom_call" | custom-call | flops 41943040 | bytes 6291456 | tf_op jit(solution)/shard_map/pallas_call | solution.py:318
  89.9 7.9 %collective-permute-done.6.refs_3_ = f32[32,32,128]{2,1,0:T(8,128)} collective-permute-done((f32[32,32,128]{2,1,0:T(8,128)}, f32[32,32,128]{2,1,0:T(8,128)}, u32[]{:S(2)}, u32[]{:S(2)}) %collective-permute-start.6) | collective-permute-done | bytes 524320 | tf_op jit(solution)/shard_map/ppermute | solution.py:682
  97.8 10.5 %shard_map.67 = (f32[32,32,128]{2,1,0:T(8,128)S(1)}, f32[32,32,128]{2,1,0:T(8,128)S(1)}, f32[32,32,128]{2,1,0:T(8,128)S(1)}, f32[32,32,128]{2,1,0:T(8,128)S(1)},...) custom-call(s32[1]{0:T(128)} %bitcast.me_ref, ...), custom_call_target="tpu_custom_call" | custom-call | flops 3221225472 | bytes 4194304 | tf_op jit(solution)/shard_map/pallas_call | solution.py:348
  109.0 2.9 %collective-permute-start.9 = (f32[32,32,128]{2,1,0:T(8,128)S(1)}, f32[32,32,128]{2,1,0:T(8,128)S(1)}, u32[]{:S(2)}, u32[]{:S(2)}) collective-permute-start(f32[32,32,128]{2,1,0:T(8,128)S(1)} %get-tuple-element.39), channel_id=1, source_target_pairs={{0,3},{1,2},{2,1},{3,0},{4,7},{5,6},{6,5},{7,4},{8,11},{9,10},{10,... | collective-permute-start | bytes 1572872 | tf_op jit(solution)/shard_map/ppermute | solution.py:682
  115.0 7.3 %collective-permute-done.7.refs_1_ = f32[32,32,128]{2,1,0:T(8,128)S(1)} collective-permute-done((f32[32,32,128]{2,1,0:T(8,128)S(1)}, f32[32,32,128]{2,1,0:T(8,128)S(1)}, u32[]{:S(2)}, u32[]{:S(2)}) %collective-permute-start.7) | collective-permute-done | bytes 524320 | tf_op jit(solution)/shard_map/ppermute | solution.py:682
  124.8 17.6 %collective-permute-done.8.refs_2_ = f32[32,32,128]{2,1,0:T(8,128)S(1)} collective-permute-done((f32[32,32,128]{2,1,0:T(8,128)S(1)}, f32[32,32,128]{2,1,0:T(8,128)S(1)}, u32[]{:S(2)}, u32[]{:S(2)}) %collective-permute-start.8) | collective-permute-done | bytes 524320 | tf_op jit(solution)/shard_map/ppermute | solution.py:682
  144.0 8.7 %collective-permute-done.9.refs_3_ = f32[32,32,128]{2,1,0:T(8,128)S(1)} collective-permute-done((f32[32,32,128]{2,1,0:T(8,128)S(1)}, f32[32,32,128]{2,1,0:T(8,128)S(1)}, u32[]{:S(2)}, u32[]{:S(2)}) %collective-permute-start.9) | collective-permute-done | bytes 524320 | tf_op jit(solution)/shard_map/ppermute | solution.py:682
  152.7 29.8 %collective-permute-done.11.refs_5_ = f32[32,32,128]{2,1,0:T(8,128)S(1)} collective-permute-done((f32[32,32,128]{2,1,0:T(8,128)S(1)}, f32[32,32,128]{2,1,0:T(8,128)S(1)}, u32[]{:S(2)}, u32[]{:S(2)}) %collective-permute-start.11) | collective-permute-done | bytes 524320 | tf_op jit(solution)/shard_map/ppermute | solution.py:682
  182.5 12.2 %collective-permute-done.12.refs_6_ = f32[32,32,128]{2,1,0:T(8,128)S(1)} collective-permute-done((f32[32,32,128]{2,1,0:T(8,128)S(1)}, f32[32,32,128]{2,1,0:T(8,128)S(1)}, u32[]{:S(2)}, u32[]{:S(2)}) %collective-permute-start.12) | collective-permute-done | bytes 524320 | tf_op jit(solution)/shard_map/ppermute | solution.py:682
  194.8 9.7 %collective-permute-done.13.refs_7_ = f32[32,32,128]{2,1,0:T(8,128)S(1)} collective-permute-done((f32[32,32,128]{2,1,0:T(8,128)S(1)}, f32[32,32,128]{2,1,0:T(8,128)S(1)}, u32[]{:S(2)}, u32[]{:S(2)}) %collective-permute-start.13) | collective-permute-done | bytes 524320 | tf_op jit(solution)/shard_map/ppermute | solution.py:682
  212.0 4.3 %shard_map.69 = (f32[64,32,512]{2,1,0:T(8,128)S(1)}, f32[2,32,128]{2,1,0:T(8,128)S(1)}) custom-call(f32[64,32,512]{2,1,0:T(8,128)S(1)} %copy-done.3, f32[8,512]{1,0:T(8,128)S(1)} %select_maximum_fusion.geo_ref, f32[32,128]{1,0:T(8,128)S(1)} %broadcast_in_dim.27.mass_ref), custom_call_target="tpu_custom_call" | custom-call | flops 41943040 | bytes 8388608 | tf_op jit(solution)/shard_map/pallas_call | solution.py:476
  216.4 3.4 %copy-done = bf16[2048,2048]{1,0:T(8,128)(2,1)S(1)} copy-done((bf16[2048,2048]{1,0:T(8,128)(2,1)S(1)}, bf16[2048,2048]{1,0:T(8,128)(2,1)}, u32[]{:S(2)}) %copy-start) | copy-done | bytes 8388632
  219.8 5.7 %shard_map.70 = (f32[64,32,512]{2,1,0:T(8,128)S(1)}, f32[8,32,128]{2,1,0:T(8,128)S(1)}, f32[2,32,128]{2,1,0:T(8,128)S(1)}) custom-call(f32[64,32,512]{2,1,0:T(8,128)S(1)} %get-tuple-element.45.q_ref, f32[2,32,128]{2,1,0:T(8,128)S(1)} %get-tuple-element.46.sums_ref, f32[8,128]{1,0:T(8,128)S(1)} %pad_convert_fusion.1.mask_ref, ...), custom_call_target="tpu_custom_call", output_to_operand_aliasing={{0}: (0, {})} | custom-call | flops 2147483648 | bytes 8388608 | tf_op jit(solution)/shard_map/pallas_call | solution.py:609
  227.3 4.5 %shard_map.71.second_ref = f32[2,32,128]{2,1,0:T(8,128)S(1)} custom-call(f32[64,32,512]{2,1,0:T(8,128)S(1)} %get-tuple-element.48.field_ref.q0_ref, f32[8,512]{1,0:T(8,128)S(1)} %select_maximum_fusion.geo_ref, f32[32,128]{1,0:T(8,128)S(1)} %broadcast_in_dim.27.mass_ref), custom_call_target="tpu_custom_call" | custom-call | flops 41943040 | bytes 8388608 | tf_op jit(solution)/shard_map/pallas_call | solution.py:476
  231.9 3.4 %copy-done.1 = bf16[2048,2048]{1,0:T(8,128)(2,1)S(1)} copy-done((bf16[2048,2048]{1,0:T(8,128)(2,1)S(1)}, bf16[2048,2048]{1,0:T(8,128)(2,1)}, u32[]{:S(2)}) %copy-start.1) | copy-done | bytes 8388632
  235.3 5.1 %shard_map.72.refs_0_ = f32[32,128]{1,0:T(8,128)S(1)} custom-call(f32[2,32,128]{2,1,0:T(8,128)S(1)} %get-tuple-element.49.first_ref, f32[2,32,128]{2,1,0:T(8,128)S(1)} %shard_map.71.second_ref, f32[64,32,512]{2,1,0:T(8,128)S(1)} %get-tuple-element.48.field_ref.q0_ref, f32[32,128]{1,0:T(8,128)S(1)} %broadcast_in_dim.40.flag_ref, ...), custom_call_target="tpu_custom_call" | custom-call | flops 2147483648 | bytes 8388608 | tf_op jit(solution)/shard_map/pallas_call | solution.py:627
  245.1 4.6 %shard_map.73 = f32[32,64,512]{2,1,0:T(8,128)} custom-call(f32[64,32,512]{2,1,0:T(8,128)S(1)} %copy-done.4, f32[64,32,512]{2,1,0:T(8,128)S(1)} %get-tuple-element.48.field_ref.q0_ref, f32[32,128]{1,0:T(8,128)S(1)} %shard_map.72.refs_0_, f32[32,128]{1,0:T(8,128)S(1)} %collective-permute-done.18.refs_1_, f32[32,128]{1,0:T(8,128)S(1)} %collective-permute-done.19.refs_2_, ...), custom_call_target="tpu_custom_call" | custom-call | tf_op jit(solution)/shard_map/pallas_call | solution.py:662
  (73 shorter events, 29.2 us)
Async XLA Ops:
  4.3 85.6 %collective-permute-start.3 = (f32[32,32,128]{2,1,0:T(8,128)}, f32[32,32,128]{2,1,0:T(8,128)S(1)}, u32[]{:S(2)}, u32[]{:S(2)}) collective-permute-start(f32[32,32,128]{2,1,0:T(8,128)} %get-tuple-element.32), channel_id=1, source_target_pairs={{0,4},{1,5},{2,6},{3,7},{4,0},{5,1},{6,2},{7,3},{8,12},{9,13},{10,... | collective-permute-start | bytes 1572872 | tf_op jit(solution)/shard_map/ppermute | solution.py:682
  6.9 83.0 %collective-permute-start.4 = (f32[32,32,128]{2,1,0:T(8,128)}, f32[32,32,128]{2,1,0:T(8,128)S(1)}, u32[]{:S(2)}, u32[]{:S(2)}) collective-permute-start(f32[32,32,128]{2,1,0:T(8,128)} %get-tuple-element.33), channel_id=1, source_target_pairs={{0,5},{1,4},{2,7},{3,6},{4,1},{5,0},{6,3},{7,2},{8,13},{9,12},{10,... | collective-permute-start | bytes 1572872 | tf_op jit(solution)/shard_map/ppermute | solution.py:682
  8.1 81.7 %collective-permute-start.5 = (f32[32,32,128]{2,1,0:T(8,128)}, f32[32,32,128]{2,1,0:T(8,128)}, u32[]{:S(2)}, u32[]{:S(2)}) collective-permute-start(f32[32,32,128]{2,1,0:T(8,128)} %get-tuple-element.34), channel_id=1, source_target_pairs={{0,6},{1,7},{2,4},{3,5},{4,2},{5,3},{6,0},{7,1},{8,14},{9,15},{10,... | collective-permute-start | bytes 1572872 | tf_op jit(solution)/shard_map/ppermute | solution.py:682
  13.9 24.3 %collective-permute-start = (f32[32,32,128]{2,1,0:T(8,128)}, f32[32,32,128]{2,1,0:T(8,128)S(1)}, u32[]{:S(2)}, u32[]{:S(2)}) collective-permute-start(f32[32,32,128]{2,1,0:T(8,128)} %get-tuple-element.29), channel_id=1, source_target_pairs={{0,1},{1,0},{2,3},{3,2},{4,5},{5,4},{6,7},{7,6},{8,9},{9,8},{10,11... | collective-permute-start | bytes 1572872 | tf_op jit(solution)/shard_map/ppermute | solution.py:682
  14.5 39.6 %collective-permute-start.1 = (f32[32,32,128]{2,1,0:T(8,128)}, f32[32,32,128]{2,1,0:T(8,128)S(1)}, u32[]{:S(2)}, u32[]{:S(2)}) collective-permute-start(f32[32,32,128]{2,1,0:T(8,128)} %get-tuple-element.30), channel_id=1, source_target_pairs={{0,2},{1,3},{2,0},{3,1},{4,6},{5,7},{6,4},{7,5},{8,10},{9,11},{10,... | collective-permute-start | bytes 1572872 | tf_op jit(solution)/shard_map/ppermute | solution.py:682
  17.0 67.5 %copy-start.5 = (f32[32,32,128]{2,1,0:T(8,128)S(1)}, f32[32,32,128]{2,1,0:T(8,128)}, u32[]{:S(2)}) copy-start(f32[32,32,128]{2,1,0:T(8,128)} %get-tuple-element.28.refs_0_) | copy-start | bytes 1572868
  38.2 59.6 %collective-permute-start.6 = (f32[32,32,128]{2,1,0:T(8,128)}, f32[32,32,128]{2,1,0:T(8,128)}, u32[]{:S(2)}, u32[]{:S(2)}) collective-permute-start(f32[32,32,128]{2,1,0:T(8,128)} %get-tuple-element.35), channel_id=1, source_target_pairs={{0,7},{1,6},{2,5},{3,4},{4,3},{5,2},{6,1},{7,0},{8,15},{9,14},{10,... | collective-permute-start | bytes 1572872 | tf_op jit(solution)/shard_map/ppermute | solution.py:682
  54.1 30.4 %collective-permute-start.2 = (f32[32,32,128]{2,1,0:T(8,128)}, f32[32,32,128]{2,1,0:T(8,128)S(1)}, u32[]{:S(2)}, u32[]{:S(2)}) collective-permute-start(f32[32,32,128]{2,1,0:T(8,128)} %get-tuple-element.31), channel_id=1, source_target_pairs={{0,3},{1,2},{2,1},{3,0},{4,7},{5,6},{6,5},{7,4},{8,11},{9,10},{10,... | collective-permute-start | bytes 1572872 | tf_op jit(solution)/shard_map/ppermute | solution.py:682
  54.9 42.9 %copy-start.6 = (bf16[2,256,768]{2,1,0:T(8,128)(2,1)S(1)}, bf16[2,256,768]{2,1,0:T(8,128)(2,1)}, u32[]{:S(2)}) copy-start(bf16[2,256,768]{2,1,0:T(8,128)(2,1)} %constant.96.clone.table_ref) | copy-start | bytes 2359300
  108.3 101.4 %copy-start.10 = (s32[32]{0:T(128)S(1)}, s32[32]{0:T(128)}, u32[]{:S(2)}) copy-start(s32[32]{0:T(128)} %param.10) | copy-start | bytes 388
  108.3 14.0 %collective-permute-start.7 = (f32[32,32,128]{2,1,0:T(8,128)S(1)}, f32[32,32,128]{2,1,0:T(8,128)S(1)}, u32[]{:S(2)}, u32[]{:S(2)}) collective-permute-start(f32[32,32,128]{2,1,0:T(8,128)S(1)} %get-tuple-element.37), channel_id=1, source_target_pairs={{0,1},{1,0},{2,3},{3,2},{4,5},{5,4},{6,7},{7,6},{8,9},{9,8},{10,11... | collective-permute-start | bytes 1572872 | tf_op jit(solution)/shard_map/ppermute | solution.py:682
  109.0 33.4 %collective-permute-start.8 = (f32[32,32,128]{2,1,0:T(8,128)S(1)}, f32[32,32,128]{2,1,0:T(8,128)S(1)}, u32[]{:S(2)}, u32[]{:S(2)}) collective-permute-start(f32[32,32,128]{2,1,0:T(8,128)S(1)} %get-tuple-element.38), channel_id=1, source_target_pairs={{0,2},{1,3},{2,0},{3,1},{4,6},{5,7},{6,4},{7,5},{8,10},{9,11},{10,... | collective-permute-start | bytes 1572872 | tf_op jit(solution)/shard_map/ppermute | solution.py:682
  109.0 43.6 %collective-permute-start.9 = (f32[32,32,128]{2,1,0:T(8,128)S(1)}, f32[32,32,128]{2,1,0:T(8,128)S(1)}, u32[]{:S(2)}, u32[]{:S(2)}) collective-permute-start(f32[32,32,128]{2,1,0:T(8,128)S(1)} %get-tuple-element.39), channel_id=1, source_target_pairs={{0,3},{1,2},{2,1},{3,0},{4,7},{5,6},{6,5},{7,4},{8,11},{9,10},{10,... | collective-permute-start | bytes 1572872 | tf_op jit(solution)/shard_map/ppermute | solution.py:682
  111.9 40.8 %collective-permute-start.10 = (f32[32,32,128]{2,1,0:T(8,128)S(1)}, f32[32,32,128]{2,1,0:T(8,128)S(1)}, u32[]{:S(2)}, u32[]{:S(2)}) collective-permute-start(f32[32,32,128]{2,1,0:T(8,128)S(1)} %get-tuple-element.40), channel_id=1, source_target_pairs={{0,4},{1,5},{2,6},{3,7},{4,0},{5,1},{6,2},{7,3},{8,12},{9,13},{10,... | collective-permute-start | bytes 1572872 | tf_op jit(solution)/shard_map/ppermute | solution.py:682
  114.0 68.6 %collective-permute-start.11 = (f32[32,32,128]{2,1,0:T(8,128)S(1)}, f32[32,32,128]{2,1,0:T(8,128)S(1)}, u32[]{:S(2)}, u32[]{:S(2)}) collective-permute-start(f32[32,32,128]{2,1,0:T(8,128)S(1)} %get-tuple-element.41), channel_id=1, source_target_pairs={{0,5},{1,4},{2,7},{3,6},{4,1},{5,0},{6,3},{7,2},{8,13},{9,12},{10,... | collective-permute-start | bytes 1572872 | tf_op jit(solution)/shard_map/ppermute | solution.py:682
  122.3 72.5 %collective-permute-start.12 = (f32[32,32,128]{2,1,0:T(8,128)S(1)}, f32[32,32,128]{2,1,0:T(8,128)S(1)}, u32[]{:S(2)}, u32[]{:S(2)}) collective-permute-start(f32[32,32,128]{2,1,0:T(8,128)S(1)} %get-tuple-element.42), channel_id=1, source_target_pairs={{0,6},{1,7},{2,4},{3,5},{4,2},{5,3},{6,0},{7,1},{8,14},{9,15},{10,... | collective-permute-start | bytes 1572872 | tf_op jit(solution)/shard_map/ppermute | solution.py:682
  142.4 62.1 %collective-permute-start.13 = (f32[32,32,128]{2,1,0:T(8,128)S(1)}, f32[32,32,128]{2,1,0:T(8,128)S(1)}, u32[]{:S(2)}, u32[]{:S(2)}) collective-permute-start(f32[32,32,128]{2,1,0:T(8,128)S(1)} %get-tuple-element.43), channel_id=1, source_target_pairs={{0,7},{1,6},{2,5},{3,4},{4,3},{5,2},{6,1},{7,0},{8,15},{9,14},{10,... | collective-permute-start | bytes 1572872 | tf_op jit(solution)/shard_map/ppermute | solution.py:682
  207.9 8.4 %collective-permute-start.15 = (f32[8,32,128]{2,1,0:T(8,128)S(1)}, f32[8,32,128]{2,1,0:T(8,128)S(1)}, u32[]{:S(2)}, u32[]{:S(2)}) collective-permute-start(f32[8,32,128]{2,1,0:T(8,128)S(1)} %get-tuple-element.47), channel_id=1, source_target_pairs={{0,8},{8,16},{16,24},{24,0},{1,9},{9,17},{17,25},{25,1},{2,10},{10... | collective-permute-start | bytes 393224 | tf_op jit(solution)/shard_map/ppermute | solution.py:674
  207.9 8.4 %collective-permute-start.14 = (f32[8,32,128]{2,1,0:T(8,128)S(1)}, f32[8,32,128]{2,1,0:T(8,128)S(1)}, u32[]{:S(2)}, u32[]{:S(2)}) collective-permute-start(f32[8,32,128]{2,1,0:T(8,128)S(1)} %get-tuple-element.47), channel_id=1, source_target_pairs={{0,24},{8,0},{16,8},{24,16},{1,25},{9,1},{17,9},{25,17},{2,26},{10... | collective-permute-start | bytes 393224 | tf_op jit(solution)/shard_map/ppermute | solution.py:674
  225.6 6.3 %collective-permute-start.17 = (f32[8,32,128]{2,1,0:T(8,128)S(1)}, f32[8,32,128]{2,1,0:T(8,128)S(1)}, u32[]{:S(2)}, u32[]{:S(2)}) collective-permute-start(f32[8,32,128]{2,1,0:T(8,128)S(1)} %get-tuple-element.50), channel_id=1, source_target_pairs={{0,8},{8,16},{16,24},{24,0},{1,9},{9,17},{17,25},{25,1},{2,10},{10... | collective-permute-start | bytes 393224 | tf_op jit(solution)/shard_map/ppermute | solution.py:674
  225.6 6.3 %collective-permute-start.16 = (f32[8,32,128]{2,1,0:T(8,128)S(1)}, f32[8,32,128]{2,1,0:T(8,128)S(1)}, u32[]{:S(2)}, u32[]{:S(2)}) collective-permute-start(f32[8,32,128]{2,1,0:T(8,128)S(1)} %get-tuple-element.50), channel_id=1, source_target_pairs={{0,24},{8,0},{16,8},{24,16},{1,25},{9,1},{17,9},{25,17},{2,26},{10... | collective-permute-start | bytes 393224 | tf_op jit(solution)/shard_map/ppermute | solution.py:674
  240.4 1.9 collective-permute-start.20
  240.8 3.7 %collective-permute-start.19 = (f32[32,128]{1,0:T(8,128)S(1)}, f32[32,128]{1,0:T(8,128)S(1)}, u32[]{:S(2)}, u32[]{:S(2)}) collective-permute-start(f32[32,128]{1,0:T(8,128)S(1)} %shard_map.72.refs_0_), channel_id=1, source_target_pairs={{0,16},{8,24},{16,0},{24,8},{1,17},{9,25},{17,1},{25,9},{2,18},{10... | collective-permute-start | bytes 49160 | tf_op jit(solution)/shard_map/ppermute | solution.py:674
  242.0 3.2 %collective-permute-start.18 = (f32[32,128]{1,0:T(8,128)S(1)}, f32[32,128]{1,0:T(8,128)S(1)}, u32[]{:S(2)}, u32[]{:S(2)}) collective-permute-start(f32[32,128]{1,0:T(8,128)S(1)} %shard_map.72.refs_0_), channel_id=1, source_target_pairs={{0,8},{8,16},{16,24},{24,0},{1,9},{9,17},{17,25},{25,1},{2,10},{10... | collective-permute-start | bytes 49160 | tf_op jit(solution)/shard_map/ppermute | solution.py:674
  (8 other events, 56.8 us)

commit v3 on v2

--- a/solution.py
+++ b/solution.py
@@ -176,9 +176,10 @@
 
         @pl.when(pl.program_id(0) == step)
         def _():
+            by_node = jnp.swapaxes(c_ref[...], 0, 1)
             for jp in range(fold.count_j):
                 for ip in range(fold.count_i):
-                    loads = [c_ref[:, fold.node(jp, ip, q), :] for q in range(fold.parts)]
+                    loads = [by_node[fold.node(jp, ip, q)] for q in range(fold.parts)]
                     made = []
                     for r in range(fold.parts):
                         parts = [rolled(loads[q], (q - r) * fold.width) for q in range(fold.parts)]
@@ -727,20 +728,24 @@
     mine = lax.dynamic_slice_in_dim(geo, me * fold.width, fold.width, axis=1)
     mine = jnp.tile(mine, (1, fold.parts))
     index = me.astype(jnp.int32).reshape(1)
-    near_sent = pack(index, concentration, fold, groups, 0)
-    far_sent = pack(index, concentration, fold, groups, groups // 2)
-    near_field = exchanged(near_sent)
-    far_field = exchanged(far_sent, groups // 2)
-    near = near_terms(index, mine, near_field, fold)
-    parts = exchanged(right_hand_side(index, mine, near, far_field, fold))
-
     mode_ids = me * planes + jnp.arange(planes, dtype=jnp.int32)
     wave = ((mode_ids + 1) // 2).astype(jnp.float32)
     mass = jnp.broadcast_to(
         (1.0 / time_step + axial_stiffness * wave * wave)[:, None], (planes, LANES)
     )
     flag = jnp.broadcast_to(wall_flags.astype(jnp.float32)[:, None], (planes, LANES))
-    local, far, mask, edges = edge_tables(nbr_elem, nbr_edge)
+    tables = edge_tables(nbr_elem, nbr_edge)
+    near_sent = pack(index, concentration, fold, groups, 0)
+    far_sent = pack(index, concentration, fold, groups, groups // 2)
+    near_field = exchanged(near_sent)
+    far_field = exchanged(far_sent, groups // 2)
+    near_field, geo, mine, mass, flag, tables = lax.optimization_barrier(
+        (near_field, geo, mine, mass, flag, tables)
+    )
+    local, far, mask, edges = tables
+    near = near_terms(index, mine, near_field, fold)
+    parts = exchanged(right_hand_side(index, mine, near, far_field, fold))
+
     r0, send = unpack(index, mask, parts, fold)
     image, sums = volume(r0, geo, mass, True)
     halo = both_sides(send)

time: 250 us -> 236 us (0.944)
  local copies, waits for them, and re-layouts: 11.3 us -> 0.37 us
  Pallas kernels: 50.1 us -> 47 us
    unnamed x23 -> x17, local copies, waits for them, and re-layouts: 11 us -> 0.04 us
where the time goes in v3:
time: 236 us
  waiting for transfers between devices  155 us (66%)
  Pallas kernels  47 us (20%)
  starting transfers between devices  25.7 us (11%)
  other arithmetic  7.64 us (3%)
    ppermute x14, waiting for transfers between devices, exchanged(): lax.ppermute(value, 'gz', [(i, i ^ d) for i in range(size)])  152 us
    ppermute x14, starting transfers between devices, exchanged(): lax.ppermute(value, 'gz', [(i, i ^ d) for i in range(size)])  20.3 us
    pallas_call x1, Pallas kernels, right_hand_side(): pl.pallas_call(functools.partial(far_kernel, fold, count), in_specs=[smem...  9.3 us
    pallas_call x2, Pallas kernels, volume(): pl.pallas_call(functools.partial(volume_kernel, want_image), in_specs=vme...  8.84 us
    convert_element_type x1, other arithmetic, edge_tables(): local = (source == place[None, :]).astype(jnp.bfloat16)  7.45 us
    pallas_call x2, Pallas kernels, pack(): pl.pallas_call(functools.partial(pack_kernel, fold), grid_spec=pltpu.Pref...  6.89 us
    pallas_call x1, Pallas kernels, first_edges(): pl.pallas_call(first_edges_kernel, in_specs=vmem(4 + len(rest)), out_spec...  5.59 us
    ppermute x7, starting transfers between devices, shifted(): lax.ppermute(value, axis, [(i, (i + steps) % size) for i in range(size)])  5.33 us
  transfers between devices with their start and end apart: 21, of which 13 were waited for; matrix products, arithmetic and copies ran while one was open for 3% of the time, Pallas kernels for 7%

profile of v3, /device:TPU:8, one launch (start us, length us, event | category | flops | bytes accessed | tf_op | source)
XLA Modules:
  0.0 236.2 jit_solution(9369077693921424527)
XLA Ops:
  0.0 3.5 %shard_map.66 = (f32[32,32,128]{2,1,0:T(8,128)}, f32[32,32,128]{2,1,0:T(8,128)}, f32[32,32,128]{2,1,0:T(8,128)}, f32[32,32,128]{2,1,0:T(8,128)}) custom-call(s32[1]{0:T(128)} %bitcast.me_ref, f32[32,64,512]{2,1,0:T(8,128)} %c_ref.3), custom_call_target="tpu_custom_call" | custom-call | flops 1048576 | bytes 4194304 | tf_op jit(solution)/shard_map/pallas_call | solution.py:200
  3.5 2.6 %collective-permute-start.3 = (f32[32,32,128]{2,1,0:T(8,128)}, f32[32,32,128]{2,1,0:T(8,128)S(1)}, u32[]{:S(2)}, u32[]{:S(2)}) collective-permute-start(f32[32,32,128]{2,1,0:T(8,128)} %get-tuple-element.50), channel_id=1, source_target_pairs={{0,4},{1,5},{2,6},{3,7},{4,0},{5,1},{6,2},{7,3},{8,12},{9,13},{10,... | collective-permute-start | bytes 1572872 | tf_op jit(solution)/shard_map/ppermute | solution.py:683
  8.9 3.4 %shard_map.64 = (f32[32,32,128]{2,1,0:T(8,128)}, f32[32,32,128]{2,1,0:T(8,128)}, f32[32,32,128]{2,1,0:T(8,128)}, f32[32,32,128]{2,1,0:T(8,128)}) custom-call(s32[1]{0:T(128)} %bitcast.me_ref, f32[32,64,512]{2,1,0:T(8,128)} %c_ref.3), custom_call_target="tpu_custom_call" | custom-call | flops 1048576 | bytes 4194304 | tf_op jit(solution)/shard_map/pallas_call | solution.py:200
  12.9 2.5 %collective-permute-start.1 = (f32[32,32,128]{2,1,0:T(8,128)}, f32[32,32,128]{2,1,0:T(8,128)S(1)}, u32[]{:S(2)}, u32[]{:S(2)}) collective-permute-start(f32[32,32,128]{2,1,0:T(8,128)} %get-tuple-element.42), channel_id=1, source_target_pairs={{0,2},{1,3},{2,0},{3,1},{4,6},{5,7},{6,4},{7,5},{8,10},{9,11},{10,... | collective-permute-start | bytes 1572872 | tf_op jit(solution)/shard_map/ppermute | solution.py:683
  15.6 7.5 %fusion.local_ref = bf16[2048,2048]{1,0:T(8,128)(2,1)} fusion(s32[2048]{0:T(1024)S(1)} %bitcast.17), kind=kLoop, calls=%fused_computation.1 | loop fusion | flops 8388608 | bytes 8396800 | tf_op jit(solution)/shard_map/convert_element_type | solution.py:706
  23.3 13.3 %collective-permute-done.refs_1_ = f32[32,32,128]{2,1,0:T(8,128)S(1)} collective-permute-done((f32[32,32,128]{2,1,0:T(8,128)}, f32[32,32,128]{2,1,0:T(8,128)S(1)}, u32[]{:S(2)}, u32[]{:S(2)}) %collective-permute-start) | collective-permute-done | bytes 524320 | tf_op jit(solution)/shard_map/ppermute | solution.py:683
  37.0 16.3 %collective-permute-done.1.refs_2_ = f32[32,32,128]{2,1,0:T(8,128)S(1)} collective-permute-done((f32[32,32,128]{2,1,0:T(8,128)}, f32[32,32,128]{2,1,0:T(8,128)S(1)}, u32[]{:S(2)}, u32[]{:S(2)}) %collective-permute-start.1) | collective-permute-done | bytes 524320 | tf_op jit(solution)/shard_map/ppermute | solution.py:683
  54.0 29.7 %collective-permute-done.2.refs_3_ = f32[32,32,128]{2,1,0:T(8,128)S(1)} collective-permute-done((f32[32,32,128]{2,1,0:T(8,128)}, f32[32,32,128]{2,1,0:T(8,128)S(1)}, u32[]{:S(2)}, u32[]{:S(2)}) %collective-permute-start.2) | collective-permute-done | bytes 524320 | tf_op jit(solution)/shard_map/ppermute | solution.py:683
  83.9 5.3 %shard_map.65.near_ref = bf16[16,512,256]{2,1,0:T(8,128)(2,1)S(1)} custom-call(s32[1]{0:T(128)} %bitcast.me_ref, f32[8,128]{1,0:T(8,128)S(1)} %tile.10.geo_ref, f32[32,32,128]{2,1,0:T(8,128)S(1)} %copy-done, f32[32,32,128]{2,1,0:T(8,128)S(1)} %collective-permute-done.refs_1_, f32[32,32,128]{2,1,0:T(8,128)S(1)} %collective-permute-done.1.refs_2_, ...), custom_call_target="tpu_custom_call" | custom-call | flops 41943040 | bytes 6291456 | tf_op jit(solution)/shard_map/pallas_call | solution.py:319
  89.2 7.7 %collective-permute-done.6.refs_3_ = f32[32,32,128]{2,1,0:T(8,128)S(1)} collective-permute-done((f32[32,32,128]{2,1,0:T(8,128)}, f32[32,32,128]{2,1,0:T(8,128)S(1)}, u32[]{:S(2)}, u32[]{:S(2)}) %collective-permute-start.6) | collective-permute-done | bytes 524320 | tf_op jit(solution)/shard_map/ppermute | solution.py:683
  96.9 9.3 %shard_map.67 = (f32[32,32,128]{2,1,0:T(8,128)S(1)}, f32[32,32,128]{2,1,0:T(8,128)S(1)}, f32[32,32,128]{2,1,0:T(8,128)S(1)}, f32[32,32,128]{2,1,0:T(8,128)S(1)},...) custom-call(s32[1]{0:T(128)} %bitcast.me_ref, ...), custom_call_target="tpu_custom_call" | custom-call | flops 3221225472 | bytes 4194304 | tf_op jit(solution)/shard_map/pallas_call | solution.py:349
  107.0 2.7 %collective-permute-start.9 = (f32[32,32,128]{2,1,0:T(8,128)S(1)}, f32[32,32,128]{2,1,0:T(8,128)S(1)}, u32[]{:S(2)}, u32[]{:S(2)}) collective-permute-start(f32[32,32,128]{2,1,0:T(8,128)S(1)} %get-tuple-element.57), channel_id=1, source_target_pairs={{0,3},{1,2},{2,1},{3,0},{4,7},{5,6},{6,5},{7,4},{8,11},{9,10},{10,... | collective-permute-start | bytes 1572872 | tf_op jit(solution)/shard_map/ppermute | solution.py:683
  112.9 7.3 %collective-permute-done.7.refs_1_ = f32[32,32,128]{2,1,0:T(8,128)S(1)} collective-permute-done((f32[32,32,128]{2,1,0:T(8,128)S(1)}, f32[32,32,128]{2,1,0:T(8,128)S(1)}, u32[]{:S(2)}, u32[]{:S(2)}) %collective-permute-start.7) | collective-permute-done | bytes 524320 | tf_op jit(solution)/shard_map/ppermute | solution.py:683
  120.2 2.6 %collective-permute-start.12 = (f32[32,32,128]{2,1,0:T(8,128)S(1)}, f32[32,32,128]{2,1,0:T(8,128)S(1)}, u32[]{:S(2)}, u32[]{:S(2)}) collective-permute-start(f32[32,32,128]{2,1,0:T(8,128)S(1)} %get-tuple-element.60), channel_id=1, source_target_pairs={{0,6},{1,7},{2,4},{3,5},{4,2},{5,3},{6,0},{7,1},{8,14},{9,15},{10,... | collective-permute-start | bytes 1572872 | tf_op jit(solution)/shard_map/ppermute | solution.py:683
  122.8 17.7 %collective-permute-done.8.refs_2_ = f32[32,32,128]{2,1,0:T(8,128)S(1)} collective-permute-done((f32[32,32,128]{2,1,0:T(8,128)S(1)}, f32[32,32,128]{2,1,0:T(8,128)S(1)}, u32[]{:S(2)}, u32[]{:S(2)}) %collective-permute-start.8) | collective-permute-done | bytes 524320 | tf_op jit(solution)/shard_map/ppermute | solution.py:683
  142.1 8.6 %collective-permute-done.9.refs_3_ = f32[32,32,128]{2,1,0:T(8,128)S(1)} collective-permute-done((f32[32,32,128]{2,1,0:T(8,128)S(1)}, f32[32,32,128]{2,1,0:T(8,128)S(1)}, u32[]{:S(2)}, u32[]{:S(2)}) %collective-permute-start.9) | collective-permute-done | bytes 524320 | tf_op jit(solution)/shard_map/ppermute | solution.py:683
  150.8 29.6 %collective-permute-done.11.refs_5_ = f32[32,32,128]{2,1,0:T(8,128)S(1)} collective-permute-done((f32[32,32,128]{2,1,0:T(8,128)S(1)}, f32[32,32,128]{2,1,0:T(8,128)S(1)}, u32[]{:S(2)}, u32[]{:S(2)}) %collective-permute-start.11) | collective-permute-done | bytes 524320 | tf_op jit(solution)/shard_map/ppermute | solution.py:683
  180.3 12.3 %collective-permute-done.12.refs_6_ = f32[32,32,128]{2,1,0:T(8,128)S(1)} collective-permute-done((f32[32,32,128]{2,1,0:T(8,128)S(1)}, f32[32,32,128]{2,1,0:T(8,128)S(1)}, u32[]{:S(2)}, u32[]{:S(2)}) %collective-permute-start.12) | collective-permute-done | bytes 524320 | tf_op jit(solution)/shard_map/ppermute | solution.py:683
  192.6 9.7 %collective-permute-done.13.refs_7_ = f32[32,32,128]{2,1,0:T(8,128)S(1)} collective-permute-done((f32[32,32,128]{2,1,0:T(8,128)S(1)}, f32[32,32,128]{2,1,0:T(8,128)S(1)}, u32[]{:S(2)}, u32[]{:S(2)}) %collective-permute-start.13) | collective-permute-done | bytes 524320 | tf_op jit(solution)/shard_map/ppermute | solution.py:683
  205.5 4.3 %shard_map.69 = (f32[64,32,512]{2,1,0:T(8,128)S(1)}, f32[2,32,128]{2,1,0:T(8,128)S(1)}) custom-call(f32[64,32,512]{2,1,0:T(8,128)S(1)} %get-tuple-element.62.field_ref.r0_ref, f32[8,512]{1,0:T(8,128)S(1)} %select_maximum_fusion.geo_ref, f32[32,128]{1,0:T(8,128)S(1)} %broadcast_in_dim.25.mass_ref), custom_call_target="tpu_custom_call" | custom-call | flops 41943040 | bytes 8388608 | tf_op jit(solution)/shard_map/pallas_call | solution.py:477
  209.9 5.6 %shard_map.70 = (f32[64,32,512]{2,1,0:T(8,128)S(1)}, f32[8,32,128]{2,1,0:T(8,128)S(1)}, f32[2,32,128]{2,1,0:T(8,128)S(1)}) custom-call(f32[64,32,512]{2,1,0:T(8,128)S(1)} %get-tuple-element.65.q_ref, f32[2,32,128]{2,1,0:T(8,128)S(1)} %get-tuple-element.66.sums_ref, f32[8,128]{1,0:T(8,128)S(1)} %pad_convert_fusion.1.mask_ref, ...), custom_call_target="tpu_custom_call", output_to_operand_aliasing={{0}: (0, {})} | custom-call | flops 2147483648 | bytes 8388608 | tf_op jit(solution)/shard_map/pallas_call | solution.py:610
  217.3 4.5 %shard_map.71.second_ref = f32[2,32,128]{2,1,0:T(8,128)S(1)} custom-call(f32[64,32,512]{2,1,0:T(8,128)S(1)} %get-tuple-element.72.field_ref.q0_ref, f32[8,512]{1,0:T(8,128)S(1)} %select_maximum_fusion.geo_ref, f32[32,128]{1,0:T(8,128)S(1)} %broadcast_in_dim.25.mass_ref), custom_call_target="tpu_custom_call" | custom-call | flops 41943040 | bytes 8388608 | tf_op jit(solution)/shard_map/pallas_call | solution.py:477
  221.9 5.0 %shard_map.72.refs_0_ = f32[32,128]{1,0:T(8,128)S(1)} custom-call(f32[2,32,128]{2,1,0:T(8,128)S(1)} %get-tuple-element.73.first_ref, f32[2,32,128]{2,1,0:T(8,128)S(1)} %shard_map.71.second_ref, f32[64,32,512]{2,1,0:T(8,128)S(1)} %get-tuple-element.72.field_ref.q0_ref, f32[32,128]{1,0:T(8,128)S(1)} %broadcast_in_dim.27.flag_ref, ...), custom_call_target="tpu_custom_call" | custom-call | flops 2147483648 | bytes 8388608 | tf_op jit(solution)/shard_map/pallas_call | solution.py:628
  231.6 4.6 %shard_map.73 = f32[32,64,512]{2,1,0:T(8,128)} custom-call(f32[64,32,512]{2,1,0:T(8,128)S(1)} %get-tuple-element.62.field_ref.r0_ref, f32[64,32,512]{2,1,0:T(8,128)S(1)} %get-tuple-element.72.field_ref.q0_ref, f32[32,128]{1,0:T(8,128)S(1)} %shard_map.72.refs_0_, f32[32,128]{1,0:T(8,128)S(1)} %collective-permute-done.18.refs_1_, ...), custom_call_target="tpu_custom_call" | custom-call | tf_op jit(solution)/shard_map/pallas_call | solution.py:663
  (68 shorter events, 20.4 us)
Async XLA Ops:
  3.5 85.7 %collective-permute-start.3 = (f32[32,32,128]{2,1,0:T(8,128)}, f32[32,32,128]{2,1,0:T(8,128)S(1)}, u32[]{:S(2)}, u32[]{:S(2)}) collective-permute-start(f32[32,32,128]{2,1,0:T(8,128)} %get-tuple-element.50), channel_id=1, source_target_pairs={{0,4},{1,5},{2,6},{3,7},{4,0},{5,1},{6,2},{7,3},{8,12},{9,13},{10,... | collective-permute-start | bytes 1572872 | tf_op jit(solution)/shard_map/ppermute | solution.py:683
  6.1 83.1 %collective-permute-start.4 = (f32[32,32,128]{2,1,0:T(8,128)}, f32[32,32,128]{2,1,0:T(8,128)S(1)}, u32[]{:S(2)}, u32[]{:S(2)}) collective-permute-start(f32[32,32,128]{2,1,0:T(8,128)} %get-tuple-element.51), channel_id=1, source_target_pairs={{0,5},{1,4},{2,7},{3,6},{4,1},{5,0},{6,3},{7,2},{8,13},{9,12},{10,... | collective-permute-start | bytes 1572872 | tf_op jit(solution)/shard_map/ppermute | solution.py:683
  7.4 81.9 %collective-permute-start.5 = (f32[32,32,128]{2,1,0:T(8,128)}, f32[32,32,128]{2,1,0:T(8,128)S(1)}, u32[]{:S(2)}, u32[]{:S(2)}) collective-permute-start(f32[32,32,128]{2,1,0:T(8,128)} %get-tuple-element.52), channel_id=1, source_target_pairs={{0,6},{1,7},{2,4},{3,5},{4,2},{5,3},{6,0},{7,1},{8,14},{9,15},{10,... | collective-permute-start | bytes 1572872 | tf_op jit(solution)/shard_map/ppermute | solution.py:683
  12.3 24.3 %collective-permute-start = (f32[32,32,128]{2,1,0:T(8,128)}, f32[32,32,128]{2,1,0:T(8,128)S(1)}, u32[]{:S(2)}, u32[]{:S(2)}) collective-permute-start(f32[32,32,128]{2,1,0:T(8,128)} %get-tuple-element.41), channel_id=1, source_target_pairs={{0,1},{1,0},{2,3},{3,2},{4,5},{5,4},{6,7},{7,6},{8,9},{9,8},{10,11... | collective-permute-start | bytes 1572872 | tf_op jit(solution)/shard_map/ppermute | solution.py:683
  12.9 40.5 %collective-permute-start.1 = (f32[32,32,128]{2,1,0:T(8,128)}, f32[32,32,128]{2,1,0:T(8,128)S(1)}, u32[]{:S(2)}, u32[]{:S(2)}) collective-permute-start(f32[32,32,128]{2,1,0:T(8,128)} %get-tuple-element.42), channel_id=1, source_target_pairs={{0,2},{1,3},{2,0},{3,1},{4,6},{5,7},{6,4},{7,5},{8,10},{9,11},{10,... | collective-permute-start | bytes 1572872 | tf_op jit(solution)/shard_map/ppermute | solution.py:683
  23.2 73.7 %copy-start.1 = (bf16[2,256,768]{2,1,0:T(8,128)(2,1)S(1)}, bf16[2,256,768]{2,1,0:T(8,128)(2,1)}, u32[]{:S(2)}) copy-start(bf16[2,256,768]{2,1,0:T(8,128)(2,1)} %constant.96.clone.table_ref) | copy-start | bytes 2359300
  36.6 60.3 %collective-permute-start.6 = (f32[32,32,128]{2,1,0:T(8,128)}, f32[32,32,128]{2,1,0:T(8,128)S(1)}, u32[]{:S(2)}, u32[]{:S(2)}) collective-permute-start(f32[32,32,128]{2,1,0:T(8,128)} %get-tuple-element.53), channel_id=1, source_target_pairs={{0,7},{1,6},{2,5},{3,4},{4,3},{5,2},{6,1},{7,0},{8,15},{9,14},{10,... | collective-permute-start | bytes 1572872 | tf_op jit(solution)/shard_map/ppermute | solution.py:683
  53.4 30.4 %collective-permute-start.2 = (f32[32,32,128]{2,1,0:T(8,128)}, f32[32,32,128]{2,1,0:T(8,128)S(1)}, u32[]{:S(2)}, u32[]{:S(2)}) collective-permute-start(f32[32,32,128]{2,1,0:T(8,128)} %get-tuple-element.43), channel_id=1, source_target_pairs={{0,3},{1,2},{2,1},{3,0},{4,7},{5,6},{6,5},{7,4},{8,11},{9,10},{10,... | collective-permute-start | bytes 1572872 | tf_op jit(solution)/shard_map/ppermute | solution.py:683
  83.9 126.0 %slice-start = ((s8[8388608]{0:T(1024)(128)(4,1)}), s8[4194304]{0:T(1024)(128)(4,1)S(1)}, s32[]{:S(2)}) async-start(s8[8388608]{0:T(1024)(128)(4,1)} %bitcast.13), calls=%async_computation | async-start | bytes 8388608
  89.2 120.7 %slice-start.1 = ((s8[8388608]{0:T(1024)(128)(4,1)}), s8[4194304]{0:T(1024)(128)(4,1)S(1)}, s32[]{:S(2)}) async-start(s8[8388608]{0:T(1024)(128)(4,1)} %bitcast.13), calls=%async_computation.1 | async-start | bytes 8388608
  106.2 14.0 %collective-permute-start.7 = (f32[32,32,128]{2,1,0:T(8,128)S(1)}, f32[32,32,128]{2,1,0:T(8,128)S(1)}, u32[]{:S(2)}, u32[]{:S(2)}) collective-permute-start(f32[32,32,128]{2,1,0:T(8,128)S(1)} %get-tuple-element.55), channel_id=1, source_target_pairs={{0,1},{1,0},{2,3},{3,2},{4,5},{5,4},{6,7},{7,6},{8,9},{9,8},{10,11... | collective-permute-start | bytes 1572872 | tf_op jit(solution)/shard_map/ppermute | solution.py:683
  107.0 33.4 %collective-permute-start.8 = (f32[32,32,128]{2,1,0:T(8,128)S(1)}, f32[32,32,128]{2,1,0:T(8,128)S(1)}, u32[]{:S(2)}, u32[]{:S(2)}) collective-permute-start(f32[32,32,128]{2,1,0:T(8,128)S(1)} %get-tuple-element.56), channel_id=1, source_target_pairs={{0,2},{1,3},{2,0},{3,1},{4,6},{5,7},{6,4},{7,5},{8,10},{9,11},{10,... | collective-permute-start | bytes 1572872 | tf_op jit(solution)/shard_map/ppermute | solution.py:683
  107.0 43.7 %collective-permute-start.9 = (f32[32,32,128]{2,1,0:T(8,128)S(1)}, f32[32,32,128]{2,1,0:T(8,128)S(1)}, u32[]{:S(2)}, u32[]{:S(2)}) collective-permute-start(f32[32,32,128]{2,1,0:T(8,128)S(1)} %get-tuple-element.57), channel_id=1, source_target_pairs={{0,3},{1,2},{2,1},{3,0},{4,7},{5,6},{6,5},{7,4},{8,11},{9,10},{10,... | collective-permute-start | bytes 1572872 | tf_op jit(solution)/shard_map/ppermute | solution.py:683
  109.8 41.0 %collective-permute-start.10 = (f32[32,32,128]{2,1,0:T(8,128)S(1)}, f32[32,32,128]{2,1,0:T(8,128)S(1)}, u32[]{:S(2)}, u32[]{:S(2)}) collective-permute-start(f32[32,32,128]{2,1,0:T(8,128)S(1)} %get-tuple-element.58), channel_id=1, source_target_pairs={{0,4},{1,5},{2,6},{3,7},{4,0},{5,1},{6,2},{7,3},{8,12},{9,13},{10,... | collective-permute-start | bytes 1572872 | tf_op jit(solution)/shard_map/ppermute | solution.py:683
  111.8 68.6 %collective-permute-start.11 = (f32[32,32,128]{2,1,0:T(8,128)S(1)}, f32[32,32,128]{2,1,0:T(8,128)S(1)}, u32[]{:S(2)}, u32[]{:S(2)}) collective-permute-start(f32[32,32,128]{2,1,0:T(8,128)S(1)} %get-tuple-element.59), channel_id=1, source_target_pairs={{0,5},{1,4},{2,7},{3,6},{4,1},{5,0},{6,3},{7,2},{8,13},{9,12},{10,... | collective-permute-start | bytes 1572872 | tf_op jit(solution)/shard_map/ppermute | solution.py:683
  120.2 72.4 %collective-permute-start.12 = (f32[32,32,128]{2,1,0:T(8,128)S(1)}, f32[32,32,128]{2,1,0:T(8,128)S(1)}, u32[]{:S(2)}, u32[]{:S(2)}) collective-permute-start(f32[32,32,128]{2,1,0:T(8,128)S(1)} %get-tuple-element.60), channel_id=1, source_target_pairs={{0,6},{1,7},{2,4},{3,5},{4,2},{5,3},{6,0},{7,1},{8,14},{9,15},{10,... | collective-permute-start | bytes 1572872 | tf_op jit(solution)/shard_map/ppermute | solution.py:683
  140.5 61.8 %collective-permute-start.13 = (f32[32,32,128]{2,1,0:T(8,128)S(1)}, f32[32,32,128]{2,1,0:T(8,128)S(1)}, u32[]{:S(2)}, u32[]{:S(2)}) collective-permute-start(f32[32,32,128]{2,1,0:T(8,128)S(1)} %get-tuple-element.61), channel_id=1, source_target_pairs={{0,7},{1,6},{2,5},{3,4},{4,3},{5,2},{6,1},{7,0},{8,15},{9,14},{10,... | collective-permute-start | bytes 1572872 | tf_op jit(solution)/shard_map/ppermute | solution.py:683
  203.7 6.1 %collective-permute-start.15 = (f32[8,32,128]{2,1,0:T(8,128)S(1)}, f32[8,32,128]{2,1,0:T(8,128)S(1)}, u32[]{:S(2)}, u32[]{:S(2)}) collective-permute-start(f32[8,32,128]{2,1,0:T(8,128)S(1)} %get-tuple-element.68), channel_id=1, source_target_pairs={{0,8},{8,16},{16,24},{24,0},{1,9},{9,17},{17,25},{25,1},{2,10},{10... | collective-permute-start | bytes 393224 | tf_op jit(solution)/shard_map/ppermute | solution.py:675
  203.8 6.1 %collective-permute-start.14 = (f32[8,32,128]{2,1,0:T(8,128)S(1)}, f32[8,32,128]{2,1,0:T(8,128)S(1)}, u32[]{:S(2)}, u32[]{:S(2)}) collective-permute-start(f32[8,32,128]{2,1,0:T(8,128)S(1)} %get-tuple-element.68), channel_id=1, source_target_pairs={{0,24},{8,0},{16,8},{24,16},{1,25},{9,1},{17,9},{25,17},{2,26},{10... | collective-permute-start | bytes 393224 | tf_op jit(solution)/shard_map/ppermute | solution.py:675
  215.5 6.3 %collective-permute-start.17 = (f32[8,32,128]{2,1,0:T(8,128)S(1)}, f32[8,32,128]{2,1,0:T(8,128)S(1)}, u32[]{:S(2)}, u32[]{:S(2)}) collective-permute-start(f32[8,32,128]{2,1,0:T(8,128)S(1)} %get-tuple-element.74), channel_id=1, source_target_pairs={{0,8},{8,16},{16,24},{24,0},{1,9},{9,17},{17,25},{25,1},{2,10},{10... | collective-permute-start | bytes 393224 | tf_op jit(solution)/shard_map/ppermute | solution.py:675
  215.6 6.3 %collective-permute-start.16 = (f32[8,32,128]{2,1,0:T(8,128)S(1)}, f32[8,32,128]{2,1,0:T(8,128)S(1)}, u32[]{:S(2)}, u32[]{:S(2)}) collective-permute-start(f32[8,32,128]{2,1,0:T(8,128)S(1)} %get-tuple-element.74), channel_id=1, source_target_pairs={{0,24},{8,0},{16,8},{24,16},{1,25},{9,1},{17,9},{25,17},{2,26},{10... | collective-permute-start | bytes 393224 | tf_op jit(solution)/shard_map/ppermute | solution.py:675
  226.8 1.9 collective-permute-start.20
  227.3 3.7 %collective-permute-start.19 = (f32[32,128]{1,0:T(8,128)S(1)}, f32[32,128]{1,0:T(8,128)S(1)}, u32[]{:S(2)}, u32[]{:S(2)}) collective-permute-start(f32[32,128]{1,0:T(8,128)S(1)} %shard_map.72.refs_0_), channel_id=1, source_target_pairs={{0,16},{8,24},{16,0},{24,8},{1,17},{9,25},{17,1},{25,9},{2,18},{10... | collective-permute-start | bytes 49160 | tf_op jit(solution)/shard_map/ppermute | solution.py:675
  228.4 3.2 %collective-permute-start.18 = (f32[32,128]{1,0:T(8,128)S(1)}, f32[32,128]{1,0:T(8,128)S(1)}, u32[]{:S(2)}, u32[]{:S(2)}) collective-permute-start(f32[32,128]{1,0:T(8,128)S(1)} %shard_map.72.refs_0_), channel_id=1, source_target_pairs={{0,8},{8,16},{16,24},{24,0},{1,9},{9,17},{17,25},{25,1},{2,10},{10... | collective-permute-start | bytes 49160 | tf_op jit(solution)/shard_map/ppermute | solution.py:675
  (5 other events, 130.0 us)

commit v4 on v3

--- a/solution.py
+++ b/solution.py
@@ -277,31 +277,55 @@
     half_terms(fold, me_ref[0], 0, y_refs, geo_ref, x_ref, acc_ref)
 
 
-def far_kernel(fold, count, me_ref, geo_ref, table_ref, near_ref, *refs):
-    y_refs, out_refs = refs[:count], refs[count : 3 * count]
-    x_ref, acc_ref, result_ref = refs[3 * count :]
-    planes = y_refs[0].shape[1]
-    half = count * planes
+def far_kernel(fold, count, sizes, me_ref, geo_ref, table_ref, near_ref, *refs):
+    y_refs, refs = refs[:count], refs[count:]
+    chunks = len(sizes)
+    out_refs = [refs[k * chunks : (k + 1) * chunks] for k in range(count)]
+    x_ref, acc_ref, result_ref = refs[count * chunks :]
+    half_terms(fold, me_ref[0], count, y_refs, geo_ref, x_ref, acc_ref)
+    transform(fold, 1, me_ref, geo_ref, table_ref, (near_ref, x_ref), out_refs, result_ref)
+
+
+def near_modes_kernel(fold, me_ref, geo_ref, table_ref, near_ref, far_ref, *refs):
+    out_refs, result_ref = [[ref] for ref in refs[:-1]], refs[-1]
+    transform(fold, 0, me_ref, geo_ref, table_ref, (near_ref, far_ref), out_refs, result_ref)
+
+
+def transform(fold, other, me_ref, geo_ref, table_ref, terms, out_refs, result_ref):
+    count = len(out_refs)
+    half = result_ref.shape[0]
+    planes = half // count
     me = me_ref[0]
-    half_terms(fold, me, count, y_refs, geo_ref, x_ref, acc_ref)
     mine = me // count
     jac = jnp.broadcast_to(geo_ref[0:1, :], (planes, LANES))
+    rows = pl.ds(pl.multiple_of((mine ^ other) * half, 16), half)
 
     def product(which, data):
-        table = table_ref[which]
+        upper, lower = slice(0, 4 * half), slice(4 * half, 6 * half)
         return jnp.dot(
-            table[:, : 4 * half], data, preferred_element_type=jnp.float32
-        ) + jnp.dot(table[:, 4 * half :], data[: 2 * half], preferred_element_type=jnp.float32)
+            table_ref[which, rows, upper], data, preferred_element_type=jnp.float32
+        ) + jnp.dot(
+            table_ref[which, rows, lower], data[: 2 * half], preferred_element_type=jnp.float32
+        )
 
     for pair in range(fold.slots // 2):
-        result_ref[...] = product(mine, near_ref[pair]) + product(1 - mine, x_ref[pair])
-        for number, out_ref in enumerate(out_refs):
-            rows = pl.ds(pl.multiple_of((me ^ number) * planes, 16), planes)
-            for k in range(2):
-                slot = 2 * pair + k
-                jp, ip = slot // fold.count_i, slot % fold.count_i
-                scale = jac * np.float32(WEIGHTS[jp] * WEIGHTS[ip])
-                out_ref[slot] = result_ref[rows, k * LANES : (k + 1) * LANES] * scale
+        result_ref[...] = product(mine, terms[0][pair]) + product(1 - mine, terms[1][pair])
+        for k in range(2):
+            slot = 2 * pair + k
+            jp, ip = slot // fold.count_i, slot % fold.count_i
+            scale = jac * np.float32(WEIGHTS[jp] * WEIGHTS[ip])
+            for number, pieces in enumerate(out_refs):
+                start = (me ^ number) % count * planes
+                for out_ref in pieces:
+                    size = out_ref.shape[1]
+                    here = pl.ds(pl.multiple_of(start, 8), size)
+                    value = result_ref[here, k * LANES : (k + 1) * LANES]
+                    out_ref[slot] = value * scale[:size]
+                    start = start + size
+
+
+def small_cost():
+    return pl.CostEstimate(flops=1, bytes_accessed=1, transcendentals=0)
 
 
 def smem():
@@ -331,48 +355,67 @@
     )(me, geo, *fields)
 
 
-def right_hand_side(me, geo, near, fields, fold):
-    slots, planes, _ = fields[0].shape
-    count = len(fields)
-    total = 2 * count * planes
-    half = total // 2
-    size = count * fields[0].size
+def transform_tables(total):
     table = fourier_table(total).astype(np.float32).astype(np.float64)
     wave = ((np.arange(total) + 1) // 2).astype(np.float64)
     upper, lower = two_parts(table)
     upper_b, lower_b = two_parts(-axial_mobility * (wave * wave)[:, None] * table)
     kinds = [upper, upper_b, upper, upper_b, lower, lower_b]
-    tables = np.stack(
-        [np.concatenate([k[:, h * half : (h + 1) * half] for k in kinds], axis=1) for h in (0, 1)]
-    )
-    slot = jax.ShapeDtypeStruct((slots, planes, LANES), jnp.float32)
-    return pl.pallas_call(
-        functools.partial(far_kernel, fold, count),
+    halves = np.split(np.stack(kinds), 2, axis=2)
+    return jnp.asarray(np.stack([np.concatenate(list(half), axis=1) for half in halves]))
+
+
+def far_modes(me, geo, tables, near, fields, fold, sizes):
+    slots, planes, _ = fields[0].shape
+    count = len(fields)
+    size = count * fields[0].size
+    chunks = len(sizes)
+    pieces = [jax.ShapeDtypeStruct((slots, k, LANES), jnp.float32) for k in sizes]
+    *outs, far = pl.pallas_call(
+        functools.partial(far_kernel, fold, count, sizes),
         in_specs=[smem()] + vmem(3 + count),
-        out_specs=vmem(2 * count),
-        out_shape=[slot] * (2 * count),
+        out_specs=vmem(chunks * count + 1),
+        out_shape=pieces * count + [jax.ShapeDtypeStruct(near.shape, jnp.bfloat16)],
         scratch_shapes=[
-            pltpu.VMEM(near.shape, jnp.bfloat16),
             pltpu.VMEM((slots, 16, LANES), jnp.float32),
-            pltpu.VMEM((total, 2 * LANES), jnp.float32),
+            pltpu.VMEM((count * planes, 2 * LANES), jnp.float32),
         ],
         compiler_params=pltpu.CompilerParams(vmem_limit_bytes=24 * MIB),
         cost_estimate=pl.CostEstimate(
-            flops=12 * total * 2 * size, bytes_accessed=8 * size, transcendentals=0
+            flops=12 * count * planes * size, bytes_accessed=8 * size, transcendentals=0
         ),
-    )(me, geo, jnp.asarray(tables), near, *fields)
-
-
-def edge_send(mask_ref, edge, out_ref):
+    )(me, geo, tables, near, *fields)
+    return [outs[k::chunks] for k in range(chunks)], far
+
+
+def near_modes(me, geo, tables, near, far, fold, planes):
+    slots = fold.slots
+    count = near.shape[1] // (4 * planes)
+    size = count * slots * planes * LANES
+    slot = jax.ShapeDtypeStruct((slots, planes, LANES), jnp.float32)
+    return pl.pallas_call(
+        functools.partial(near_modes_kernel, fold),
+        in_specs=[smem()] + vmem(4),
+        out_specs=vmem(count),
+        out_shape=[slot] * count,
+        scratch_shapes=[pltpu.VMEM((count * planes, 2 * LANES), jnp.float32)],
+        compiler_params=pltpu.CompilerParams(vmem_limit_bytes=16 * MIB),
+        cost_estimate=pl.CostEstimate(
+            flops=12 * count * planes * size, bytes_accessed=8 * size, transcendentals=0
+        ),
+    )(me, geo, tables, near, far)
+
+
+def edge_send(mask_ref, edge, write):
     for t in range(8):
         total = None
         for a in range(4):
             term = edge(a, t) * mask_ref[a : a + 1, :]
             total = term if total is None else total + term
-        out_ref[t] = total
-
-
-def send_from(field_ref, mask_ref, out_ref):
+        write(t, total)
+
+
+def send_from(field_ref, mask_ref, out_ref, start):
     modes, elems = field_ref.shape[1:]
     lane = lane_of((modes, LANES))
 
@@ -381,16 +424,24 @@
         ends = field_ref[node, :, :LANES], field_ref[node, :, elems - LANES :]
         return jnp.where(lane < ROWS, ends[0], ends[1])
 
-    edge_send(mask_ref, edge, out_ref)
-
-
-def unpack_kernel(fold, groups, me_ref, mask_ref, *refs):
-    parts, (r0_ref, send_ref) = refs[:groups], refs[groups:]
+    def write(t, value):
+        out_ref[t, start : start + modes, :] = value
+
+    edge_send(mask_ref, edge, write)
+
+
+def unpack_kernel(fold, groups, start, me_ref, mask_ref, *refs):
+    parts, (r0_ref, send_ref) = refs[:groups], refs[-2:]
     modes = r0_ref.shape[1]
     me = me_ref[0]
 
     def tile(part, _):
         rows = pl.ds(pl.multiple_of(part * 8, 8), 8)
+        whole_rows = pl.ds(pl.multiple_of(part * 8 + start, 8), 8)
+
+        def load(ref, slot):
+            return ref[slot, rows if ref.shape[1] == modes else whole_rows, :]
+
         lane = lane_of((8, LANES))
         for k in range(groups // fold.parts):
             block = k ^ (me // fold.parts)
@@ -398,7 +449,7 @@
             mine = parts[k * fold.parts : (k + 1) * fold.parts]
             for jp in range(fold.count_j):
                 for ip in range(fold.count_i):
-                    loads = swapped(me, [ref[fold.slot(jp, ip), rows, :] for ref in mine])
+                    loads = swapped(me, [load(ref, fold.slot(jp, ip)) for ref in mine])
                     for q in range(fold.parts):
                         shifts = [
                             rolled(loads[r], (r - q) * fold.width) for r in range(fold.parts)
@@ -408,40 +459,39 @@
         return 0
 
     lax.fori_loop(0, modes // 8, tile, 0)
-    send_from(r0_ref, mask_ref, send_ref)
-
-
-def unpack(me, mask, parts, fold):
-    slots, modes, _ = parts[0].shape
+    if start:
+        send_ref[:, :start, :] = refs[groups][...]
+    send_from(r0_ref, mask_ref, send_ref, start)
+
+
+def unpack(me, mask, parts, fold, sends):
+    _, modes, _ = parts[-1].shape
     groups = len(parts)
     elems = groups * fold.width
-    size = groups * parts[0].size
+    start = sum(value.shape[1] for value in sends)
     return pl.pallas_call(
-        functools.partial(unpack_kernel, fold, groups),
-        in_specs=[smem()] + vmem(1 + groups),
+        functools.partial(unpack_kernel, fold, groups, start),
+        in_specs=[smem()] + vmem(1 + groups + len(sends)),
         out_specs=vmem(2),
         out_shape=[
             jax.ShapeDtypeStruct((64, modes, elems), jnp.float32),
-            jax.ShapeDtypeStruct((8, modes, LANES), jnp.float32),
+            jax.ShapeDtypeStruct((8, start + modes, LANES), jnp.float32),
         ],
         compiler_params=pltpu.CompilerParams(vmem_limit_bytes=4 * MIB),
-        cost_estimate=pl.CostEstimate(flops=8 * size, bytes_accessed=8 * size, transcendentals=0),
-    )(me, mask, *parts)
-
-
-def volume_kernel(want_image, field_ref, geo_ref, mass_ref, *refs):
-    if want_image:
-        image_ref, sums_ref, acc_ref = refs
-    else:
-        sums_ref, acc_ref = refs
+        cost_estimate=small_cost(),
+    )(me, mask, *parts, *sends)
+
+
+def volume(field_ref, geo_ref, mass_ref, first, image_ref, sums_ref, row_of_sums, acc_ref):
     modes, elems = field_ref.shape[1:]
-    sums_ref[...] = jnp.zeros_like(sums_ref)
     tiles = modes // 8
 
     def tile(number, _):
-        rows = pl.ds(pl.multiple_of(number % tiles * 8, 8), 8)
+        row = pl.multiple_of(number % tiles * 8, 8)
+        rows = pl.ds(row, 8)
+        sum_rows = pl.ds(row + row_of_sums, 8)
         lanes = pl.ds(pl.multiple_of(number // tiles * LANES, LANES), LANES)
-        jac = geo_ref[0:1, lanes] * mass_ref[rows, :]
+        jac = geo_ref[0:1, lanes] * mass_ref[pl.ds(row + first, 8), :]
         square_x = jnp.broadcast_to(geo_ref[0:1, lanes] * geo_ref[1:2, lanes], (8, LANES))
         square_y = jnp.broadcast_to(geo_ref[0:1, lanes] * geo_ref[2:3, lanes], (8, LANES))
         stiff = plane_stiffness * STIFF
@@ -459,186 +509,239 @@
             scale = square_y * np.float32(WEIGHTS[i])
             for j in range(8):
                 image = acc_ref[8 * j + i] + result[j] * scale
-                if want_image:
+                if image_ref is not None:
                     image_ref[8 * j + i, rows, lanes] = image
                 for k, term in enumerate((values[j] * values[j], values[j] * image)):
                     totals[k] = term if totals[k] is None else totals[k] + term
         for k in range(2):
-            sums_ref[k, rows, :] += totals[k]
+            sums_ref[k, sum_rows, :] += totals[k]
         return 0
 
     lax.fori_loop(0, tiles * (elems // LANES), tile, 0)
 
 
-def volume(field, geo, mass, want_image):
-    _, modes, elems = field.shape
-    sums = jax.ShapeDtypeStruct((2, modes, LANES), jnp.float32)
-    shapes = [jax.ShapeDtypeStruct(field.shape, jnp.float32), sums] if want_image else [sums]
-    return pl.pallas_call(
-        functools.partial(volume_kernel, want_image),
-        in_specs=vmem(3),
-        out_specs=vmem(len(shapes)),
-        out_shape=shapes,
-        scratch_shapes=[pltpu.VMEM((64, 8, LANES), jnp.float32)],
-        compiler_params=pltpu.CompilerParams(vmem_limit_bytes=4 * MIB),
-        cost_estimate=pl.CostEstimate(
-            flops=40 * field.size, bytes_accessed=8 * field.size, transcendentals=0
-        ),
-    )(field, geo, mass)
-
-
-def gather_edges(
-    field_ref, flag_ref, after_ref, before_ref, far_ref, local_ref, edges_ref, scratch, visit
-):
-    trace_ref, parts_ref, val_ref = scratch
-    modes, elems = field_ref.shape[1:]
-    rows = 8 * modes
-    lane = lane_of((modes, LANES))
+def fill_pairs(target_ref, first, modes, lanes, value_of, parts):
+    total = target_ref.shape[0] // (8 * parts)
+    for t in range(0, 8, 2):
+        pieces = split(jnp.concatenate([value_of(t), value_of(t + 1)], axis=0))
+        for part in range(parts):
+            row = (8 * part + t) * total
+            target_ref[pl.ds(row, 2 * total), lanes] = pieces[part]
+
+
+def gathered(trace_ref, table, parts):
+    value = jnp.dot(trace_ref[...], table, preferred_element_type=jnp.float32)
+    if parts == 2:
+        half = value.shape[0] // 2
+        value = value[:half] + value[half:]
+    return value.reshape(8, value.shape[0] // 8, value.shape[1])
+
+
+def local_edges(fields, first, flag_ref, local_ref, edges_ref, trace_ref, val_ref, parts, visit):
+    elems = val_ref.shape[2]
     for a in range(4):
-        for t in range(8):
-            upper, lower = split(field_ref[EDGE_NODES[a][t]])
-            where = pl.ds(a * elems, elems)
-            trace_ref[pl.ds(t * modes, modes), where] = upper
-            trace_ref[pl.ds((8 + t) * modes, modes), where] = lower
-    for t in range(8):
-        upper, lower = split(jnp.where(lane < ROWS, after_ref[t], before_ref[t]))
-        parts_ref[pl.ds(t * modes, modes), :] = upper
-        parts_ref[pl.ds((8 + t) * modes, modes), :] = lower
+
+        def value_of(t):
+            pieces = [field_ref[EDGE_NODES[a][t]] for field_ref in fields]
+            return pieces[0] if len(pieces) == 1 else jnp.concatenate(pieces, axis=0)
+
+        fill_pairs(trace_ref, 0, 0, pl.ds(a * elems, elems), value_of, parts)
     for edge in range(4):
-        mine = slice(edge * elems, (edge + 1) * elems)
-        value = jnp.dot(trace_ref[...], local_ref[:, mine], preferred_element_type=jnp.float32)
-        val_ref[...] = (value[:rows] + value[rows:]).reshape(8, modes, elems)
-        mine = slice(edge * LANES, (edge + 1) * LANES)
-        value = jnp.dot(parts_ref[...], far_ref[:, mine], preferred_element_type=jnp.float32)
-        far = (value[:rows] + value[rows:]).reshape(8, modes, LANES)
-        wide = lane_of(far.shape)
-        val_ref[:, :, :LANES] += jnp.where(wide < ROWS, far, 0.0)
-        val_ref[:, :, elems - LANES :] += jnp.where(wide < ROWS, 0.0, far)
+        val_ref[...] = gathered(
+            trace_ref, local_ref[:, edge * elems : (edge + 1) * elems], parts
+        )
         for block in range(elems // LANES):
             lanes = pl.ds(block * LANES, LANES)
             wall = edges_ref[8 * edge : 8 * edge + 1, lanes]
-            turned = edges_ref[8 * edge + 1 : 8 * edge + 2, lanes]
-            turned = jnp.broadcast_to(turned, (modes, LANES)) > 0.5
-            coef = 1.0 - wall * (1.0 - flag_ref[...])
-            for t in range(8):
-                node = EDGE_NODES[edge][t]
-                value = field_ref[node, :, lanes]
-                other = jnp.where(turned, val_ref[7 - t, :, lanes], val_ref[t, :, lanes])
-                weight = np.float32(edge_penalty * WEIGHTS[t])
-                visit(node, lanes, value, weight * (coef * value - other))
-
-
-def gather_scratch(modes, elems):
-    return [
-        pltpu.VMEM((16 * modes, 4 * elems), jnp.bfloat16),
-        pltpu.VMEM((16 * modes, LANES), jnp.bfloat16),
-        pltpu.VMEM((8, modes, elems), jnp.float32),
-    ]
-
-
-def first_edges_kernel(
-    q_ref,
-    sums_ref,
-    mask_ref,
-    r0_ref,
-    flag_ref,
-    after_ref,
-    before_ref,
-    far_ref,
-    local_ref,
-    edges_ref,
-    q0_ref,
-    send_ref,
-    out_ref,
-    *scratch,
-):
-    totals = [sums_ref[1]]
-    q0_ref[...] = q_ref[...]
-
-    def visit(node, lanes, value, term):
-        q0_ref[node, :, lanes] += term
-        totals[0] = totals[0] + value * term
-
-    gather_edges(
-        r0_ref, flag_ref, after_ref, before_ref, far_ref, local_ref, edges_ref, scratch, visit
+            flip = edges_ref[8 * edge + 1 : 8 * edge + 2, lanes]
+            start = 0
+            for chunk, field_ref in enumerate(fields):
+                modes = field_ref.shape[1]
+                rows = slice(start, start + modes)
+                start += modes
+                turned = jnp.broadcast_to(flip, (modes, LANES)) > 0.5
+                coef = 1.0 - wall * (1.0 - flag_ref[first + start - modes : first + start])
+                for t in range(8):
+                    node = EDGE_NODES[edge][t]
+                    value = field_ref[node, :, lanes]
+                    other = jnp.where(turned, val_ref[7 - t, rows, lanes], val_ref[t, rows, lanes])
+                    weight = np.float32(edge_penalty * WEIGHTS[t])
+                    visit(chunk, rows, node, lanes, value, weight * (coef * value - other))
+
+
+def far_edges(after_ref, before_ref, far_ref, edges_ref, trace_ref, elems, visit):
+    modes = after_ref.shape[1]
+    lane = lane_of((modes, LANES))
+
+    def value_of(t):
+        return jnp.where(lane < ROWS, after_ref[t], before_ref[t])
+
+    fill_pairs(trace_ref, 0, modes, pl.ds(0, LANES), value_of, 2)
+    for edge in range(4):
+        values = gathered(trace_ref, far_ref[:, edge * LANES : (edge + 1) * LANES], 2)
+        flips = edges_ref[8 * edge + 1 : 8 * edge + 2, :]
+        flip = jnp.where(lane < ROWS, flips[:, :LANES], flips[:, elems - LANES :])
+        for t in range(8):
+            other = jnp.where(flip > 0.5, values[7 - t], values[t])
+            visit(edge, t, other * np.float32(-edge_penalty * WEIGHTS[t]))
+
+
+def apply_kernel(want_image, count, first, *refs):
+    fields, refs = refs[:count], refs[count:]
+    geo_ref, mass_ref, flag_ref, local_ref, edges_ref = refs[:5]
+    refs = refs[5:]
+    image_ref = refs[0] if want_image else None
+    sums_ref, trace_ref, val_ref, acc_ref = refs[-4:]
+    sums_ref[...] = jnp.zeros_like(sums_ref)
+    start = 0
+    for field_ref in fields:
+        row = first + start
+        volume(field_ref, geo_ref, mass_ref, row, image_ref, sums_ref, start, acc_ref)
+        start += field_ref.shape[1]
+    totals = [None] * count
+
+    def visit(chunk, rows, node, lanes, value, term):
+        if want_image:
+            image_ref[node, :, lanes] += term
+        product = value * term
+        totals[chunk] = product if totals[chunk] is None else totals[chunk] + product
+
+    parts = 2 if want_image else 1
+    local_edges(
+        fields, first, flag_ref, local_ref, edges_ref, trace_ref, val_ref, parts, visit
     )
-    out_ref[0] = sums_ref[0]
+    start = 0
+    for chunk, field_ref in enumerate(fields):
+        rows = slice(start, start + field_ref.shape[1])
+        start = rows.stop
+        sums_ref[1, rows, :] += totals[chunk]
+
+
+def apply_local(fields, first, geo, mass, flag, local, edges, want_image):
+    elems = fields[0].shape[2]
+    modes = sum(field.shape[1] for field in fields)
+    sums = jax.ShapeDtypeStruct((2, modes, LANES), jnp.float32)
+    shapes = [jax.ShapeDtypeStruct(fields[0].shape, jnp.float32), sums] if want_image else [sums]
+    parts = 2 if want_image else 1
+    return pl.pallas_call(
+        functools.partial(apply_kernel, want_image, len(fields), first),
+        in_specs=vmem(5 + len(fields)),
+        out_specs=vmem(len(shapes)),
+        out_shape=shapes,
+        scratch_shapes=[
+            pltpu.VMEM((parts * 8 * modes, 4 * elems), jnp.bfloat16),
+            pltpu.VMEM((8, modes, elems), jnp.float32),
+            pltpu.VMEM((64, 8, LANES), jnp.float32),
+        ],
+        compiler_params=pltpu.CompilerParams(vmem_limit_bytes=16 * MIB),
+        cost_estimate=small_cost(),
+    )(*fields, geo, mass, flag, local, edges)
+
+
+def ends_of(node, field_refs, lane):
+    elems = field_refs[0].shape[2]
+    pieces = []
+    for ref in field_refs:
+        pieces.append((ref[node, :, :LANES], ref[node, :, elems - LANES :]))
+    first = [p[0] for p in pieces]
+    last = [p[1] for p in pieces]
+    if len(pieces) > 1:
+        first, last = [jnp.concatenate(first, axis=0)], [jnp.concatenate(last, axis=0)]
+    return jnp.where(lane < ROWS, first[0], last[0])
+
+
+def first_far_kernel(count, *refs):
+    images, fields, refs = refs[:count], refs[count : 2 * count], refs[2 * count :]
+    sum_refs, refs = refs[:count], refs[count:]
+    after_ref, before_ref, far_ref, edges_ref, mask_ref = refs[:5]
+    outs, (send_ref, out_ref, trace_ref) = refs[5 : 5 + count], refs[5 + count :]
+    modes = after_ref.shape[1]
+    elems = fields[0].shape[2]
+    lane = lane_of((modes, LANES))
+    sums = [[ref[k] for ref in sum_refs] for k in range(2)]
+    sums = [jnp.concatenate(pieces, axis=0) if count > 1 else pieces[0] for pieces in sums]
+    totals = [sums[1]]
+    done = set()
+
+    def visit(edge, t, term):
+        node = EDGE_NODES[edge][t]
+        totals[0] = totals[0] + ends_of(node, fields, lane) * term
+        start = 0
+        for image_ref, ref in zip(images, outs):
+            size = ref.shape[1]
+            part = term[start : start + size]
+            here = lane_of((size, LANES)) < ROWS
+            start += size
+            source = ref if node in done else image_ref
+            ref[node, :, :LANES] = source[node, :, :LANES] + jnp.where(here, part, 0.0)
+            ref[node, :, elems - LANES :] = source[node, :, elems - LANES :] + jnp.where(
+                here, 0.0, part
+            )
+        done.add(node)
+
+    far_edges(after_ref, before_ref, far_ref, edges_ref, trace_ref, elems, visit)
+    out_ref[0] = sums[0]
     out_ref[1] = totals[0]
-    send_from(q0_ref, mask_ref, send_ref)
-
-
-def second_edges_kernel(
-    first_ref,
-    second_ref,
-    q0_ref,
-    flag_ref,
-    after_ref,
-    before_ref,
-    far_ref,
-    local_ref,
-    edges_ref,
-    out_ref,
-    *scratch,
-):
-    totals = [second_ref[1]]
-
-    def visit(node, lanes, value, term):
-        totals[0] = totals[0] + value * term
-
-    gather_edges(
-        q0_ref, flag_ref, after_ref, before_ref, far_ref, local_ref, edges_ref, scratch, visit
-    )
-    modes = q0_ref.shape[1]
+    start = 0
+    for ref in outs:
+        send_from(ref, mask_ref, send_ref, start)
+        start += ref.shape[1]
+
+
+def first_far(images, fields, halo, far, edges, mask, sums):
+    count = len(fields)
+    modes = sum(value.shape[1] for value in sums)
+    return pl.pallas_call(
+        functools.partial(first_far_kernel, count),
+        in_specs=vmem(3 * count + 5),
+        out_specs=vmem(count + 2),
+        out_shape=[jax.ShapeDtypeStruct(image.shape, jnp.float32) for image in images]
+        + [
+            jax.ShapeDtypeStruct((8, modes, LANES), jnp.float32),
+            jax.ShapeDtypeStruct((2, modes, LANES), jnp.float32),
+        ],
+        scratch_shapes=[pltpu.VMEM((16 * modes, LANES), jnp.bfloat16)],
+        input_output_aliases={k: k for k in range(count)},
+        compiler_params=pltpu.CompilerParams(vmem_limit_bytes=8 * MIB),
+        cost_estimate=small_cost(),
+    )(*images, *fields, *sums, *halo, far, edges, mask)
+
+
+def second_far_kernel(count, *refs):
+    fields, refs = refs[:count], refs[count:]
+    after_ref, before_ref, far_ref, edges_ref, first_ref, more_ref, out_ref, trace_ref = refs
+    modes = after_ref.shape[1]
+    elems = fields[0].shape[2]
     lane = lane_of((modes, LANES))
-    sums = [first_ref[0], first_ref[1], second_ref[0], totals[0]]
+    totals = [more_ref[1]]
+
+    def visit(edge, t, term):
+        totals[0] = totals[0] + ends_of(EDGE_NODES[edge][t], fields, lane) * term
+
+    far_edges(after_ref, before_ref, far_ref, edges_ref, trace_ref, elems, visit)
+    sums = [first_ref[0], first_ref[1], more_ref[0], totals[0]]
     packed = jnp.zeros((modes, LANES), jnp.float32)
     for k, value in enumerate(sums):
         packed = jnp.where(lane == k, jnp.sum(value, axis=1, keepdims=True), packed)
     out_ref[...] = packed
 
 
-def edges_cost(modes, elems):
-    return pl.CostEstimate(
-        flops=256 * modes * elems * elems,
-        bytes_accessed=8 * elems * elems * 4,
-        transcendentals=0,
-    )
-
-
-def first_edges(image, sums, mask, field, rest):
-    _, modes, elems = field.shape
+def second_far(fields, halo, far, edges, first, more):
+    modes = first.shape[1]
     return pl.pallas_call(
-        first_edges_kernel,
-        in_specs=vmem(4 + len(rest)),
-        out_specs=vmem(3),
-        out_shape=[
-            jax.ShapeDtypeStruct(field.shape, jnp.float32),
-            jax.ShapeDtypeStruct((8, modes, LANES), jnp.float32),
-            jax.ShapeDtypeStruct((2, modes, LANES), jnp.float32),
-        ],
-        scratch_shapes=gather_scratch(modes, elems),
-        input_output_aliases={0: 0},
-        compiler_params=pltpu.CompilerParams(vmem_limit_bytes=16 * MIB),
-        cost_estimate=edges_cost(modes, elems),
-    )(image, sums, mask, field, *rest)
-
-
-def second_edges(first, second, field, rest):
-    _, modes, elems = field.shape
-    return pl.pallas_call(
-        second_edges_kernel,
-        in_specs=vmem(3 + len(rest)),
+        functools.partial(second_far_kernel, len(fields)),
+        in_specs=vmem(6 + len(fields)),
         out_specs=vmem(1)[0],
         out_shape=jax.ShapeDtypeStruct((modes, LANES), jnp.float32),
-        scratch_shapes=gather_scratch(modes, elems),
-        compiler_params=pltpu.CompilerParams(vmem_limit_bytes=16 * MIB),
-        cost_estimate=edges_cost(modes, elems),
-    )(first, second, field, *rest)
-
-
-def finish_kernel(count, r0_ref, q0_ref, *refs):
+        scratch_shapes=[pltpu.VMEM((16 * modes, LANES), jnp.bfloat16)],
+        compiler_params=pltpu.CompilerParams(vmem_limit_bytes=8 * MIB),
+        cost_estimate=small_cost(),
+    )(*fields, *halo, far, edges, first, more)
+
+
+def finish_kernel(count, chunks, *refs):
+    fields, refs = refs[: 2 * chunks], refs[2 * chunks :]
     sum_refs, out_ref = refs[:count], refs[count]
-    modes = out_ref.shape[0]
     total = sum_refs[0][...]
     for ref in sum_refs[1:]:
         total = total + ref[...]
@@ -648,26 +751,33 @@
     energy = m1 - 2.0 * (alpha * m2) + alpha * (alpha * m3)
     beta = norm / m0
     second = norm / (energy - beta * (norm / alpha))
-    on_r = jnp.broadcast_to(alpha + second * (1.0 + beta), (modes, LANES))
-    on_q = jnp.broadcast_to(second * alpha, (modes, LANES))
-    for j in range(8):
-        rows = slice(8 * j, 8 * j + 8)
-        value = on_r * r0_ref[rows] - on_q * q0_ref[rows]
-        out_ref[:, rows, :] = jnp.swapaxes(value, 0, 1)
-
-
-def finish(r0, q0, sums):
-    _, modes, elems = r0.shape
-    field = pl.BlockSpec((64, modes, LANES), lambda b: (0, 0, b))
-    small = pl.BlockSpec((modes, LANES), lambda b: (0, 0))
+    on_r = jnp.broadcast_to(alpha + second * (1.0 + beta), total.shape)
+    on_q = jnp.broadcast_to(second * alpha, total.shape)
+    start = 0
+    for chunk in range(chunks):
+        r0_ref, q0_ref = fields[2 * chunk : 2 * chunk + 2]
+        mine = slice(start, start + r0_ref.shape[1])
+        start = mine.stop
+        for j in range(8):
+            rows = slice(8 * j, 8 * j + 8)
+            value = on_r[mine] * r0_ref[rows] - on_q[mine] * q0_ref[rows]
+            out_ref[mine, rows, :] = jnp.swapaxes(value, 0, 1)
+
+
+def finish(fields, sums):
+    elems = fields[0].shape[2]
+    chunks = len(fields) // 2
+    total = sums[0].shape[0]
+    blocks = [pl.BlockSpec((64, field.shape[1], LANES), lambda b: (0, 0, b)) for field in fields]
+    small = pl.BlockSpec((total, LANES), lambda b: (0, 0))
     return pl.pallas_call(
-        functools.partial(finish_kernel, len(sums)),
+        functools.partial(finish_kernel, len(sums), chunks),
         grid=(elems // LANES,),
-        in_specs=[field, field] + [small] * len(sums),
-        out_specs=pl.BlockSpec((modes, 64, LANES), lambda b: (0, 0, b)),
-        out_shape=jax.ShapeDtypeStruct((modes, 64, elems), jnp.float32),
+        in_specs=blocks + [small] * len(sums),
+        out_specs=pl.BlockSpec((total, 64, LANES), lambda b: (0, 0, b)),
+        out_shape=jax.ShapeDtypeStruct((total, 64, elems), jnp.float32),
         compiler_params=pltpu.CompilerParams(vmem_limit_bytes=16 * MIB),
-    )(r0, q0, *sums)
+    )(*fields, *sums)
 
 
 def shifted(value, axis, steps):
@@ -744,18 +854,30 @@
     )
     local, far, mask, edges = tables
     near = near_terms(index, mine, near_field, fold)
-    parts = exchanged(right_hand_side(index, mine, near, far_field, fold))
-
-    r0, send = unpack(index, mask, parts, fold)
-    image, sums = volume(r0, geo, mass, True)
-    halo = both_sides(send)
-    q0, send, sums = first_edges(image, sums, mask, r0, [flag, *halo, far, local, edges])
-    (more,) = volume(q0, geo, mass, False)
-    halo = both_sides(send)
-    packed = second_edges(sums, more, q0, [flag, *halo, far, local, edges])
+    sizes = [planes - 8, 8] if planes > 16 else [planes]
+    tables = transform_tables(planes * groups)
+    sent, far_terms = far_modes(index, mine, tables, near, far_field, fold, sizes)
+    far_parts = [exchanged(piece, groups // 2) for piece in sent]
+    near_parts = exchanged(near_modes(index, mine, tables, near, far_terms, fold, planes))
+    fields, images, sums, sends = [], [], [], []
+    start = 0
+    for piece, size in enumerate(sizes):
+        parts = near_parts + far_parts[piece]
+        field, send = unpack(index, mask, parts, fold, sends)
+        sends = [send]
+        image, more = apply_local([field], start, geo, mass, flag, local, edges, True)
+        start += size
+        mask, more = lax.optimization_barrier((mask, more))
+        fields.append(field)
+        images.append(image)
+        sums.append(more)
+    halo = both_sides(sends[0])
+    *images, send, sums = first_far(images, fields, halo, far, edges, mask, sums)
+    (more,) = apply_local(images, 0, geo, mass, flag, local, edges, False)
+    packed = second_far(images, both_sides(send), far, edges, sums, more)
     size = lax.axis_size("xy")
-    packs = [packed] + [shifted(packed, "xy", k) for k in range(1, size)]
-    return finish(r0, q0, packs)
+    pairs = [value for pair in zip(fields, images) for value in pair]
+    return finish(pairs, [packed] + [shifted(packed, "xy", k) for k in range(1, size)])
 
 
 def solution(mesh):

time: 236 us -> 222 us (0.941)
  waiting for transfers between devices: 155 us -> 141 us
    ppermute x14 -> x18, waiting for transfers between devices: 152 us -> 137 us  [exchanged(): lax.ppermute(value, 'gz', [(i, i ^ d) for i in range(size)])]
    pallas_call x7 -> x10, Pallas kernels: 34.8 us -> 32.8 us  [the longest x3 16.3 us: apply_local(): pl.pallas_call(functools.partial(apply_kernel, want_image, len(fields), f...]
    ppermute x14 -> x18, starting transfers between devices: 20.3 us -> 21.6 us  [exchanged(): lax.ppermute(value, 'gz', [(i, i ^ d) for i in range(size)])]
  transfers between devices with their start and end apart: 21 -> 25, of which waited for: 13 -> 16; matrix products, arithmetic and copies ran while one was open for 3% -> 4% of each run, Pallas kernels for 7% -> 13%
where the time goes in v4:
time: 222 us
  waiting for transfers between devices  141 us (64%)
  Pallas kernels  46 us (21%)
  starting transfers between devices  27.1 us (12%)
  other arithmetic  7.65 us (3%)
    ppermute x18, waiting for transfers between devices, exchanged(): lax.ppermute(value, 'gz', [(i, i ^ d) for i in range(size)])  137 us
    ppermute x18, starting transfers between devices, exchanged(): lax.ppermute(value, 'gz', [(i, i ^ d) for i in range(size)])  21.6 us
    pallas_call x3, Pallas kernels, apply_local(): pl.pallas_call(functools.partial(apply_kernel, want_image, len(fields), f...  16.3 us
    pallas_call x1, Pallas kernels, far_modes(): pl.pallas_call(functools.partial(far_kernel, fold, count, sizes), in_spec...  7.48 us
    convert_element_type x1, other arithmetic, edge_tables(): local = (source == place[None, :]).astype(jnp.bfloat16)  7.46 us
    pallas_call x2, Pallas kernels, pack(): pl.pallas_call(functools.partial(pack_kernel, fold), grid_spec=pltpu.Pref...  6.86 us
    pallas_call x1, Pallas kernels, near_terms(): pl.pallas_call(functools.partial(near_kernel, fold, count), in_specs=[sme...  6.38 us
    ppermute x7, starting transfers between devices, shifted(): lax.ppermute(value, axis, [(i, (i + steps) % size) for i in range(size)])  5.53 us
  transfers between devices with their start and end apart: 25, of which 16 were waited for; matrix products, arithmetic and copies ran while one was open for 4% of the time, Pallas kernels for 13%

profile of v4, /device:TPU:8, one launch (start us, length us, event | category | flops | bytes accessed | tf_op | source)
XLA Modules:
  0.0 222.3 jit_solution(16659236619249797082)
XLA Ops:
  0.0 3.5 %shard_map.66 = (f32[32,32,128]{2,1,0:T(8,128)}, f32[32,32,128]{2,1,0:T(8,128)}, f32[32,32,128]{2,1,0:T(8,128)}, f32[32,32,128]{2,1,0:T(8,128)}) custom-call(s32[1]{0:T(128)} %bitcast.me_ref, f32[32,64,512]{2,1,0:T(8,128)} %c_ref.3), custom_call_target="tpu_custom_call" | custom-call | flops 1048576 | bytes 4194304 | tf_op jit(solution)/shard_map/pallas_call | solution.py:200
  3.5 2.6 %collective-permute-start.3 = (f32[32,32,128]{2,1,0:T(8,128)}, f32[32,32,128]{2,1,0:T(8,128)S(1)}, u32[]{:S(2)}, u32[]{:S(2)}) collective-permute-start(f32[32,32,128]{2,1,0:T(8,128)} %get-tuple-element.64), channel_id=1, source_target_pairs={{0,4},{1,5},{2,6},{3,7},{4,0},{5,1},{6,2},{7,3},{8,12},{9,13},{10,... | collective-permute-start | bytes 1572872 | tf_op jit(solution)/shard_map/ppermute | solution.py:793
  8.9 3.4 %shard_map.64 = (f32[32,32,128]{2,1,0:T(8,128)}, f32[32,32,128]{2,1,0:T(8,128)}, f32[32,32,128]{2,1,0:T(8,128)}, f32[32,32,128]{2,1,0:T(8,128)}) custom-call(s32[1]{0:T(128)} %bitcast.me_ref, f32[32,64,512]{2,1,0:T(8,128)} %c_ref.3), custom_call_target="tpu_custom_call" | custom-call | flops 1048576 | bytes 4194304 | tf_op jit(solution)/shard_map/pallas_call | solution.py:200
  12.8 2.5 %collective-permute-start.1 = (f32[32,32,128]{2,1,0:T(8,128)}, f32[32,32,128]{2,1,0:T(8,128)}, u32[]{:S(2)}, u32[]{:S(2)}) collective-permute-start(f32[32,32,128]{2,1,0:T(8,128)} %get-tuple-element.56), channel_id=1, source_target_pairs={{0,2},{1,3},{2,0},{3,1},{4,6},{5,7},{6,4},{7,5},{8,10},{9,11},{10,... | collective-permute-start | bytes 1572872 | tf_op jit(solution)/shard_map/ppermute | solution.py:793
  15.5 7.5 %fusion.refs_4_.refs_5_ = bf16[2048,2048]{1,0:T(8,128)(2,1)} fusion(s32[2048]{0:T(1024)S(1)} %bitcast.20), kind=kLoop, calls=%fused_computation.1 | loop fusion | flops 8388608 | bytes 8396800 | tf_op jit(solution)/shard_map/convert_element_type | solution.py:816
  23.3 13.3 %collective-permute-done.refs_1_ = f32[32,32,128]{2,1,0:T(8,128)S(1)} collective-permute-done((f32[32,32,128]{2,1,0:T(8,128)}, f32[32,32,128]{2,1,0:T(8,128)S(1)}, u32[]{:S(2)}, u32[]{:S(2)}) %collective-permute-start) | collective-permute-done | bytes 524320 | tf_op jit(solution)/shard_map/ppermute | solution.py:793
  37.0 16.4 %collective-permute-done.1.refs_2_ = f32[32,32,128]{2,1,0:T(8,128)} collective-permute-done((f32[32,32,128]{2,1,0:T(8,128)}, f32[32,32,128]{2,1,0:T(8,128)}, u32[]{:S(2)}, u32[]{:S(2)}) %collective-permute-start.1) | collective-permute-done | bytes 524320 | tf_op jit(solution)/shard_map/ppermute | solution.py:793
  54.0 29.7 %collective-permute-done.2.refs_3_ = f32[32,32,128]{2,1,0:T(8,128)S(1)} collective-permute-done((f32[32,32,128]{2,1,0:T(8,128)}, f32[32,32,128]{2,1,0:T(8,128)S(1)}, u32[]{:S(2)}, u32[]{:S(2)}) %collective-permute-start.2) | collective-permute-done | bytes 524320 | tf_op jit(solution)/shard_map/ppermute | solution.py:793
  83.8 6.4 %shard_map.65.near_ref = bf16[16,512,256]{2,1,0:T(8,128)(2,1)S(1)} custom-call(s32[1]{0:T(128)} %bitcast.me_ref, f32[8,128]{1,0:T(8,128)S(1)} %tile.10.geo_ref, f32[32,32,128]{2,1,0:T(8,128)S(1)} %copy-done.1, f32[32,32,128]{2,1,0:T(8,128)S(1)} %collective-permute-done.refs_1_, f32[32,32,128]{2,1,0:T(8,128)} %collective-permute-done.1.refs_2_, ...), custom_call_target="tpu_custom_call" | custom-call | flops 41943040 | bytes 6291456 | tf_op jit(solution)/shard_map/pallas_call | solution.py:343
  90.3 6.6 %collective-permute-done.6.refs_3_ = f32[32,32,128]{2,1,0:T(8,128)S(1)} collective-permute-done((f32[32,32,128]{2,1,0:T(8,128)}, f32[32,32,128]{2,1,0:T(8,128)S(1)}, u32[]{:S(2)}, u32[]{:S(2)}) %collective-permute-start.6) | collective-permute-done | bytes 524320 | tf_op jit(solution)/shard_map/ppermute | solution.py:793
  96.9 7.5 %shard_map.67 = (f32[32,24,128]{2,1,0:T(8,128)S(1)}, f32[32,8,128]{2,1,0:T(8,128)S(1)}, f32[32,24,128]{2,1,0:T(8,128)S(1)}, f32[32,8,128]{2,1,0:T(8,128)S(1)}, f...) custom-call(s32[1]{0:T(128)} %bitcast.me_ref, ...), custom_call_target="tpu_custom_call" | custom-call | flops 805306368 | bytes 4194304 | tf_op jit(solution)/shard_map/pallas_call | solution.py:374
  104.4 3.1 %collective-permute-start.11 = (f32[32,24,128]{2,1,0:T(8,128)S(1)}, f32[32,24,128]{2,1,0:T(8,128)S(1)}, u32[]{:S(2)}, u32[]{:S(2)}) collective-permute-start(f32[32,24,128]{2,1,0:T(8,128)S(1)} %get-tuple-element.74), channel_id=1, source_target_pairs={{0,5},{1,4},{2,7},{3,6},{4,1},{5,0},{6,3},{7,2},{8,13},{9,12},{10,... | collective-permute-start | bytes 1179656 | tf_op jit(solution)/shard_map/ppermute | solution.py:793
  113.1 17.8 %collective-permute-done.10.refs_4_ = f32[32,24,128]{2,1,0:T(8,128)S(1)} collective-permute-done((f32[32,24,128]{2,1,0:T(8,128)S(1)}, f32[32,24,128]{2,1,0:T(8,128)S(1)}, u32[]{:S(2)}, u32[]{:S(2)}) %collective-permute-start.10) | collective-permute-done | bytes 393248 | tf_op jit(solution)/shard_map/ppermute | solution.py:793
  132.2 7.2 %collective-permute-done.11.refs_5_ = f32[32,24,128]{2,1,0:T(8,128)S(1)} collective-permute-done((f32[32,24,128]{2,1,0:T(8,128)S(1)}, f32[32,24,128]{2,1,0:T(8,128)S(1)}, u32[]{:S(2)}, u32[]{:S(2)}) %collective-permute-start.11) | collective-permute-done | bytes 393248 | tf_op jit(solution)/shard_map/ppermute | solution.py:793
  139.3 2.2 collective-permute-start.13
  141.5 24.8 %collective-permute-done.12.refs_6_ = f32[32,24,128]{2,1,0:T(8,128)S(1)} collective-permute-done((f32[32,24,128]{2,1,0:T(8,128)S(1)}, f32[32,24,128]{2,1,0:T(8,128)S(1)}, u32[]{:S(2)}, u32[]{:S(2)}) %collective-permute-start.12) | collective-permute-done | bytes 393248 | tf_op jit(solution)/shard_map/ppermute | solution.py:793
  166.3 12.1 %collective-permute-done.13.refs_7_ = f32[32,24,128]{2,1,0:T(8,128)S(1)} collective-permute-done((f32[32,24,128]{2,1,0:T(8,128)S(1)}, f32[32,24,128]{2,1,0:T(8,128)S(1)}, u32[]{:S(2)}, u32[]{:S(2)}) %collective-permute-start.13) | collective-permute-done | bytes 393248 | tf_op jit(solution)/shard_map/ppermute | solution.py:793
  181.6 7.0 %shard_map.70 = (f32[64,24,512]{2,1,0:T(8,128)S(1)}, f32[2,24,128]{2,1,0:T(8,128)S(1)}) custom-call(f32[64,24,512]{2,1,0:T(8,128)S(1)} %get-tuple-element.77.refs_0_.refs_2_, f32[8,512]{1,0:T(8,128)S(1)} %select_maximum_fusion.refs_1_.refs_2_, f32[32,128]{1,0:T(8,128)S(1)} %broadcast_in_dim.25.refs_2_.refs_3_, ...), custom_call_target="tpu_custom_call" | custom-call | flops 1 | bytes 1 | tf_op jit(solution)/shard_map/pallas_call | solution.py:626
  189.8 4.6 %collective-permute-done.16.refs_6_ = f32[32,8,128]{2,1,0:T(8,128)S(1)} collective-permute-done((f32[32,8,128]{2,1,0:T(8,128)S(1)}, f32[32,8,128]{2,1,0:T(8,128)S(1)}, u32[]{:S(2)}, u32[]{:S(2)}) %collective-permute-start.16) | collective-permute-done | bytes 131104 | tf_op jit(solution)/shard_map/ppermute | solution.py:793
  194.4 3.4 %collective-permute-done.17.refs_7_ = f32[32,8,128]{2,1,0:T(8,128)S(1)} collective-permute-done((f32[32,8,128]{2,1,0:T(8,128)S(1)}, f32[32,8,128]{2,1,0:T(8,128)S(1)}, u32[]{:S(2)}, u32[]{:S(2)}) %collective-permute-start.17) | collective-permute-done | bytes 131104 | tf_op jit(solution)/shard_map/ppermute | solution.py:793
  200.0 2.5 %shard_map.72 = (f32[64,8,512]{2,1,0:T(8,128)S(1)}, f32[2,8,128]{2,1,0:T(8,128)S(1)}) custom-call(f32[64,8,512]{2,1,0:T(8,128)S(1)} %get-tuple-element.91.refs_0_.refs_3_.refs_2_, f32[8,512]{1,0:T(8,128)S(1)} %select_maximum_fusion.refs_1_.refs_2_, f32[32,128]{1,0:T(8,128)S(1)} %broadcast_in_dim.25.refs_2_.refs_3_, ...), custom_call_target="tpu_custom_call" | custom-call | flops 1 | bytes 1 | tf_op jit(solution)/shard_map/pallas_call | solution.py:626
  205.6 6.9 %shard_map.74.refs_7_ = f32[2,32,128]{2,1,0:T(8,128)S(1)} custom-call(f32[64,24,512]{2,1,0:T(8,128)S(1)} %get-tuple-element.99.refs_0_.refs_1_, f32[64,8,512]{2,1,0:T(8,128)S(1)} %get-tuple-element.100.refs_1_.refs_3_, f32[8,512]{1,0:T(8,128)S(1)} %select_maximum_fusion.refs_1_.refs_2_, f32[32,128]{1,0:T(8,128)S(1)} %broadcast_in_dim.25.refs_2_.refs_3_, ...), custom_call_target="tpu_custom_call" | custom-call | flops 1 | bytes 1 | tf_op jit(solution)/shard_map/pallas_call | solution.py:626
  214.8 2.3 %collective-permute-done.23.refs_6_ = f32[32,128]{1,0:T(8,128)S(1)} collective-permute-done((f32[32,128]{1,0:T(8,128)S(1)}, f32[32,128]{1,0:T(8,128)S(1)}, u32[]{:S(2)}, u32[]{:S(2)}) %collective-permute-start.23) | collective-permute-done | bytes 16416 | tf_op jit(solution)/shard_map/ppermute | solution.py:785
  217.6 4.6 %shard_map.76 = f32[32,64,512]{2,1,0:T(8,128)} custom-call(f32[64,24,512]{2,1,0:T(8,128)S(1)} %get-tuple-element.77.refs_0_.refs_2_, f32[64,24,512]{2,1,0:T(8,128)S(1)} %get-tuple-element.99.refs_0_.refs_1_, f32[64,8,512]{2,1,0:T(8,128)S(1)} %get-tuple-element.91.refs_0_.refs_3_.refs_2_, f32[64,8,512]{2,1,0:T(8,128)S(1)} %get-tuple-element.100.refs_1_.refs_3_, ...), custom_call_target="tpu_custom_call" | custom-call | tf_op jit(solution)/shard_map/pallas_call | solution.py:773
  (79 shorter events, 24.1 us)
Async XLA Ops:
  3.5 86.7 %collective-permute-start.3 = (f32[32,32,128]{2,1,0:T(8,128)}, f32[32,32,128]{2,1,0:T(8,128)S(1)}, u32[]{:S(2)}, u32[]{:S(2)}) collective-permute-start(f32[32,32,128]{2,1,0:T(8,128)} %get-tuple-element.64), channel_id=1, source_target_pairs={{0,4},{1,5},{2,6},{3,7},{4,0},{5,1},{6,2},{7,3},{8,12},{9,13},{10,... | collective-permute-start | bytes 1572872 | tf_op jit(solution)/shard_map/ppermute | solution.py:793
  6.1 84.2 %collective-permute-start.4 = (f32[32,32,128]{2,1,0:T(8,128)}, f32[32,32,128]{2,1,0:T(8,128)S(1)}, u32[]{:S(2)}, u32[]{:S(2)}) collective-permute-start(f32[32,32,128]{2,1,0:T(8,128)} %get-tuple-element.65), channel_id=1, source_target_pairs={{0,5},{1,4},{2,7},{3,6},{4,1},{5,0},{6,3},{7,2},{8,13},{9,12},{10,... | collective-permute-start | bytes 1572872 | tf_op jit(solution)/shard_map/ppermute | solution.py:793
  7.3 82.9 %collective-permute-start.5 = (f32[32,32,128]{2,1,0:T(8,128)}, f32[32,32,128]{2,1,0:T(8,128)S(1)}, u32[]{:S(2)}, u32[]{:S(2)}) collective-permute-start(f32[32,32,128]{2,1,0:T(8,128)} %get-tuple-element.66), channel_id=1, source_target_pairs={{0,6},{1,7},{2,4},{3,5},{4,2},{5,3},{6,0},{7,1},{8,14},{9,15},{10,... | collective-permute-start | bytes 1572872 | tf_op jit(solution)/shard_map/ppermute | solution.py:793
  12.3 24.3 %collective-permute-start = (f32[32,32,128]{2,1,0:T(8,128)}, f32[32,32,128]{2,1,0:T(8,128)S(1)}, u32[]{:S(2)}, u32[]{:S(2)}) collective-permute-start(f32[32,32,128]{2,1,0:T(8,128)} %get-tuple-element.55), channel_id=1, source_target_pairs={{0,1},{1,0},{2,3},{3,2},{4,5},{5,4},{6,7},{7,6},{8,9},{9,8},{10,11... | collective-permute-start | bytes 1572872 | tf_op jit(solution)/shard_map/ppermute | solution.py:793
  12.8 40.6 %collective-permute-start.1 = (f32[32,32,128]{2,1,0:T(8,128)}, f32[32,32,128]{2,1,0:T(8,128)}, u32[]{:S(2)}, u32[]{:S(2)}) collective-permute-start(f32[32,32,128]{2,1,0:T(8,128)} %get-tuple-element.56), channel_id=1, source_target_pairs={{0,2},{1,3},{2,0},{3,1},{4,6},{5,7},{6,4},{7,5},{8,10},{9,11},{10,... | collective-permute-start | bytes 1572872 | tf_op jit(solution)/shard_map/ppermute | solution.py:793
  36.6 60.3 %collective-permute-start.6 = (f32[32,32,128]{2,1,0:T(8,128)}, f32[32,32,128]{2,1,0:T(8,128)S(1)}, u32[]{:S(2)}, u32[]{:S(2)}) collective-permute-start(f32[32,32,128]{2,1,0:T(8,128)} %get-tuple-element.67), channel_id=1, source_target_pairs={{0,7},{1,6},{2,5},{3,4},{4,3},{5,2},{6,1},{7,0},{8,15},{9,14},{10,... | collective-permute-start | bytes 1572872 | tf_op jit(solution)/shard_map/ppermute | solution.py:793
  53.4 30.3 %collective-permute-start.2 = (f32[32,32,128]{2,1,0:T(8,128)}, f32[32,32,128]{2,1,0:T(8,128)S(1)}, u32[]{:S(2)}, u32[]{:S(2)}) collective-permute-start(f32[32,32,128]{2,1,0:T(8,128)} %get-tuple-element.57), channel_id=1, source_target_pairs={{0,3},{1,2},{2,1},{3,0},{4,7},{5,6},{6,5},{7,4},{8,11},{9,10},{10,... | collective-permute-start | bytes 1572872 | tf_op jit(solution)/shard_map/ppermute | solution.py:793
  104.4 26.5 %collective-permute-start.10 = (f32[32,24,128]{2,1,0:T(8,128)S(1)}, f32[32,24,128]{2,1,0:T(8,128)S(1)}, u32[]{:S(2)}, u32[]{:S(2)}) collective-permute-start(f32[32,24,128]{2,1,0:T(8,128)S(1)} %get-tuple-element.73), channel_id=1, source_target_pairs={{0,4},{1,5},{2,6},{3,7},{4,0},{5,1},{6,2},{7,3},{8,12},{9,13},{10,... | collective-permute-start | bytes 1179656 | tf_op jit(solution)/shard_map/ppermute | solution.py:793
  104.4 34.9 %collective-permute-start.11 = (f32[32,24,128]{2,1,0:T(8,128)S(1)}, f32[32,24,128]{2,1,0:T(8,128)S(1)}, u32[]{:S(2)}, u32[]{:S(2)}) collective-permute-start(f32[32,24,128]{2,1,0:T(8,128)S(1)} %get-tuple-element.74), channel_id=1, source_target_pairs={{0,5},{1,4},{2,7},{3,6},{4,1},{5,0},{6,3},{7,2},{8,13},{9,12},{10,... | collective-permute-start | bytes 1179656 | tf_op jit(solution)/shard_map/ppermute | solution.py:793
  109.6 68.9 %collective-permute-start.7 = (f32[32,32,128]{2,1,0:T(8,128)S(1)}, f32[32,32,128]{2,1,0:T(8,128)S(1)}, u32[]{:S(2)}, u32[]{:S(2)}) collective-permute-start(f32[32,32,128]{2,1,0:T(8,128)S(1)} %get-tuple-element.70), channel_id=1, source_target_pairs={{0,1},{1,0},{2,3},{3,2},{4,5},{5,4},{6,7},{7,6},{8,9},{9,8},{10,11... | collective-permute-start | bytes 1572872 | tf_op jit(solution)/shard_map/ppermute | solution.py:793
  110.9 67.6 %collective-permute-start.8 = (f32[32,32,128]{2,1,0:T(8,128)S(1)}, f32[32,32,128]{2,1,0:T(8,128)S(1)}, u32[]{:S(2)}, u32[]{:S(2)}) collective-permute-start(f32[32,32,128]{2,1,0:T(8,128)S(1)} %get-tuple-element.71), channel_id=1, source_target_pairs={{0,2},{1,3},{2,0},{3,1},{4,6},{5,7},{6,4},{7,5},{8,10},{9,11},{10,... | collective-permute-start | bytes 1572872 | tf_op jit(solution)/shard_map/ppermute | solution.py:793
  112.0 68.5 %collective-permute-start.9 = (f32[32,32,128]{2,1,0:T(8,128)S(1)}, f32[32,32,128]{2,1,0:T(8,128)S(1)}, u32[]{:S(2)}, u32[]{:S(2)}) collective-permute-start(f32[32,32,128]{2,1,0:T(8,128)S(1)} %get-tuple-element.72), channel_id=1, source_target_pairs={{0,3},{1,2},{2,1},{3,0},{4,7},{5,6},{6,5},{7,4},{8,11},{9,10},{10,... | collective-permute-start | bytes 1572872 | tf_op jit(solution)/shard_map/ppermute | solution.py:793
  130.9 35.4 %collective-permute-start.12 = (f32[32,24,128]{2,1,0:T(8,128)S(1)}, f32[32,24,128]{2,1,0:T(8,128)S(1)}, u32[]{:S(2)}, u32[]{:S(2)}) collective-permute-start(f32[32,24,128]{2,1,0:T(8,128)S(1)} %get-tuple-element.75), channel_id=1, source_target_pairs={{0,6},{1,7},{2,4},{3,5},{4,2},{5,3},{6,0},{7,1},{8,14},{9,15},{10,... | collective-permute-start | bytes 1179656 | tf_op jit(solution)/shard_map/ppermute | solution.py:793
  139.3 39.2 %collective-permute-start.13 = (f32[32,24,128]{2,1,0:T(8,128)S(1)}, f32[32,24,128]{2,1,0:T(8,128)S(1)}, u32[]{:S(2)}, u32[]{:S(2)}) collective-permute-start(f32[32,24,128]{2,1,0:T(8,128)S(1)} %get-tuple-element.76), channel_id=1, source_target_pairs={{0,7},{1,6},{2,5},{3,4},{4,3},{5,2},{6,1},{7,0},{8,15},{9,14},{10,... | collective-permute-start | bytes 1179656 | tf_op jit(solution)/shard_map/ppermute | solution.py:793
  166.3 22.3 %collective-permute-start.14 = (f32[32,8,128]{2,1,0:T(8,128)S(1)}, f32[32,8,128]{2,1,0:T(8,128)S(1)}, u32[]{:S(2)}, u32[]{:S(2)}) collective-permute-start(f32[32,8,128]{2,1,0:T(8,128)S(1)} %get-tuple-element.86), channel_id=1, source_target_pairs={{0,4},{1,5},{2,6},{3,7},{4,0},{5,1},{6,2},{7,3},{8,12},{9,13},{10,... | collective-permute-start | bytes 393224 | tf_op jit(solution)/shard_map/ppermute | solution.py:793
  178.5 11.3 %collective-permute-start.15 = (f32[32,8,128]{2,1,0:T(8,128)S(1)}, f32[32,8,128]{2,1,0:T(8,128)S(1)}, u32[]{:S(2)}, u32[]{:S(2)}) collective-permute-start(f32[32,8,128]{2,1,0:T(8,128)S(1)} %get-tuple-element.87), channel_id=1, source_target_pairs={{0,5},{1,4},{2,7},{3,6},{4,1},{5,0},{6,3},{7,2},{8,13},{9,12},{10,... | collective-permute-start | bytes 393224 | tf_op jit(solution)/shard_map/ppermute | solution.py:793
  178.5 15.9 %collective-permute-start.16 = (f32[32,8,128]{2,1,0:T(8,128)S(1)}, f32[32,8,128]{2,1,0:T(8,128)S(1)}, u32[]{:S(2)}, u32[]{:S(2)}) collective-permute-start(f32[32,8,128]{2,1,0:T(8,128)S(1)} %get-tuple-element.88), channel_id=1, source_target_pairs={{0,6},{1,7},{2,4},{3,5},{4,2},{5,3},{6,0},{7,1},{8,14},{9,15},{10,... | collective-permute-start | bytes 393224 | tf_op jit(solution)/shard_map/ppermute | solution.py:793
  178.5 19.3 %collective-permute-start.17 = (f32[32,8,128]{2,1,0:T(8,128)S(1)}, f32[32,8,128]{2,1,0:T(8,128)S(1)}, u32[]{:S(2)}, u32[]{:S(2)}) collective-permute-start(f32[32,8,128]{2,1,0:T(8,128)S(1)} %get-tuple-element.89), channel_id=1, source_target_pairs={{0,7},{1,6},{2,5},{3,4},{4,3},{5,2},{6,1},{7,0},{8,15},{9,14},{10,... | collective-permute-start | bytes 393224 | tf_op jit(solution)/shard_map/ppermute | solution.py:793
  198.2 4.4 %collective-permute-start.19 = (f32[8,32,128]{2,1,0:T(8,128)S(1)}, f32[8,32,128]{2,1,0:T(8,128)S(1)}, u32[]{:S(2)}, u32[]{:S(2)}) collective-permute-start(f32[8,32,128]{2,1,0:T(8,128)S(1)} %get-tuple-element.96), channel_id=1, source_target_pairs={{0,8},{8,16},{16,24},{24,0},{1,9},{9,17},{17,25},{25,1},{2,10},{10... | collective-permute-start | bytes 393224 | tf_op jit(solution)/shard_map/ppermute | solution.py:785
  198.2 4.8 %collective-permute-start.18 = (f32[8,32,128]{2,1,0:T(8,128)S(1)}, f32[8,32,128]{2,1,0:T(8,128)S(1)}, u32[]{:S(2)}, u32[]{:S(2)}) collective-permute-start(f32[8,32,128]{2,1,0:T(8,128)S(1)} %get-tuple-element.96), channel_id=1, source_target_pairs={{0,24},{8,0},{16,8},{24,16},{1,25},{9,1},{17,9},{25,17},{2,26},{10... | collective-permute-start | bytes 393224 | tf_op jit(solution)/shard_map/ppermute | solution.py:785
  203.6 8.9 %collective-permute-start.21 = (f32[8,32,128]{2,1,0:T(8,128)S(1)}, f32[8,32,128]{2,1,0:T(8,128)S(1)}, u32[]{:S(2)}, u32[]{:S(2)}) collective-permute-start(f32[8,32,128]{2,1,0:T(8,128)S(1)} %get-tuple-element.101), channel_id=1, source_target_pairs={{0,8},{8,16},{16,24},{24,0},{1,9},{9,17},{17,25},{25,1},{2,10},{10... | collective-permute-start | bytes 393224 | tf_op jit(solution)/shard_map/ppermute | solution.py:785
  204.8 7.7 %collective-permute-start.20 = (f32[8,32,128]{2,1,0:T(8,128)S(1)}, f32[8,32,128]{2,1,0:T(8,128)S(1)}, u32[]{:S(2)}, u32[]{:S(2)}) collective-permute-start(f32[8,32,128]{2,1,0:T(8,128)S(1)} %get-tuple-element.101), channel_id=1, source_target_pairs={{0,24},{8,0},{16,8},{24,16},{1,25},{9,1},{17,9},{25,17},{2,26},{10... | collective-permute-start | bytes 393224 | tf_op jit(solution)/shard_map/ppermute | solution.py:785
  213.4 3.7 %collective-permute-start.23 = (f32[32,128]{1,0:T(8,128)S(1)}, f32[32,128]{1,0:T(8,128)S(1)}, u32[]{:S(2)}, u32[]{:S(2)}) collective-permute-start(f32[32,128]{1,0:T(8,128)S(1)} %shard_map.75.refs_4_), channel_id=1, source_target_pairs={{0,16},{8,24},{16,0},{24,8},{1,17},{9,25},{17,1},{25,9},{2,18},{10... | collective-permute-start | bytes 49160 | tf_op jit(solution)/shard_map/ppermute | solution.py:785
  214.5 3.2 %collective-permute-start.22 = (f32[32,128]{1,0:T(8,128)S(1)}, f32[32,128]{1,0:T(8,128)S(1)}, u32[]{:S(2)}, u32[]{:S(2)}) collective-permute-start(f32[32,128]{1,0:T(8,128)S(1)} %shard_map.75.refs_4_), channel_id=1, source_target_pairs={{0,8},{8,16},{16,24},{24,0},{1,9},{9,17},{17,25},{25,1},{2,10},{10... | collective-permute-start | bytes 49160 | tf_op jit(solution)/shard_map/ppermute | solution.py:785
  (9 other events, 364.4 us)

commit v5 on v4

--- a/solution.py
+++ b/solution.py
@@ -257,11 +257,11 @@
                 x_ref[slot // 2, pl.ds((2 + kind) * half + row, 16), where] = lower
 
 
-def half_terms(fold, me, first, y_refs, geo_ref, x_ref, acc_ref):
+def slot_terms(fold, me, first, count, y_refs, geo_ref, x_ref, acc_ref):
     planes = y_refs[0].shape[1]
-    half = len(y_refs) * planes
+    half = count * planes
     for number, y_ref in enumerate(y_refs):
-        place = (me ^ (first + number)) % len(y_refs)
+        place = (me ^ (first + number)) % count
 
         def chunk(part, _, y_ref=y_ref, place=place):
             base = pl.multiple_of(part * 16, 16)
@@ -272,17 +272,16 @@
         lax.fori_loop(0, planes // 16, chunk, 0)
 
 
-def near_kernel(fold, count, me_ref, geo_ref, *refs):
-    y_refs, (x_ref, acc_ref) = refs[:count], refs[count:]
-    half_terms(fold, me_ref[0], 0, y_refs, geo_ref, x_ref, acc_ref)
-
-
-def far_kernel(fold, count, sizes, me_ref, geo_ref, table_ref, near_ref, *refs):
-    y_refs, refs = refs[:count], refs[count:]
+def terms_kernel(fold, first, count, me_ref, geo_ref, *refs):
+    y_refs, (x_ref, acc_ref) = refs[:-2], refs[-2:]
+    slot_terms(fold, me_ref[0], first, count, y_refs, geo_ref, x_ref, acc_ref)
+
+
+def far_kernel(fold, count, sizes, me_ref, geo_ref, table_ref, near_ref, given_ref, y_ref, *refs):
     chunks = len(sizes)
     out_refs = [refs[k * chunks : (k + 1) * chunks] for k in range(count)]
     x_ref, acc_ref, result_ref = refs[count * chunks :]
-    half_terms(fold, me_ref[0], count, y_refs, geo_ref, x_ref, acc_ref)
+    slot_terms(fold, me_ref[0], 2 * count - 1, count, [y_ref], geo_ref, x_ref, acc_ref)
     transform(fold, 1, me_ref, geo_ref, table_ref, (near_ref, x_ref), out_refs, result_ref)
 
 
@@ -336,13 +335,12 @@
     return [pl.BlockSpec(memory_space=pltpu.VMEM)] * count
 
 
-def near_terms(me, geo, fields, fold):
+def some_terms(me, geo, fields, fold, first, count):
     slots, planes, _ = fields[0].shape
-    count = len(fields)
-    size = count * fields[0].size
+    size = len(fields) * fields[0].size
     return pl.pallas_call(
-        functools.partial(near_kernel, fold, count),
-        in_specs=[smem()] + vmem(1 + count),
+        functools.partial(terms_kernel, fold, first, count),
+        in_specs=[smem()] + vmem(1 + len(fields)),
         out_specs=vmem(1)[0],
         out_shape=jax.ShapeDtypeStruct(
             (slots // 2, 4 * count * planes, 2 * LANES), jnp.bfloat16
@@ -365,16 +363,16 @@
     return jnp.asarray(np.stack([np.concatenate(list(half), axis=1) for half in halves]))
 
 
-def far_modes(me, geo, tables, near, fields, fold, sizes):
-    slots, planes, _ = fields[0].shape
-    count = len(fields)
-    size = count * fields[0].size
+def far_modes(me, geo, tables, near, far, field, fold, count, sizes):
+    slots, planes, _ = field.shape
+    size = count * field.size
     chunks = len(sizes)
     pieces = [jax.ShapeDtypeStruct((slots, k, LANES), jnp.float32) for k in sizes]
     *outs, far = pl.pallas_call(
         functools.partial(far_kernel, fold, count, sizes),
-        in_specs=[smem()] + vmem(3 + count),
+        in_specs=[smem()] + vmem(5),
         out_specs=vmem(chunks * count + 1),
+        input_output_aliases={4: chunks * count},
         out_shape=pieces * count + [jax.ShapeDtypeStruct(near.shape, jnp.bfloat16)],
         scratch_shapes=[
             pltpu.VMEM((slots, 16, LANES), jnp.float32),
@@ -384,7 +382,7 @@
         cost_estimate=pl.CostEstimate(
             flops=12 * count * planes * size, bytes_accessed=8 * size, transcendentals=0
         ),
-    )(me, geo, tables, near, *fields)
+    )(me, geo, tables, near, far, field)
     return [outs[k::chunks] for k in range(chunks)], far
 
 
@@ -846,17 +844,22 @@
     flag = jnp.broadcast_to(wall_flags.astype(jnp.float32)[:, None], (planes, LANES))
     tables = edge_tables(nbr_elem, nbr_edge)
     near_sent = pack(index, concentration, fold, groups, 0)
-    far_sent = pack(index, concentration, fold, groups, groups // 2)
+    far_sent = list(pack(index, concentration, fold, groups, groups // 2))
+    half = groups // 2
     near_field = exchanged(near_sent)
-    far_field = exchanged(far_sent, groups // 2)
+    near_field[2], far_sent[-1] = lax.optimization_barrier((near_field[2], far_sent[-1]))
+    far_field = exchanged(far_sent, half)
     near_field, geo, mine, mass, flag, tables = lax.optimization_barrier(
         (near_field, geo, mine, mass, flag, tables)
     )
     local, far, mask, edges = tables
-    near = near_terms(index, mine, near_field, fold)
+    near = some_terms(index, mine, near_field, fold, 0, half)
+    far_terms = some_terms(index, mine, far_field[:-1], fold, half, half)
     sizes = [planes - 8, 8] if planes > 16 else [planes]
     tables = transform_tables(planes * groups)
-    sent, far_terms = far_modes(index, mine, tables, near, far_field, fold, sizes)
+    sent, far_terms = far_modes(
+        index, mine, tables, near, far_terms, far_field[-1], fold, half, sizes
+    )
     far_parts = [exchanged(piece, groups // 2) for piece in sent]
     near_parts = exchanged(near_modes(index, mine, tables, near, far_terms, fold, planes))
     fields, images, sums, sends = [], [], [], []

time: 222 us -> 218 us (0.982)
    pallas_call x1, Pallas kernels: 7.48 us -> 3.49 us  [far_modes(): pl.pallas_call(functools.partial(far_kernel, fold, count, sizes), in_spec...]
    pallas_call x1 -> x2, Pallas kernels: 6.38 us -> 9.33 us  [some_terms(): pl.pallas_call(functools.partial(terms_kernel, fold, first, count), in_sp...]
  transfers between devices with their start and end apart: 25 -> 25, of which waited for: 16 -> 16; matrix products, arithmetic and copies ran while one was open for 4% -> 4% of each run, Pallas kernels for 13% -> 15%
where the time goes in v5:
time: 218 us
  waiting for transfers between devices  140 us (64%)
  Pallas kernels  44.9 us (21%)
  starting transfers between devices  25.1 us (12%)
  other arithmetic  7.65 us (4%)
    ppermute x18, waiting for transfers between devices, exchanged(): lax.ppermute(value, 'gz', [(i, i ^ d) for i in range(size)])  136 us
    ppermute x18, starting transfers between devices, exchanged(): lax.ppermute(value, 'gz', [(i, i ^ d) for i in range(size)])  19.6 us
    pallas_call x3, Pallas kernels, apply_local(): pl.pallas_call(functools.partial(apply_kernel, want_image, len(fields), f...  16.3 us
    pallas_call x2, Pallas kernels, some_terms(): pl.pallas_call(functools.partial(terms_kernel, fold, first, count), in_sp...  9.33 us
    convert_element_type x1, other arithmetic, edge_tables(): local = (source == place[None, :]).astype(jnp.bfloat16)  7.46 us
    pallas_call x2, Pallas kernels, pack(): pl.pallas_call(functools.partial(pack_kernel, fold), grid_spec=pltpu.Pref...  6.86 us
    ppermute x7, starting transfers between devices, shifted(): lax.ppermute(value, axis, [(i, (i + steps) % size) for i in range(size)])  5.52 us
    pallas_call x1, Pallas kernels, finish(): pl.pallas_call(functools.partial(finish_kernel, len(sums), chunks), grid=...  4.63 us
  transfers between devices with their start and end apart: 25, of which 16 were waited for; matrix products, arithmetic and copies ran while one was open for 4% of the time, Pallas kernels for 15%

profile of v5, /device:TPU:8, one launch (start us, length us, event | category | flops | bytes accessed | tf_op | source)
XLA Modules:
  0.0 218.3 jit_solution(2829335578309756081)
XLA Ops:
  0.0 3.5 %shard_map.65 = (f32[32,32,128]{2,1,0:T(8,128)}, f32[32,32,128]{2,1,0:T(8,128)}, f32[32,32,128]{2,1,0:T(8,128)}, f32[32,32,128]{2,1,0:T(8,128)}) custom-call(s32[1]{0:T(128)} %bitcast.me_ref, f32[32,64,512]{2,1,0:T(8,128)} %c_ref.3), custom_call_target="tpu_custom_call" | custom-call | flops 1048576 | bytes 4194304 | tf_op jit(solution)/shard_map/pallas_call | solution.py:200
  3.5 2.6 %collective-permute-start.3 = (f32[32,32,128]{2,1,0:T(8,128)}, f32[32,32,128]{2,1,0:T(8,128)S(1)}, u32[]{:S(2)}, u32[]{:S(2)}) collective-permute-start(f32[32,32,128]{2,1,0:T(8,128)} %get-tuple-element.68), channel_id=1, source_target_pairs={{0,4},{1,5},{2,6},{3,7},{4,0},{5,1},{6,2},{7,3},{8,12},{9,13},{10,... | collective-permute-start | bytes 1572872 | tf_op jit(solution)/shard_map/ppermute | solution.py:791
  8.9 3.4 %shard_map.64 = (f32[32,32,128]{2,1,0:T(8,128)}, f32[32,32,128]{2,1,0:T(8,128)}, f32[32,32,128]{2,1,0:T(8,128)}, f32[32,32,128]{2,1,0:T(8,128)}) custom-call(s32[1]{0:T(128)} %bitcast.me_ref, f32[32,64,512]{2,1,0:T(8,128)} %c_ref.3), custom_call_target="tpu_custom_call" | custom-call | flops 1048576 | bytes 4194304 | tf_op jit(solution)/shard_map/pallas_call | solution.py:200
  12.8 2.5 %collective-permute-start.1 = (f32[32,32,128]{2,1,0:T(8,128)}, f32[32,32,128]{2,1,0:T(8,128)S(1)}, u32[]{:S(2)}, u32[]{:S(2)}) collective-permute-start(f32[32,32,128]{2,1,0:T(8,128)} %get-tuple-element.58), channel_id=1, source_target_pairs={{0,2},{1,3},{2,0},{3,1},{4,6},{5,7},{6,4},{7,5},{8,10},{9,11},{10,... | collective-permute-start | bytes 1572872 | tf_op jit(solution)/shard_map/ppermute | solution.py:791
  15.5 7.5 %fusion.refs_4_.refs_5_ = bf16[2048,2048]{1,0:T(8,128)(2,1)} fusion(s32[2048]{0:T(1024)S(1)} %bitcast.20), kind=kLoop, calls=%fused_computation.1 | loop fusion | flops 8388608 | bytes 8396800 | tf_op jit(solution)/shard_map/convert_element_type | solution.py:814
  23.2 28.9 %collective-permute-done.1.refs_2_ = f32[32,32,128]{2,1,0:T(8,128)S(1)} collective-permute-done((f32[32,32,128]{2,1,0:T(8,128)}, f32[32,32,128]{2,1,0:T(8,128)S(1)}, u32[]{:S(2)}, u32[]{:S(2)}) %collective-permute-start.1) | collective-permute-done | bytes 524320 | tf_op jit(solution)/shard_map/ppermute | solution.py:791
  53.6 30.1 %collective-permute-done.2.refs_3_ = f32[32,32,128]{2,1,0:T(8,128)S(1)} collective-permute-done((f32[32,32,128]{2,1,0:T(8,128)}, f32[32,32,128]{2,1,0:T(8,128)S(1)}, u32[]{:S(2)}, u32[]{:S(2)}) %collective-permute-start.2) | collective-permute-done | bytes 524320 | tf_op jit(solution)/shard_map/ppermute | solution.py:791
  85.5 4.0 %shard_map.67.given_ref = bf16[16,512,256]{2,1,0:T(8,128)(2,1)S(1)} custom-call(s32[1]{0:T(128)} %bitcast.me_ref, f32[8,128]{1,0:T(8,128)S(1)} %tile.10.geo_ref, f32[32,32,128]{2,1,0:T(8,128)S(1)} %collective-permute-done.3.refs_0_, f32[32,32,128]{2,1,0:T(8,128)S(1)} %collective-permute-done.4.refs_1_, f32[32,32,128]{2,1,0:T(8,128)S(1)} %collective-permute-done.5.refs_2_), custom_call_target="tpu_custom_call" | custom-call | flops 31457280 | bytes 4718592 | tf_op jit(solution)/shard_map/pallas_call | solution.py:341
  89.5 5.3 %shard_map.66.near_ref = bf16[16,512,256]{2,1,0:T(8,128)(2,1)S(1)} custom-call(s32[1]{0:T(128)} %bitcast.me_ref, f32[8,128]{1,0:T(8,128)S(1)} %tile.10.geo_ref, f32[32,32,128]{2,1,0:T(8,128)S(1)} %copy-done.1, f32[32,32,128]{2,1,0:T(8,128)S(1)} %collective-permute-done.refs_1_, f32[32,32,128]{2,1,0:T(8,128)S(1)} %collective-permute-done.1.refs_2_, ...), custom_call_target="tpu_custom_call" | custom-call | flops 41943040 | bytes 6291456 | tf_op jit(solution)/shard_map/pallas_call | solution.py:341
  94.8 2.0 collective-permute-done.6.y_ref
  96.9 3.5 %shard_map.68 = (f32[32,24,128]{2,1,0:T(8,128)S(1)}, f32[32,8,128]{2,1,0:T(8,128)S(1)}, f32[32,24,128]{2,1,0:T(8,128)S(1)}, f32[32,8,128]{2,1,0:T(8,128)S(1)}, f...) custom-call(s32[1]{0:T(128)} %bitcast.me_ref, ...), custom_call_target="tpu_custom_call", output_to_operand_aliasing={{8}: (4, {})} | custom-call | flops 805306368 | bytes 4194304 | tf_op jit(solution)/shard_map/pallas_call | solution.py:371
  103.6 2.0 shard_map.69
  109.1 19.5 %collective-permute-done.10.refs_4_ = f32[32,24,128]{2,1,0:T(8,128)S(1)} collective-permute-done((f32[32,24,128]{2,1,0:T(8,128)S(1)}, f32[32,24,128]{2,1,0:T(8,128)S(1)}, u32[]{:S(2)}, u32[]{:S(2)}) %collective-permute-start.10) | collective-permute-done | bytes 393248 | tf_op jit(solution)/shard_map/ppermute | solution.py:791
  128.6 8.4 %collective-permute-done.11.refs_5_ = f32[32,24,128]{2,1,0:T(8,128)S(1)} collective-permute-done((f32[32,24,128]{2,1,0:T(8,128)S(1)}, f32[32,24,128]{2,1,0:T(8,128)S(1)}, u32[]{:S(2)}, u32[]{:S(2)}) %collective-permute-start.11) | collective-permute-done | bytes 393248 | tf_op jit(solution)/shard_map/ppermute | solution.py:791
  137.5 24.8 %collective-permute-done.12.refs_6_ = f32[32,24,128]{2,1,0:T(8,128)S(1)} collective-permute-done((f32[32,24,128]{2,1,0:T(8,128)S(1)}, f32[32,24,128]{2,1,0:T(8,128)S(1)}, u32[]{:S(2)}, u32[]{:S(2)}) %collective-permute-start.12) | collective-permute-done | bytes 393248 | tf_op jit(solution)/shard_map/ppermute | solution.py:791
  162.3 12.1 %collective-permute-done.13.refs_7_ = f32[32,24,128]{2,1,0:T(8,128)S(1)} collective-permute-done((f32[32,24,128]{2,1,0:T(8,128)S(1)}, f32[32,24,128]{2,1,0:T(8,128)S(1)}, u32[]{:S(2)}, u32[]{:S(2)}) %collective-permute-start.13) | collective-permute-done | bytes 393248 | tf_op jit(solution)/shard_map/ppermute | solution.py:791
  178.2 7.0 %shard_map.71 = (f32[64,24,512]{2,1,0:T(8,128)S(1)}, f32[2,24,128]{2,1,0:T(8,128)S(1)}) custom-call(f32[64,24,512]{2,1,0:T(8,128)S(1)} %get-tuple-element.81.refs_0_.refs_2_, f32[8,512]{1,0:T(8,128)S(1)} %select_maximum_fusion.refs_1_.refs_2_, f32[32,128]{1,0:T(8,128)S(1)} %broadcast_in_dim.25.refs_2_.refs_3_, ...), custom_call_target="tpu_custom_call" | custom-call | flops 1 | bytes 1 | tf_op jit(solution)/shard_map/pallas_call | solution.py:624
  185.1 2.5 %collective-permute-done.15.refs_5_ = f32[32,8,128]{2,1,0:T(8,128)S(1)} collective-permute-done((f32[32,8,128]{2,1,0:T(8,128)S(1)}, f32[32,8,128]{2,1,0:T(8,128)S(1)}, u32[]{:S(2)}, u32[]{:S(2)}) %collective-permute-start.15) | collective-permute-done | bytes 131104 | tf_op jit(solution)/shard_map/ppermute | solution.py:791
  187.6 4.1 %collective-permute-done.16.refs_6_ = f32[32,8,128]{2,1,0:T(8,128)S(1)} collective-permute-done((f32[32,8,128]{2,1,0:T(8,128)S(1)}, f32[32,8,128]{2,1,0:T(8,128)S(1)}, u32[]{:S(2)}, u32[]{:S(2)}) %collective-permute-start.16) | collective-permute-done | bytes 131104 | tf_op jit(solution)/shard_map/ppermute | solution.py:791
  191.7 2.1 collective-permute-done.17.refs_7_
  196.0 2.5 %shard_map.73 = (f32[64,8,512]{2,1,0:T(8,128)S(1)}, f32[2,8,128]{2,1,0:T(8,128)S(1)}) custom-call(f32[64,8,512]{2,1,0:T(8,128)S(1)} %get-tuple-element.95.refs_0_.refs_3_.refs_2_, f32[8,512]{1,0:T(8,128)S(1)} %select_maximum_fusion.refs_1_.refs_2_, f32[32,128]{1,0:T(8,128)S(1)} %broadcast_in_dim.25.refs_2_.refs_3_, ...), custom_call_target="tpu_custom_call" | custom-call | flops 1 | bytes 1 | tf_op jit(solution)/shard_map/pallas_call | solution.py:624
  201.6 6.9 %shard_map.75.refs_7_ = f32[2,32,128]{2,1,0:T(8,128)S(1)} custom-call(f32[64,24,512]{2,1,0:T(8,128)S(1)} %get-tuple-element.103.refs_0_.refs_1_, f32[64,8,512]{2,1,0:T(8,128)S(1)} %get-tuple-element.104.refs_1_.refs_3_, f32[8,512]{1,0:T(8,128)S(1)} %select_maximum_fusion.refs_1_.refs_2_, f32[32,128]{1,0:T(8,128)S(1)} %broadcast_in_dim.25.refs_2_.refs_3_, ...), custom_call_target="tpu_custom_call" | custom-call | flops 1 | bytes 1 | tf_op jit(solution)/shard_map/pallas_call | solution.py:624
  210.8 2.3 %collective-permute-done.23.refs_6_ = f32[32,128]{1,0:T(8,128)S(1)} collective-permute-done((f32[32,128]{1,0:T(8,128)S(1)}, f32[32,128]{1,0:T(8,128)S(1)}, u32[]{:S(2)}, u32[]{:S(2)}) %collective-permute-start.23) | collective-permute-done | bytes 16416 | tf_op jit(solution)/shard_map/ppermute | solution.py:783
  213.6 4.6 %shard_map.77 = f32[32,64,512]{2,1,0:T(8,128)} custom-call(f32[64,24,512]{2,1,0:T(8,128)S(1)} %get-tuple-element.81.refs_0_.refs_2_, f32[64,24,512]{2,1,0:T(8,128)S(1)} %get-tuple-element.103.refs_0_.refs_1_, f32[64,8,512]{2,1,0:T(8,128)S(1)} %get-tuple-element.95.refs_0_.refs_3_.refs_2_, f32[64,8,512]{2,1,0:T(8,128)S(1)} %get-tuple-element.104.refs_1_.refs_3_, ...), custom_call_target="tpu_custom_call" | custom-call | tf_op jit(solution)/shard_map/pallas_call | solution.py:771
  (80 shorter events, 26.0 us)
Async XLA Ops:
  3.5 80.3 %collective-permute-start.3 = (f32[32,32,128]{2,1,0:T(8,128)}, f32[32,32,128]{2,1,0:T(8,128)S(1)}, u32[]{:S(2)}, u32[]{:S(2)}) collective-permute-start(f32[32,32,128]{2,1,0:T(8,128)} %get-tuple-element.68), channel_id=1, source_target_pairs={{0,4},{1,5},{2,6},{3,7},{4,0},{5,1},{6,2},{7,3},{8,12},{9,13},{10,... | collective-permute-start | bytes 1572872 | tf_op jit(solution)/shard_map/ppermute | solution.py:791
  6.1 77.8 %collective-permute-start.4 = (f32[32,32,128]{2,1,0:T(8,128)}, f32[32,32,128]{2,1,0:T(8,128)S(1)}, u32[]{:S(2)}, u32[]{:S(2)}) collective-permute-start(f32[32,32,128]{2,1,0:T(8,128)} %get-tuple-element.69), channel_id=1, source_target_pairs={{0,5},{1,4},{2,7},{3,6},{4,1},{5,0},{6,3},{7,2},{8,13},{9,12},{10,... | collective-permute-start | bytes 1572872 | tf_op jit(solution)/shard_map/ppermute | solution.py:791
  7.3 78.1 %collective-permute-start.5 = (f32[32,32,128]{2,1,0:T(8,128)}, f32[32,32,128]{2,1,0:T(8,128)S(1)}, u32[]{:S(2)}, u32[]{:S(2)}) collective-permute-start(f32[32,32,128]{2,1,0:T(8,128)} %get-tuple-element.70), channel_id=1, source_target_pairs={{0,6},{1,7},{2,4},{3,5},{4,2},{5,3},{6,0},{7,1},{8,14},{9,15},{10,... | collective-permute-start | bytes 1572872 | tf_op jit(solution)/shard_map/ppermute | solution.py:791
  12.3 40.5 %collective-permute-start = (f32[32,32,128]{2,1,0:T(8,128)}, f32[32,32,128]{2,1,0:T(8,128)S(1)}, u32[]{:S(2)}, u32[]{:S(2)}) collective-permute-start(f32[32,32,128]{2,1,0:T(8,128)} %get-tuple-element.57), channel_id=1, source_target_pairs={{0,1},{1,0},{2,3},{3,2},{4,5},{5,4},{6,7},{7,6},{8,9},{9,8},{10,11... | collective-permute-start | bytes 1572872 | tf_op jit(solution)/shard_map/ppermute | solution.py:791
  12.8 39.3 %collective-permute-start.1 = (f32[32,32,128]{2,1,0:T(8,128)}, f32[32,32,128]{2,1,0:T(8,128)S(1)}, u32[]{:S(2)}, u32[]{:S(2)}) collective-permute-start(f32[32,32,128]{2,1,0:T(8,128)} %get-tuple-element.58), channel_id=1, source_target_pairs={{0,2},{1,3},{2,0},{3,1},{4,6},{5,7},{6,4},{7,5},{8,10},{9,11},{10,... | collective-permute-start | bytes 1572872 | tf_op jit(solution)/shard_map/ppermute | solution.py:791
  52.2 31.5 %collective-permute-start.2 = (f32[32,32,128]{2,1,0:T(8,128)}, f32[32,32,128]{2,1,0:T(8,128)S(1)}, u32[]{:S(2)}, u32[]{:S(2)}) collective-permute-start(f32[32,32,128]{2,1,0:T(8,128)} %get-tuple-element.61), channel_id=1, source_target_pairs={{0,3},{1,2},{2,1},{3,0},{4,7},{5,6},{6,5},{7,4},{8,11},{9,10},{10,... | collective-permute-start | bytes 1572872 | tf_op jit(solution)/shard_map/ppermute | solution.py:791
  52.8 44.1 %collective-permute-start.6 = (f32[32,32,128]{2,1,0:T(8,128)}, f32[32,32,128]{2,1,0:T(8,128)S(1)}, u32[]{:S(2)}, u32[]{:S(2)}) collective-permute-start(f32[32,32,128]{2,1,0:T(8,128)} %get-tuple-element.71), channel_id=1, source_target_pairs={{0,7},{1,6},{2,5},{3,4},{4,3},{5,2},{6,1},{7,0},{8,15},{9,14},{10,... | collective-permute-start | bytes 1572872 | tf_op jit(solution)/shard_map/ppermute | solution.py:791
  100.4 28.2 %collective-permute-start.10 = (f32[32,24,128]{2,1,0:T(8,128)S(1)}, f32[32,24,128]{2,1,0:T(8,128)S(1)}, u32[]{:S(2)}, u32[]{:S(2)}) collective-permute-start(f32[32,24,128]{2,1,0:T(8,128)S(1)} %get-tuple-element.77), channel_id=1, source_target_pairs={{0,4},{1,5},{2,6},{3,7},{4,0},{5,1},{6,2},{7,3},{8,12},{9,13},{10,... | collective-permute-start | bytes 1179656 | tf_op jit(solution)/shard_map/ppermute | solution.py:791
  102.2 34.8 %collective-permute-start.11 = (f32[32,24,128]{2,1,0:T(8,128)S(1)}, f32[32,24,128]{2,1,0:T(8,128)S(1)}, u32[]{:S(2)}, u32[]{:S(2)}) collective-permute-start(f32[32,24,128]{2,1,0:T(8,128)S(1)} %get-tuple-element.78), channel_id=1, source_target_pairs={{0,5},{1,4},{2,7},{3,6},{4,1},{5,0},{6,3},{7,2},{8,13},{9,12},{10,... | collective-permute-start | bytes 1179656 | tf_op jit(solution)/shard_map/ppermute | solution.py:791
  105.6 68.9 %collective-permute-start.7 = (f32[32,32,128]{2,1,0:T(8,128)S(1)}, f32[32,32,128]{2,1,0:T(8,128)S(1)}, u32[]{:S(2)}, u32[]{:S(2)}) collective-permute-start(f32[32,32,128]{2,1,0:T(8,128)S(1)} %get-tuple-element.74), channel_id=1, source_target_pairs={{0,1},{1,0},{2,3},{3,2},{4,5},{5,4},{6,7},{7,6},{8,9},{9,8},{10,11... | collective-permute-start | bytes 1572872 | tf_op jit(solution)/shard_map/ppermute | solution.py:791
  106.9 69.1 %collective-permute-start.8 = (f32[32,32,128]{2,1,0:T(8,128)S(1)}, f32[32,32,128]{2,1,0:T(8,128)S(1)}, u32[]{:S(2)}, u32[]{:S(2)}) collective-permute-start(f32[32,32,128]{2,1,0:T(8,128)S(1)} %get-tuple-element.75), channel_id=1, source_target_pairs={{0,2},{1,3},{2,0},{3,1},{4,6},{5,7},{6,4},{7,5},{8,10},{9,11},{10,... | collective-permute-start | bytes 1572872 | tf_op jit(solution)/shard_map/ppermute | solution.py:791
  108.1 69.0 %collective-permute-start.9 = (f32[32,32,128]{2,1,0:T(8,128)S(1)}, f32[32,32,128]{2,1,0:T(8,128)S(1)}, u32[]{:S(2)}, u32[]{:S(2)}) collective-permute-start(f32[32,32,128]{2,1,0:T(8,128)S(1)} %get-tuple-element.76), channel_id=1, source_target_pairs={{0,3},{1,2},{2,1},{3,0},{4,7},{5,6},{6,5},{7,4},{8,11},{9,10},{10,... | collective-permute-start | bytes 1572872 | tf_op jit(solution)/shard_map/ppermute | solution.py:791
  128.6 33.7 %collective-permute-start.12 = (f32[32,24,128]{2,1,0:T(8,128)S(1)}, f32[32,24,128]{2,1,0:T(8,128)S(1)}, u32[]{:S(2)}, u32[]{:S(2)}) collective-permute-start(f32[32,24,128]{2,1,0:T(8,128)S(1)} %get-tuple-element.79), channel_id=1, source_target_pairs={{0,6},{1,7},{2,4},{3,5},{4,2},{5,3},{6,0},{7,1},{8,14},{9,15},{10,... | collective-permute-start | bytes 1179656 | tf_op jit(solution)/shard_map/ppermute | solution.py:791
  137.0 37.4 %collective-permute-start.13 = (f32[32,24,128]{2,1,0:T(8,128)S(1)}, f32[32,24,128]{2,1,0:T(8,128)S(1)}, u32[]{:S(2)}, u32[]{:S(2)}) collective-permute-start(f32[32,24,128]{2,1,0:T(8,128)S(1)} %get-tuple-element.80), channel_id=1, source_target_pairs={{0,7},{1,6},{2,5},{3,4},{4,3},{5,2},{6,1},{7,0},{8,15},{9,14},{10,... | collective-permute-start | bytes 1179656 | tf_op jit(solution)/shard_map/ppermute | solution.py:791
  162.3 22.8 %collective-permute-start.14 = (f32[32,8,128]{2,1,0:T(8,128)S(1)}, f32[32,8,128]{2,1,0:T(8,128)S(1)}, u32[]{:S(2)}, u32[]{:S(2)}) collective-permute-start(f32[32,8,128]{2,1,0:T(8,128)S(1)} %get-tuple-element.90), channel_id=1, source_target_pairs={{0,4},{1,5},{2,6},{3,7},{4,0},{5,1},{6,2},{7,3},{8,12},{9,13},{10,... | collective-permute-start | bytes 393224 | tf_op jit(solution)/shard_map/ppermute | solution.py:791
  174.5 13.1 %collective-permute-start.15 = (f32[32,8,128]{2,1,0:T(8,128)S(1)}, f32[32,8,128]{2,1,0:T(8,128)S(1)}, u32[]{:S(2)}, u32[]{:S(2)}) collective-permute-start(f32[32,8,128]{2,1,0:T(8,128)S(1)} %get-tuple-element.91), channel_id=1, source_target_pairs={{0,5},{1,4},{2,7},{3,6},{4,1},{5,0},{6,3},{7,2},{8,13},{9,12},{10,... | collective-permute-start | bytes 393224 | tf_op jit(solution)/shard_map/ppermute | solution.py:791
  174.5 17.2 %collective-permute-start.16 = (f32[32,8,128]{2,1,0:T(8,128)S(1)}, f32[32,8,128]{2,1,0:T(8,128)S(1)}, u32[]{:S(2)}, u32[]{:S(2)}) collective-permute-start(f32[32,8,128]{2,1,0:T(8,128)S(1)} %get-tuple-element.92), channel_id=1, source_target_pairs={{0,6},{1,7},{2,4},{3,5},{4,2},{5,3},{6,0},{7,1},{8,14},{9,15},{10,... | collective-permute-start | bytes 393224 | tf_op jit(solution)/shard_map/ppermute | solution.py:791
  176.0 17.8 %collective-permute-start.17 = (f32[32,8,128]{2,1,0:T(8,128)S(1)}, f32[32,8,128]{2,1,0:T(8,128)S(1)}, u32[]{:S(2)}, u32[]{:S(2)}) collective-permute-start(f32[32,8,128]{2,1,0:T(8,128)S(1)} %get-tuple-element.93), channel_id=1, source_target_pairs={{0,7},{1,6},{2,5},{3,4},{4,3},{5,2},{6,1},{7,0},{8,15},{9,14},{10,... | collective-permute-start | bytes 393224 | tf_op jit(solution)/shard_map/ppermute | solution.py:791
  194.2 4.4 %collective-permute-start.19 = (f32[8,32,128]{2,1,0:T(8,128)S(1)}, f32[8,32,128]{2,1,0:T(8,128)S(1)}, u32[]{:S(2)}, u32[]{:S(2)}) collective-permute-start(f32[8,32,128]{2,1,0:T(8,128)S(1)} %get-tuple-element.100), channel_id=1, source_target_pairs={{0,8},{8,16},{16,24},{24,0},{1,9},{9,17},{17,25},{25,1},{2,10},{10... | collective-permute-start | bytes 393224 | tf_op jit(solution)/shard_map/ppermute | solution.py:783
  194.2 4.8 %collective-permute-start.18 = (f32[8,32,128]{2,1,0:T(8,128)S(1)}, f32[8,32,128]{2,1,0:T(8,128)S(1)}, u32[]{:S(2)}, u32[]{:S(2)}) collective-permute-start(f32[8,32,128]{2,1,0:T(8,128)S(1)} %get-tuple-element.100), channel_id=1, source_target_pairs={{0,24},{8,0},{16,8},{24,16},{1,25},{9,1},{17,9},{25,17},{2,26},{10... | collective-permute-start | bytes 393224 | tf_op jit(solution)/shard_map/ppermute | solution.py:783
  199.6 8.9 %collective-permute-start.21 = (f32[8,32,128]{2,1,0:T(8,128)S(1)}, f32[8,32,128]{2,1,0:T(8,128)S(1)}, u32[]{:S(2)}, u32[]{:S(2)}) collective-permute-start(f32[8,32,128]{2,1,0:T(8,128)S(1)} %get-tuple-element.105), channel_id=1, source_target_pairs={{0,8},{8,16},{16,24},{24,0},{1,9},{9,17},{17,25},{25,1},{2,10},{10... | collective-permute-start | bytes 393224 | tf_op jit(solution)/shard_map/ppermute | solution.py:783
  200.9 7.7 %collective-permute-start.20 = (f32[8,32,128]{2,1,0:T(8,128)S(1)}, f32[8,32,128]{2,1,0:T(8,128)S(1)}, u32[]{:S(2)}, u32[]{:S(2)}) collective-permute-start(f32[8,32,128]{2,1,0:T(8,128)S(1)} %get-tuple-element.105), channel_id=1, source_target_pairs={{0,24},{8,0},{16,8},{24,16},{1,25},{9,1},{17,9},{25,17},{2,26},{10... | collective-permute-start | bytes 393224 | tf_op jit(solution)/shard_map/ppermute | solution.py:783
  209.4 3.7 %collective-permute-start.23 = (f32[32,128]{1,0:T(8,128)S(1)}, f32[32,128]{1,0:T(8,128)S(1)}, u32[]{:S(2)}, u32[]{:S(2)}) collective-permute-start(f32[32,128]{1,0:T(8,128)S(1)} %shard_map.76.refs_4_), channel_id=1, source_target_pairs={{0,16},{8,24},{16,0},{24,8},{1,17},{9,25},{17,1},{25,9},{2,18},{10... | collective-permute-start | bytes 49160 | tf_op jit(solution)/shard_map/ppermute | solution.py:783
  210.5 3.2 %collective-permute-start.22 = (f32[32,128]{1,0:T(8,128)S(1)}, f32[32,128]{1,0:T(8,128)S(1)}, u32[]{:S(2)}, u32[]{:S(2)}) collective-permute-start(f32[32,128]{1,0:T(8,128)S(1)} %shard_map.76.refs_4_), channel_id=1, source_target_pairs={{0,8},{8,16},{16,24},{24,0},{1,9},{9,17},{17,25},{25,1},{2,10},{10... | collective-permute-start | bytes 49160 | tf_op jit(solution)/shard_map/ppermute | solution.py:783
  (9 other events, 293.2 us)

commit v6 on v5

--- a/solution.py
+++ b/solution.py
@@ -188,9 +188,8 @@
                         out_refs[step * fold.parts + p][fold.slot(jp, ip)] = value
 
 
-def pack(me, conc, fold, groups, first):
+def pack(me, conc, fold, groups, first, count):
     planes, nodes, elems = conc.shape
-    count = groups // 2
     offset = first // fold.parts
 
     def block(step, me_ref):
@@ -480,7 +479,9 @@
     )(me, mask, *parts, *sends)
 
 
-def volume(field_ref, geo_ref, mass_ref, first, image_ref, sums_ref, row_of_sums, acc_ref):
+def volume(
+    field_ref, geo_ref, mass_ref, first, image_ref, sums_ref, row_of_sums, acc_ref, start=0, step=1
+):
     modes, elems = field_ref.shape[1:]
     tiles = modes // 8
 
@@ -488,7 +489,8 @@
         row = pl.multiple_of(number % tiles * 8, 8)
         rows = pl.ds(row, 8)
         sum_rows = pl.ds(row + row_of_sums, 8)
-        lanes = pl.ds(pl.multiple_of(number // tiles * LANES, LANES), LANES)
+        block = number // tiles * step + start
+        lanes = pl.ds(pl.multiple_of(block * LANES, LANES), LANES)
         jac = geo_ref[0:1, lanes] * mass_ref[pl.ds(row + first, 8), :]
         square_x = jnp.broadcast_to(geo_ref[0:1, lanes] * geo_ref[1:2, lanes], (8, LANES))
         square_y = jnp.broadcast_to(geo_ref[0:1, lanes] * geo_ref[2:3, lanes], (8, LANES))
@@ -515,7 +517,28 @@
             sums_ref[k, sum_rows, :] += totals[k]
         return 0
 
-    lax.fori_loop(0, tiles * (elems // LANES), tile, 0)
+    blocks = -(-(elems // LANES - start) // step)
+    lax.fori_loop(0, tiles * blocks, tile, 0)
+
+
+def inner_kernel(field_ref, geo_ref, mass_ref, sums_ref, acc_ref):
+    sums_ref[...] = jnp.zeros_like(sums_ref)
+    blocks = field_ref.shape[2] // LANES
+    for block in range(1, blocks - 1):
+        volume(field_ref, geo_ref, mass_ref, 0, None, sums_ref, 0, acc_ref, block, blocks)
+
+
+def inner_sums(field, geo, mass):
+    _, modes, _ = field.shape
+    return pl.pallas_call(
+        inner_kernel,
+        in_specs=vmem(3),
+        out_specs=vmem(1)[0],
+        out_shape=jax.ShapeDtypeStruct((2, modes, LANES), jnp.float32),
+        scratch_shapes=[pltpu.VMEM((64, 8, LANES), jnp.float32)],
+        compiler_params=pltpu.CompilerParams(vmem_limit_bytes=4 * MIB),
+        cost_estimate=small_cost(),
+    )(field, geo, mass)
 
 
 def fill_pairs(target_ref, first, modes, lanes, value_of, parts):
@@ -584,8 +607,9 @@
             visit(edge, t, other * np.float32(-edge_penalty * WEIGHTS[t]))
 
 
-def apply_kernel(want_image, count, first, *refs):
+def apply_kernel(want_image, count, first, given, *refs):
     fields, refs = refs[:count], refs[count:]
+    inner, refs = refs[:given], refs[given:]
     geo_ref, mass_ref, flag_ref, local_ref, edges_ref = refs[:5]
     refs = refs[5:]
     image_ref = refs[0] if want_image else None
@@ -594,7 +618,11 @@
     start = 0
     for field_ref in fields:
         row = first + start
-        volume(field_ref, geo_ref, mass_ref, row, image_ref, sums_ref, start, acc_ref)
+        step = 1
+        if inner and start == 0:
+            sums_ref[:, : field_ref.shape[1], :] = inner[0][...]
+            step = field_ref.shape[2] // LANES - 1
+        volume(field_ref, geo_ref, mass_ref, row, image_ref, sums_ref, start, acc_ref, 0, step)
         start += field_ref.shape[1]
     totals = [None] * count
 
@@ -615,15 +643,15 @@
         sums_ref[1, rows, :] += totals[chunk]
 
 
-def apply_local(fields, first, geo, mass, flag, local, edges, want_image):
+def apply_local(fields, first, geo, mass, flag, local, edges, want_image, inner=()):
     elems = fields[0].shape[2]
     modes = sum(field.shape[1] for field in fields)
     sums = jax.ShapeDtypeStruct((2, modes, LANES), jnp.float32)
     shapes = [jax.ShapeDtypeStruct(fields[0].shape, jnp.float32), sums] if want_image else [sums]
     parts = 2 if want_image else 1
     return pl.pallas_call(
-        functools.partial(apply_kernel, want_image, len(fields), first),
-        in_specs=vmem(5 + len(fields)),
+        functools.partial(apply_kernel, want_image, len(fields), first, len(inner)),
+        in_specs=vmem(5 + len(fields) + len(inner)),
         out_specs=vmem(len(shapes)),
         out_shape=shapes,
         scratch_shapes=[
@@ -633,7 +661,7 @@
         ],
         compiler_params=pltpu.CompilerParams(vmem_limit_bytes=16 * MIB),
         cost_estimate=small_cost(),
-    )(*fields, geo, mass, flag, local, edges)
+    )(*fields, *inner, geo, mass, flag, local, edges)
 
 
 def ends_of(node, field_refs, lane):
@@ -739,7 +767,7 @@
 
 def finish_kernel(count, chunks, *refs):
     fields, refs = refs[: 2 * chunks], refs[2 * chunks :]
-    sum_refs, out_ref = refs[:count], refs[count]
+    sum_refs, (out_ref, buffer_ref, sems) = refs[:count], refs[count:]
     total = sum_refs[0][...]
     for ref in sum_refs[1:]:
         total = total + ref[...]
@@ -751,29 +779,48 @@
     second = norm / (energy - beta * (norm / alpha))
     on_r = jnp.broadcast_to(alpha + second * (1.0 + beta), total.shape)
     on_q = jnp.broadcast_to(second * alpha, total.shape)
-    start = 0
+    elems = out_ref.shape[2]
+    slots = buffer_ref.shape[0]
+    tiles = total.shape[0] // 8
+
+    def copy(tile):
+        target = out_ref.at[pl.ds(8 * tile, 8)]
+        return pltpu.make_async_copy(buffer_ref.at[tile % slots], target, sems.at[tile % slots])
+
+    tile = 0
     for chunk in range(chunks):
         r0_ref, q0_ref = fields[2 * chunk : 2 * chunk + 2]
-        mine = slice(start, start + r0_ref.shape[1])
-        start = mine.stop
-        for j in range(8):
-            rows = slice(8 * j, 8 * j + 8)
-            value = on_r[mine] * r0_ref[rows] - on_q[mine] * q0_ref[rows]
-            out_ref[mine, rows, :] = jnp.swapaxes(value, 0, 1)
+        for first in range(0, r0_ref.shape[1], 8):
+            if tile >= slots:
+                copy(tile - slots).wait()
+            mine = slice(8 * tile, 8 * tile + 8)
+            rows = slice(first, first + 8)
+            on_r0, on_q0 = on_r[mine], on_q[mine]
+            for block in range(elems // LANES):
+                lanes = slice(block * LANES, (block + 1) * LANES)
+                for j in range(8):
+                    nodes = slice(8 * j, 8 * j + 8)
+                    value = on_r0 * r0_ref[nodes, rows, lanes] - on_q0 * q0_ref[nodes, rows, lanes]
+                    buffer_ref[tile % slots, :, nodes, lanes] = jnp.swapaxes(value, 0, 1)
+            copy(tile).start()
+            tile += 1
+    for left in range(max(tiles - slots, 0), tiles):
+        copy(left).wait()
 
 
 def finish(fields, sums):
     elems = fields[0].shape[2]
-    chunks = len(fields) // 2
     total = sums[0].shape[0]
-    blocks = [pl.BlockSpec((64, field.shape[1], LANES), lambda b: (0, 0, b)) for field in fields]
-    small = pl.BlockSpec((total, LANES), lambda b: (0, 0))
+    slots = min(4, total // 8)
     return pl.pallas_call(
-        functools.partial(finish_kernel, len(sums), chunks),
-        grid=(elems // LANES,),
-        in_specs=blocks + [small] * len(sums),
-        out_specs=pl.BlockSpec((total, 64, LANES), lambda b: (0, 0, b)),
+        functools.partial(finish_kernel, len(sums), len(fields) // 2),
+        in_specs=vmem(len(fields) + len(sums)),
+        out_specs=pl.BlockSpec(memory_space=pl.ANY),
         out_shape=jax.ShapeDtypeStruct((total, 64, elems), jnp.float32),
+        scratch_shapes=[
+            pltpu.VMEM((slots, 8, 64, elems), jnp.float32),
+            pltpu.SemaphoreType.DMA((slots,)),
+        ],
         compiler_params=pltpu.CompilerParams(vmem_limit_bytes=16 * MIB),
     )(*fields, *sums)
 
@@ -843,9 +890,11 @@
     )
     flag = jnp.broadcast_to(wall_flags.astype(jnp.float32)[:, None], (planes, LANES))
     tables = edge_tables(nbr_elem, nbr_edge)
-    near_sent = pack(index, concentration, fold, groups, 0)
-    far_sent = list(pack(index, concentration, fold, groups, groups // 2))
     half = groups // 2
+    far_sent = list(pack(index, concentration, fold, groups, half, fold.parts))
+    more = half - fold.parts
+    far_sent += pack(index, concentration, fold, groups, half + fold.parts, more) if more else []
+    near_sent = pack(index, concentration, fold, groups, 0, half)
     near_field = exchanged(near_sent)
     near_field[2], far_sent[-1] = lax.optimization_barrier((near_field[2], far_sent[-1]))
     far_field = exchanged(far_sent, half)
@@ -862,7 +911,7 @@
     )
     far_parts = [exchanged(piece, groups // 2) for piece in sent]
     near_parts = exchanged(near_modes(index, mine, tables, near, far_terms, fold, planes))
-    fields, images, sums, sends = [], [], [], []
+    fields, images, sums, sends, inner = [], [], [], [], []
     start = 0
     for piece, size in enumerate(sizes):
         parts = near_parts + far_parts[piece]
@@ -870,13 +919,15 @@
         sends = [send]
         image, more = apply_local([field], start, geo, mass, flag, local, edges, True)
         start += size
-        mask, more = lax.optimization_barrier((mask, more))
+        if piece + 1 < len(sizes):
+            inner = [inner_sums(image, geo, mass)]
+            mask, inner = lax.optimization_barrier((mask, inner))
         fields.append(field)
         images.append(image)
         sums.append(more)
     halo = both_sides(sends[0])
     *images, send, sums = first_far(images, fields, halo, far, edges, mask, sums)
-    (more,) = apply_local(images, 0, geo, mass, flag, local, edges, False)
+    (more,) = apply_local(images, 0, geo, mass, flag, local, edges, False, inner)
     packed = second_far(images, both_sides(send), far, edges, sums, more)
     size = lax.axis_size("xy")
     pairs = [value for pair in zip(fields, images) for value in pair]

time: 218 us -> 214 us (0.982)
  waiting for transfers between devices: 140 us -> 136 us
    ppermute x18, waiting for transfers between devices: 136 us -> 132 us  [exchanged(): lax.ppermute(value, 'gz', [(i, i ^ d) for i in range(size)])]
    pallas_call x2 -> x3, Pallas kernels: 6.86 us -> 8.59 us  [pack(): pl.pallas_call(functools.partial(pack_kernel, fold), grid_spec=pltpu.Pref...]
    pallas_call x1 -> x2, Pallas kernels: 4.63 us -> 4.19 us  [the longest x1 2.63 us: finish(): pl.pallas_call(functools.partial(finish_kernel, len(sums), len(fields) //...]
  transfers between devices with their start and end apart: 25 -> 25, of which waited for: 16 -> 16; matrix products, arithmetic and copies ran while one was open for 4% -> 4% of each run, Pallas kernels for 15% -> 16%
where the time goes in v6:
time: 214 us
  waiting for transfers between devices  136 us (64%)
  Pallas kernels  44.7 us (21%)
  starting transfers between devices  25.2 us (12%)
  other arithmetic  7.66 us (4%)
    ppermute x18, waiting for transfers between devices, exchanged(): lax.ppermute(value, 'gz', [(i, i ^ d) for i in range(size)])  132 us
    ppermute x18, starting transfers between devices, exchanged(): lax.ppermute(value, 'gz', [(i, i ^ d) for i in range(size)])  19.7 us
    pallas_call x3, Pallas kernels, apply_local(): pl.pallas_call(functools.partial(apply_kernel, want_image, len(fields), f...  14.7 us
    pallas_call x2, Pallas kernels, some_terms(): pl.pallas_call(functools.partial(terms_kernel, fold, first, count), in_sp...  9.33 us
    pallas_call x3, Pallas kernels, pack(): pl.pallas_call(functools.partial(pack_kernel, fold), grid_spec=pltpu.Pref...  8.59 us
    convert_element_type x1, other arithmetic, edge_tables(): local = (source == place[None, :]).astype(jnp.bfloat16)  7.47 us
    ppermute x7, starting transfers between devices, shifted(): lax.ppermute(value, axis, [(i, (i + steps) % size) for i in range(size)])  5.53 us
  transfers between devices with their start and end apart: 25, of which 16 were waited for; matrix products, arithmetic and copies ran while one was open for 4% of the time, Pallas kernels for 16%

profile of v6, /device:TPU:8, one launch (start us, length us, event | category | flops | bytes accessed | tf_op | source)
XLA Modules:
  0.0 214.0 jit_solution(7947718225690414993)
XLA Ops:
  0.0 2.6 %shard_map.67 = (f32[32,32,128]{2,1,0:T(8,128)}, f32[32,32,128]{2,1,0:T(8,128)}) custom-call(s32[1]{0:T(128)} %bitcast.me_ref, f32[32,64,512]{2,1,0:T(8,128)} %c_ref.5), custom_call_target="tpu_custom_call" | custom-call | flops 1048576 | bytes 4194304 | tf_op jit(solution)/shard_map/pallas_call | solution.py:199
  2.6 2.6 %collective-permute-start.3 = (f32[32,32,128]{2,1,0:T(8,128)}, f32[32,32,128]{2,1,0:T(8,128)S(1)}, u32[]{:S(2)}, u32[]{:S(2)}) collective-permute-start(f32[32,32,128]{2,1,0:T(8,128)} %get-tuple-element.66), channel_id=1, source_target_pairs={{0,4},{1,5},{2,6},{3,7},{4,0},{5,1},{6,2},{7,3},{8,12},{9,13},{10,... | collective-permute-start | bytes 1572872 | tf_op jit(solution)/shard_map/ppermute | solution.py:838
  6.5 2.6 %shard_map.65 = (f32[32,32,128]{2,1,0:T(8,128)}, f32[32,32,128]{2,1,0:T(8,128)}) custom-call(s32[1]{0:T(128)} %bitcast.me_ref, f32[32,64,512]{2,1,0:T(8,128)} %c_ref.5), custom_call_target="tpu_custom_call" | custom-call | flops 1048576 | bytes 4194304 | tf_op jit(solution)/shard_map/pallas_call | solution.py:199
  10.7 3.4 %shard_map.64 = (f32[32,32,128]{2,1,0:T(8,128)}, f32[32,32,128]{2,1,0:T(8,128)}, f32[32,32,128]{2,1,0:T(8,128)}, f32[32,32,128]{2,1,0:T(8,128)}) custom-call(s32[1]{0:T(128)} %bitcast.me_ref, f32[32,64,512]{2,1,0:T(8,128)} %c_ref.5), custom_call_target="tpu_custom_call" | custom-call | flops 1048576 | bytes 4194304 | tf_op jit(solution)/shard_map/pallas_call | solution.py:199
  14.6 2.5 %collective-permute-start.1 = (f32[32,32,128]{2,1,0:T(8,128)}, f32[32,32,128]{2,1,0:T(8,128)S(1)}, u32[]{:S(2)}, u32[]{:S(2)}) collective-permute-start(f32[32,32,128]{2,1,0:T(8,128)} %get-tuple-element.56), channel_id=1, source_target_pairs={{0,2},{1,3},{2,0},{3,1},{4,6},{5,7},{6,4},{7,5},{8,10},{9,11},{10,... | collective-permute-start | bytes 1572872 | tf_op jit(solution)/shard_map/ppermute | solution.py:838
  17.3 7.5 %fusion.refs_4_.refs_6_ = bf16[2048,2048]{1,0:T(8,128)(2,1)} fusion(s32[2048]{0:T(1024)S(1)} %bitcast.20), kind=kLoop, calls=%fused_computation.1 | loop fusion | flops 8388608 | bytes 8396800 | tf_op jit(solution)/shard_map/convert_element_type | solution.py:861
  25.1 26.2 %collective-permute-done.1.refs_2_ = f32[32,32,128]{2,1,0:T(8,128)S(1)} collective-permute-done((f32[32,32,128]{2,1,0:T(8,128)}, f32[32,32,128]{2,1,0:T(8,128)S(1)}, u32[]{:S(2)}, u32[]{:S(2)}) %collective-permute-start.1) | collective-permute-done | bytes 524320 | tf_op jit(solution)/shard_map/ppermute | solution.py:838
  52.7 30.1 %collective-permute-done.2.refs_3_ = f32[32,32,128]{2,1,0:T(8,128)S(1)} collective-permute-done((f32[32,32,128]{2,1,0:T(8,128)}, f32[32,32,128]{2,1,0:T(8,128)S(1)}, u32[]{:S(2)}, u32[]{:S(2)}) %collective-permute-start.2) | collective-permute-done | bytes 524320 | tf_op jit(solution)/shard_map/ppermute | solution.py:838
  84.6 4.0 %shard_map.68.given_ref = bf16[16,512,256]{2,1,0:T(8,128)(2,1)S(1)} custom-call(s32[1]{0:T(128)} %bitcast.me_ref, f32[8,128]{1,0:T(8,128)S(1)} %tile.10.geo_ref, f32[32,32,128]{2,1,0:T(8,128)S(1)} %collective-permute-done.3.refs_0_, f32[32,32,128]{2,1,0:T(8,128)S(1)} %collective-permute-done.4.refs_1_, f32[32,32,128]{2,1,0:T(8,128)S(1)} %collective-permute-done.5.refs_2_), custom_call_target="tpu_custom_call" | custom-call | flops 31457280 | bytes 4718592 | tf_op jit(solution)/shard_map/pallas_call | solution.py:340
  88.6 5.3 %shard_map.66.near_ref = bf16[16,512,256]{2,1,0:T(8,128)(2,1)S(1)} custom-call(s32[1]{0:T(128)} %bitcast.me_ref, f32[8,128]{1,0:T(8,128)S(1)} %tile.10.geo_ref, f32[32,32,128]{2,1,0:T(8,128)S(1)} %copy-done.1, f32[32,32,128]{2,1,0:T(8,128)S(1)} %collective-permute-done.refs_1_, f32[32,32,128]{2,1,0:T(8,128)S(1)} %collective-permute-done.1.refs_2_, ...), custom_call_target="tpu_custom_call" | custom-call | flops 41943040 | bytes 6291456 | tf_op jit(solution)/shard_map/pallas_call | solution.py:340
  94.0 2.0 collective-permute-done.6.y_ref
  96.0 3.5 %shard_map.69 = (f32[32,24,128]{2,1,0:T(8,128)S(1)}, f32[32,8,128]{2,1,0:T(8,128)S(1)}, f32[32,24,128]{2,1,0:T(8,128)S(1)}, f32[32,8,128]{2,1,0:T(8,128)S(1)}, f...) custom-call(s32[1]{0:T(128)} %bitcast.me_ref, ...), custom_call_target="tpu_custom_call", output_to_operand_aliasing={{8}: (4, {})} | custom-call | flops 805306368 | bytes 4194304 | tf_op jit(solution)/shard_map/pallas_call | solution.py:370
  102.7 2.0 shard_map.70
  108.2 19.5 %collective-permute-done.10.refs_4_ = f32[32,24,128]{2,1,0:T(8,128)S(1)} collective-permute-done((f32[32,24,128]{2,1,0:T(8,128)S(1)}, f32[32,24,128]{2,1,0:T(8,128)S(1)}, u32[]{:S(2)}, u32[]{:S(2)}) %collective-permute-start.10) | collective-permute-done | bytes 393248 | tf_op jit(solution)/shard_map/ppermute | solution.py:838
  127.7 8.4 %collective-permute-done.11.refs_5_ = f32[32,24,128]{2,1,0:T(8,128)S(1)} collective-permute-done((f32[32,24,128]{2,1,0:T(8,128)S(1)}, f32[32,24,128]{2,1,0:T(8,128)S(1)}, u32[]{:S(2)}, u32[]{:S(2)}) %collective-permute-start.11) | collective-permute-done | bytes 393248 | tf_op jit(solution)/shard_map/ppermute | solution.py:838
  136.6 24.8 %collective-permute-done.12.refs_6_ = f32[32,24,128]{2,1,0:T(8,128)S(1)} collective-permute-done((f32[32,24,128]{2,1,0:T(8,128)S(1)}, f32[32,24,128]{2,1,0:T(8,128)S(1)}, u32[]{:S(2)}, u32[]{:S(2)}) %collective-permute-start.12) | collective-permute-done | bytes 393248 | tf_op jit(solution)/shard_map/ppermute | solution.py:838
  161.4 12.2 %collective-permute-done.13.refs_7_ = f32[32,24,128]{2,1,0:T(8,128)S(1)} collective-permute-done((f32[32,24,128]{2,1,0:T(8,128)S(1)}, f32[32,24,128]{2,1,0:T(8,128)S(1)}, u32[]{:S(2)}, u32[]{:S(2)}) %collective-permute-start.13) | collective-permute-done | bytes 393248 | tf_op jit(solution)/shard_map/ppermute | solution.py:838
  177.3 7.0 %shard_map.72 = (f32[64,24,512]{2,1,0:T(8,128)S(1)}, f32[2,24,128]{2,1,0:T(8,128)S(1)}) custom-call(f32[64,24,512]{2,1,0:T(8,128)S(1)} %get-tuple-element.79.refs_0_.refs_2_, f32[8,512]{1,0:T(8,128)S(1)} %select_maximum_fusion.refs_1_.geo_ref.refs_3_, f32[32,128]{1,0:T(8,128)S(1)} %broadcast_in_dim.25.refs_2_.mass_ref.refs_4_, ...), custom_call_target="tpu_custom_call" | custom-call | flops 1 | bytes 1 | tf_op jit(solution)/shard_map/pallas_call | solution.py:652
  186.7 4.1 %collective-permute-done.16.refs_6_ = f32[32,8,128]{2,1,0:T(8,128)S(1)} collective-permute-done((f32[32,8,128]{2,1,0:T(8,128)S(1)}, f32[32,8,128]{2,1,0:T(8,128)S(1)}, u32[]{:S(2)}, u32[]{:S(2)}) %collective-permute-start.16) | collective-permute-done | bytes 131104 | tf_op jit(solution)/shard_map/ppermute | solution.py:838
  190.8 2.1 collective-permute-done.17.refs_7_
  195.1 2.5 %shard_map.75 = (f32[64,8,512]{2,1,0:T(8,128)S(1)}, f32[2,8,128]{2,1,0:T(8,128)S(1)}) custom-call(f32[64,8,512]{2,1,0:T(8,128)S(1)} %get-tuple-element.92.refs_0_.refs_3_.refs_2_, f32[8,512]{1,0:T(8,128)S(1)} %select_maximum_fusion.refs_1_.geo_ref.refs_3_, f32[32,128]{1,0:T(8,128)S(1)} %broadcast_in_dim.25.refs_2_.mass_ref.refs_4_, ...), custom_call_target="tpu_custom_call" | custom-call | flops 1 | bytes 1 | tf_op jit(solution)/shard_map/pallas_call | solution.py:652
  200.7 5.3 %shard_map.77.refs_7_ = f32[2,32,128]{2,1,0:T(8,128)S(1)} custom-call(f32[64,24,512]{2,1,0:T(8,128)S(1)} %get-tuple-element.98.refs_0_.refs_1_, f32[64,8,512]{2,1,0:T(8,128)S(1)} %get-tuple-element.99.refs_1_.refs_3_, f32[2,24,128]{2,1,0:T(8,128)S(1)} %shard_map.73.refs_2_, f32[8,512]{1,0:T(8,128)S(1)} %select_maximum_fusion.refs_1_.geo_ref.refs_3_, ...), custom_call_target="tpu_custom_call" | custom-call | flops 1 | bytes 1 | tf_op jit(solution)/shard_map/pallas_call | solution.py:652
  208.4 2.3 %collective-permute-done.23.refs_6_ = f32[32,128]{1,0:T(8,128)S(1)} collective-permute-done((f32[32,128]{1,0:T(8,128)S(1)}, f32[32,128]{1,0:T(8,128)S(1)}, u32[]{:S(2)}, u32[]{:S(2)}) %collective-permute-start.23) | collective-permute-done | bytes 16416 | tf_op jit(solution)/shard_map/ppermute | solution.py:830
  211.2 2.6 %shard_map.79 = f32[32,64,512]{2,1,0:T(8,128)} custom-call(f32[64,24,512]{2,1,0:T(8,128)S(1)} %get-tuple-element.79.refs_0_.refs_2_, f32[64,24,512]{2,1,0:T(8,128)S(1)} %get-tuple-element.98.refs_0_.refs_1_, f32[64,8,512]{2,1,0:T(8,128)S(1)} %get-tuple-element.92.refs_0_.refs_3_.refs_2_, f32[64,8,512]{2,1,0:T(8,128)S(1)} %get-tuple-element.99.refs_1_.refs_3_, ...), custom_call_target="tpu_custom_call" | custom-call | tf_op jit(solution)/shard_map/pallas_call | solution.py:815
  (82 shorter events, 28.5 us)
Async XLA Ops:
  2.6 80.3 %collective-permute-start.3 = (f32[32,32,128]{2,1,0:T(8,128)}, f32[32,32,128]{2,1,0:T(8,128)S(1)}, u32[]{:S(2)}, u32[]{:S(2)}) collective-permute-start(f32[32,32,128]{2,1,0:T(8,128)} %get-tuple-element.66), channel_id=1, source_target_pairs={{0,4},{1,5},{2,6},{3,7},{4,0},{5,1},{6,2},{7,3},{8,12},{9,13},{10,... | collective-permute-start | bytes 1572872 | tf_op jit(solution)/shard_map/ppermute | solution.py:838
  5.2 77.8 %collective-permute-start.4 = (f32[32,32,128]{2,1,0:T(8,128)}, f32[32,32,128]{2,1,0:T(8,128)S(1)}, u32[]{:S(2)}, u32[]{:S(2)}) collective-permute-start(f32[32,32,128]{2,1,0:T(8,128)} %get-tuple-element.67), channel_id=1, source_target_pairs={{0,5},{1,4},{2,7},{3,6},{4,1},{5,0},{6,3},{7,2},{8,13},{9,12},{10,... | collective-permute-start | bytes 1572872 | tf_op jit(solution)/shard_map/ppermute | solution.py:838
  9.1 75.5 %collective-permute-start.5 = (f32[32,32,128]{2,1,0:T(8,128)}, f32[32,32,128]{2,1,0:T(8,128)S(1)}, u32[]{:S(2)}, u32[]{:S(2)}) collective-permute-start(f32[32,32,128]{2,1,0:T(8,128)} %get-tuple-element.68), channel_id=1, source_target_pairs={{0,6},{1,7},{2,4},{3,5},{4,2},{5,3},{6,0},{7,1},{8,14},{9,15},{10,... | collective-permute-start | bytes 1572872 | tf_op jit(solution)/shard_map/ppermute | solution.py:838
  14.1 37.8 %collective-permute-start = (f32[32,32,128]{2,1,0:T(8,128)}, f32[32,32,128]{2,1,0:T(8,128)S(1)}, u32[]{:S(2)}, u32[]{:S(2)}) collective-permute-start(f32[32,32,128]{2,1,0:T(8,128)} %get-tuple-element.55), channel_id=1, source_target_pairs={{0,1},{1,0},{2,3},{3,2},{4,5},{5,4},{6,7},{7,6},{8,9},{9,8},{10,11... | collective-permute-start | bytes 1572872 | tf_op jit(solution)/shard_map/ppermute | solution.py:838
  14.6 36.7 %collective-permute-start.1 = (f32[32,32,128]{2,1,0:T(8,128)}, f32[32,32,128]{2,1,0:T(8,128)S(1)}, u32[]{:S(2)}, u32[]{:S(2)}) collective-permute-start(f32[32,32,128]{2,1,0:T(8,128)} %get-tuple-element.56), channel_id=1, source_target_pairs={{0,2},{1,3},{2,0},{3,1},{4,6},{5,7},{6,4},{7,5},{8,10},{9,11},{10,... | collective-permute-start | bytes 1572872 | tf_op jit(solution)/shard_map/ppermute | solution.py:838
  51.3 31.5 %collective-permute-start.2 = (f32[32,32,128]{2,1,0:T(8,128)}, f32[32,32,128]{2,1,0:T(8,128)S(1)}, u32[]{:S(2)}, u32[]{:S(2)}) collective-permute-start(f32[32,32,128]{2,1,0:T(8,128)} %get-tuple-element.59), channel_id=1, source_target_pairs={{0,3},{1,2},{2,1},{3,0},{4,7},{5,6},{6,5},{7,4},{8,11},{9,10},{10,... | collective-permute-start | bytes 1572872 | tf_op jit(solution)/shard_map/ppermute | solution.py:838
  51.9 44.1 %collective-permute-start.6 = (f32[32,32,128]{2,1,0:T(8,128)}, f32[32,32,128]{2,1,0:T(8,128)S(1)}, u32[]{:S(2)}, u32[]{:S(2)}) collective-permute-start(f32[32,32,128]{2,1,0:T(8,128)} %get-tuple-element.69), channel_id=1, source_target_pairs={{0,7},{1,6},{2,5},{3,4},{4,3},{5,2},{6,1},{7,0},{8,15},{9,14},{10,... | collective-permute-start | bytes 1572872 | tf_op jit(solution)/shard_map/ppermute | solution.py:838
  99.5 28.2 %collective-permute-start.10 = (f32[32,24,128]{2,1,0:T(8,128)S(1)}, f32[32,24,128]{2,1,0:T(8,128)S(1)}, u32[]{:S(2)}, u32[]{:S(2)}) collective-permute-start(f32[32,24,128]{2,1,0:T(8,128)S(1)} %get-tuple-element.75), channel_id=1, source_target_pairs={{0,4},{1,5},{2,6},{3,7},{4,0},{5,1},{6,2},{7,3},{8,12},{9,13},{10,... | collective-permute-start | bytes 1179656 | tf_op jit(solution)/shard_map/ppermute | solution.py:838
  101.3 34.8 %collective-permute-start.11 = (f32[32,24,128]{2,1,0:T(8,128)S(1)}, f32[32,24,128]{2,1,0:T(8,128)S(1)}, u32[]{:S(2)}, u32[]{:S(2)}) collective-permute-start(f32[32,24,128]{2,1,0:T(8,128)S(1)} %get-tuple-element.76), channel_id=1, source_target_pairs={{0,5},{1,4},{2,7},{3,6},{4,1},{5,0},{6,3},{7,2},{8,13},{9,12},{10,... | collective-permute-start | bytes 1179656 | tf_op jit(solution)/shard_map/ppermute | solution.py:838
  104.7 68.9 %collective-permute-start.7 = (f32[32,32,128]{2,1,0:T(8,128)S(1)}, f32[32,32,128]{2,1,0:T(8,128)S(1)}, u32[]{:S(2)}, u32[]{:S(2)}) collective-permute-start(f32[32,32,128]{2,1,0:T(8,128)S(1)} %get-tuple-element.72), channel_id=1, source_target_pairs={{0,1},{1,0},{2,3},{3,2},{4,5},{5,4},{6,7},{7,6},{8,9},{9,8},{10,11... | collective-permute-start | bytes 1572872 | tf_op jit(solution)/shard_map/ppermute | solution.py:838
  106.0 69.1 %collective-permute-start.8 = (f32[32,32,128]{2,1,0:T(8,128)S(1)}, f32[32,32,128]{2,1,0:T(8,128)S(1)}, u32[]{:S(2)}, u32[]{:S(2)}) collective-permute-start(f32[32,32,128]{2,1,0:T(8,128)S(1)} %get-tuple-element.73), channel_id=1, source_target_pairs={{0,2},{1,3},{2,0},{3,1},{4,6},{5,7},{6,4},{7,5},{8,10},{9,11},{10,... | collective-permute-start | bytes 1572872 | tf_op jit(solution)/shard_map/ppermute | solution.py:838
  107.2 69.0 %collective-permute-start.9 = (f32[32,32,128]{2,1,0:T(8,128)S(1)}, f32[32,32,128]{2,1,0:T(8,128)S(1)}, u32[]{:S(2)}, u32[]{:S(2)}) collective-permute-start(f32[32,32,128]{2,1,0:T(8,128)S(1)} %get-tuple-element.74), channel_id=1, source_target_pairs={{0,3},{1,2},{2,1},{3,0},{4,7},{5,6},{6,5},{7,4},{8,11},{9,10},{10,... | collective-permute-start | bytes 1572872 | tf_op jit(solution)/shard_map/ppermute | solution.py:838
  127.7 33.7 %collective-permute-start.12 = (f32[32,24,128]{2,1,0:T(8,128)S(1)}, f32[32,24,128]{2,1,0:T(8,128)S(1)}, u32[]{:S(2)}, u32[]{:S(2)}) collective-permute-start(f32[32,24,128]{2,1,0:T(8,128)S(1)} %get-tuple-element.77), channel_id=1, source_target_pairs={{0,6},{1,7},{2,4},{3,5},{4,2},{5,3},{6,0},{7,1},{8,14},{9,15},{10,... | collective-permute-start | bytes 1179656 | tf_op jit(solution)/shard_map/ppermute | solution.py:838
  136.2 37.4 %collective-permute-start.13 = (f32[32,24,128]{2,1,0:T(8,128)S(1)}, f32[32,24,128]{2,1,0:T(8,128)S(1)}, u32[]{:S(2)}, u32[]{:S(2)}) collective-permute-start(f32[32,24,128]{2,1,0:T(8,128)S(1)} %get-tuple-element.78), channel_id=1, source_target_pairs={{0,7},{1,6},{2,5},{3,4},{4,3},{5,2},{6,1},{7,0},{8,15},{9,14},{10,... | collective-permute-start | bytes 1179656 | tf_op jit(solution)/shard_map/ppermute | solution.py:838
  161.4 24.4 %collective-permute-start.14 = (f32[32,8,128]{2,1,0:T(8,128)S(1)}, f32[32,8,128]{2,1,0:T(8,128)S(1)}, u32[]{:S(2)}, u32[]{:S(2)}) collective-permute-start(f32[32,8,128]{2,1,0:T(8,128)S(1)} %get-tuple-element.87), channel_id=1, source_target_pairs={{0,4},{1,5},{2,6},{3,7},{4,0},{5,1},{6,2},{7,3},{8,12},{9,13},{10,... | collective-permute-start | bytes 393224 | tf_op jit(solution)/shard_map/ppermute | solution.py:838
  173.6 13.1 %collective-permute-start.15 = (f32[32,8,128]{2,1,0:T(8,128)S(1)}, f32[32,8,128]{2,1,0:T(8,128)S(1)}, u32[]{:S(2)}, u32[]{:S(2)}) collective-permute-start(f32[32,8,128]{2,1,0:T(8,128)S(1)} %get-tuple-element.88), channel_id=1, source_target_pairs={{0,5},{1,4},{2,7},{3,6},{4,1},{5,0},{6,3},{7,2},{8,13},{9,12},{10,... | collective-permute-start | bytes 393224 | tf_op jit(solution)/shard_map/ppermute | solution.py:838
  173.6 17.2 %collective-permute-start.16 = (f32[32,8,128]{2,1,0:T(8,128)S(1)}, f32[32,8,128]{2,1,0:T(8,128)S(1)}, u32[]{:S(2)}, u32[]{:S(2)}) collective-permute-start(f32[32,8,128]{2,1,0:T(8,128)S(1)} %get-tuple-element.89), channel_id=1, source_target_pairs={{0,6},{1,7},{2,4},{3,5},{4,2},{5,3},{6,0},{7,1},{8,14},{9,15},{10,... | collective-permute-start | bytes 393224 | tf_op jit(solution)/shard_map/ppermute | solution.py:838
  175.1 17.8 %collective-permute-start.17 = (f32[32,8,128]{2,1,0:T(8,128)S(1)}, f32[32,8,128]{2,1,0:T(8,128)S(1)}, u32[]{:S(2)}, u32[]{:S(2)}) collective-permute-start(f32[32,8,128]{2,1,0:T(8,128)S(1)} %get-tuple-element.90), channel_id=1, source_target_pairs={{0,7},{1,6},{2,5},{3,4},{4,3},{5,2},{6,1},{7,0},{8,15},{9,14},{10,... | collective-permute-start | bytes 393224 | tf_op jit(solution)/shard_map/ppermute | solution.py:838
  193.3 4.4 %collective-permute-start.19 = (f32[8,32,128]{2,1,0:T(8,128)S(1)}, f32[8,32,128]{2,1,0:T(8,128)S(1)}, u32[]{:S(2)}, u32[]{:S(2)}) collective-permute-start(f32[8,32,128]{2,1,0:T(8,128)S(1)} %get-tuple-element.96), channel_id=1, source_target_pairs={{0,8},{8,16},{16,24},{24,0},{1,9},{9,17},{17,25},{25,1},{2,10},{10... | collective-permute-start | bytes 393224 | tf_op jit(solution)/shard_map/ppermute | solution.py:830
  193.4 4.8 %collective-permute-start.18 = (f32[8,32,128]{2,1,0:T(8,128)S(1)}, f32[8,32,128]{2,1,0:T(8,128)S(1)}, u32[]{:S(2)}, u32[]{:S(2)}) collective-permute-start(f32[8,32,128]{2,1,0:T(8,128)S(1)} %get-tuple-element.96), channel_id=1, source_target_pairs={{0,24},{8,0},{16,8},{24,16},{1,25},{9,1},{17,9},{25,17},{2,26},{10... | collective-permute-start | bytes 393224 | tf_op jit(solution)/shard_map/ppermute | solution.py:830
  198.7 7.3 %collective-permute-start.21 = (f32[8,32,128]{2,1,0:T(8,128)S(1)}, f32[8,32,128]{2,1,0:T(8,128)S(1)}, u32[]{:S(2)}, u32[]{:S(2)}) collective-permute-start(f32[8,32,128]{2,1,0:T(8,128)S(1)} %get-tuple-element.100), channel_id=1, source_target_pairs={{0,8},{8,16},{16,24},{24,0},{1,9},{9,17},{17,25},{25,1},{2,10},{10... | collective-permute-start | bytes 393224 | tf_op jit(solution)/shard_map/ppermute | solution.py:830
  200.0 6.1 %collective-permute-start.20 = (f32[8,32,128]{2,1,0:T(8,128)S(1)}, f32[8,32,128]{2,1,0:T(8,128)S(1)}, u32[]{:S(2)}, u32[]{:S(2)}) collective-permute-start(f32[8,32,128]{2,1,0:T(8,128)S(1)} %get-tuple-element.100), channel_id=1, source_target_pairs={{0,24},{8,0},{16,8},{24,16},{1,25},{9,1},{17,9},{25,17},{2,26},{10... | collective-permute-start | bytes 393224 | tf_op jit(solution)/shard_map/ppermute | solution.py:830
  206.9 3.7 %collective-permute-start.23 = (f32[32,128]{1,0:T(8,128)S(1)}, f32[32,128]{1,0:T(8,128)S(1)}, u32[]{:S(2)}, u32[]{:S(2)}) collective-permute-start(f32[32,128]{1,0:T(8,128)S(1)} %shard_map.78.refs_4_), channel_id=1, source_target_pairs={{0,16},{8,24},{16,0},{24,8},{1,17},{9,25},{17,1},{25,9},{2,18},{10... | collective-permute-start | bytes 49160 | tf_op jit(solution)/shard_map/ppermute | solution.py:830
  208.0 3.2 %collective-permute-start.22 = (f32[32,128]{1,0:T(8,128)S(1)}, f32[32,128]{1,0:T(8,128)S(1)}, u32[]{:S(2)}, u32[]{:S(2)}) collective-permute-start(f32[32,128]{1,0:T(8,128)S(1)} %shard_map.78.refs_4_), channel_id=1, source_target_pairs={{0,8},{8,16},{16,24},{24,0},{1,9},{9,17},{17,25},{25,1},{2,10},{10... | collective-permute-start | bytes 49160 | tf_op jit(solution)/shard_map/ppermute | solution.py:830
  (9 other events, 276.9 us)

commit v7 on v6

--- a/solution.py
+++ b/solution.py
@@ -140,15 +140,20 @@
     return out
 
 
-def derivative_line(matrix, values, back, swap):
-    if swap is None:
+def derivative_line(matrix, values, mirror):
+    if mirror is None:
         return line_apply(matrix, values, -1)
-    other = [swap(v) for v in values]
-    sign = -1.0 if back else 1.0
+    swap, sign, first = mirror
+    mixed = [swap(v) + v * sign for v in values]
     out = []
     for a in range(4):
-        coefs = [matrix[a, b] for b in range(4)] + [sign * matrix[a, 7 - b] for b in range(4)]
-        out.append(combine(coefs, list(values) + other))
+        total = None
+        for b in range(4):
+            upper = np.float32((matrix[a, b] + matrix[a, 7 - b]) / 2)
+            lower = np.float32((matrix[a, b] - matrix[a, 7 - b]) / 2)
+            term = mixed[b] * jnp.where(first, upper, lower)
+            total = term if total is None else total + term
+        out.append(total + swap(total) * sign)
     return out
 
 
@@ -217,40 +222,37 @@
     square_x = jnp.broadcast_to(geo_ref[1:2, :], (16, LANES))
     square_y = jnp.broadcast_to(geo_ref[2:3, :], (16, LANES))
 
-    def conc(jp, ip):
-        return y_ref[fold.slot(jp, ip), pl.ds(base, 16), :]
-
-    def potential(c):
-        square = c * c
-        return square * c - c, jnp.maximum(1.0 - square, mobility_floor)
-
-    def flux(fields, swap):
-        pairs = [potential(c) for c in fields]
-        slope = derivative_line(DERIV, [p[0] for p in pairs], False, swap)
-        scaled = [s * p[1] for s, p in zip(slope, pairs)]
-        return derivative_line(BACK_SCALED, scaled, True, swap), pairs
-
-    swap_i = None
-    if fold.fold_i == 2:
-        swap_i = lambda v: mirrored(v, lane, fold.width)
-    swap_j = None
-    if fold.fold_j == 2:
-        swap_j = lambda v: mirrored(v, lane, fold.width * fold.fold_i)
+    def mirror(shift):
+        first = (lane & shift) == 0
+        return (lambda v: mirrored(v, lane, shift), jnp.where(first, 1.0, -1.0), first)
+
+    mirror_i = mirror(fold.width) if fold.fold_i == 2 else None
+    mirror_j = mirror(fold.width * fold.fold_i) if fold.fold_j == 2 else None
     for jp in range(fold.count_j):
-        fields = [conc(jp, ip) for ip in range(fold.count_i)]
-        result, _unused = flux(fields, swap_i)
+        chem, mobility = [], []
         for ip in range(fold.count_i):
-            acc_ref[fold.slot(jp, ip)] = (
-                fields[ip] * np.float32(1.0 / time_step) - result[ip] * square_x
-            )
+            slot = fold.slot(jp, ip)
+            c = y_ref[slot, pl.ds(base, 16), :]
+            square = c * c
+            chem.append(square * c - c)
+            mobility.append(jnp.maximum(1.0 - square, mobility_floor))
+            acc_ref[0, slot] = c * np.float32(1.0 / time_step)
+            acc_ref[1, slot] = chem[ip]
+            acc_ref[2, slot] = mobility[ip]
+        slope = derivative_line(DERIV, chem, mirror_i)
+        result = derivative_line(BACK_SCALED, [s * m for s, m in zip(slope, mobility)], mirror_i)
+        for ip in range(fold.count_i):
+            acc_ref[0, fold.slot(jp, ip)] -= result[ip] * square_x
     for ip in range(fold.count_i):
-        fields = [conc(jp, ip) for jp in range(fold.count_j)]
-        result, pairs = flux(fields, swap_j)
-        for jp in range(fold.count_j):
-            slot = fold.slot(jp, ip)
-            explicit = acc_ref[slot] - result[jp] * square_y
+        slots = [fold.slot(jp, ip) for jp in range(fold.count_j)]
+        chem = [acc_ref[1, slot] for slot in slots]
+        slope = derivative_line(DERIV, chem, mirror_j)
+        scaled = [s * acc_ref[2, slot] for s, slot in zip(slope, slots)]
+        result = derivative_line(BACK_SCALED, scaled, mirror_j)
+        for jp, slot in enumerate(slots):
+            explicit = acc_ref[0, slot] - result[jp] * square_y
             where = pl.ds((slot % 2) * LANES, LANES)
-            for kind, value in enumerate((explicit, pairs[jp][0])):
+            for kind, value in enumerate((explicit, chem[jp])):
                 upper, lower = split(value)
                 x_ref[slot // 2, pl.ds(kind * half + row, 16), where] = upper
                 x_ref[slot // 2, pl.ds((2 + kind) * half + row, 16), where] = lower
@@ -271,54 +273,73 @@
         lax.fori_loop(0, planes // 16, chunk, 0)
 
 
-def terms_kernel(fold, first, count, me_ref, geo_ref, *refs):
+def terms_kernel(fold, first, count, clear, me_ref, geo_ref, *refs):
     y_refs, (x_ref, acc_ref) = refs[:-2], refs[-2:]
-    slot_terms(fold, me_ref[0], first, count, y_refs, geo_ref, x_ref, acc_ref)
-
-
-def far_kernel(fold, count, sizes, me_ref, geo_ref, table_ref, near_ref, given_ref, y_ref, *refs):
+    me = me_ref[0]
+    if clear:
+        planes = y_refs[0].shape[1]
+        place = (me ^ (2 * count - 1)) % count
+        for kind in range(4):
+            row = pl.multiple_of((kind * count + place) * planes, 16)
+            x_ref[:, pl.ds(row, planes), :] = jnp.zeros(
+                (x_ref.shape[0], planes, 2 * LANES), jnp.bfloat16
+            )
+    slot_terms(fold, me, first, count, y_refs, geo_ref, x_ref, acc_ref)
+
+
+def product(table, data):
+    split_at = data.shape[0]
+    return jnp.dot(table[:, :split_at], data, preferred_element_type=jnp.float32) + jnp.dot(
+        table[:, split_at:], data[: split_at // 2], preferred_element_type=jnp.float32
+    )
+
+
+def rows_of(me, count, planes, other):
+    half = count * planes
+    return pl.ds(pl.multiple_of((me // count ^ other) * half, 16), half)
+
+
+def partial_kernel(count, planes, other, me_ref, table_ref, near_ref, far_ref, out_ref):
+    mine = me_ref[0] // count
+    rows = rows_of(me_ref[0], count, planes, other)
+    for pair in range(near_ref.shape[0]):
+        out_ref[pair] = product(table_ref[mine, rows, :], near_ref[pair]) + product(
+            table_ref[1 - mine, rows, :], far_ref[pair]
+        )
+
+
+def far_kernel(fold, count, sizes, me_ref, geo_ref, last_ref, partial_ref, y_ref, *refs):
     chunks = len(sizes)
     out_refs = [refs[k * chunks : (k + 1) * chunks] for k in range(count)]
     x_ref, acc_ref, result_ref = refs[count * chunks :]
-    slot_terms(fold, me_ref[0], 2 * count - 1, count, [y_ref], geo_ref, x_ref, acc_ref)
-    transform(fold, 1, me_ref, geo_ref, table_ref, (near_ref, x_ref), out_refs, result_ref)
-
-
-def near_modes_kernel(fold, me_ref, geo_ref, table_ref, near_ref, far_ref, *refs):
+    slot_terms(fold, me_ref[0], 0, 1, [y_ref], geo_ref, x_ref, acc_ref)
+    transform(fold, 1, me_ref, geo_ref, last_ref, partial_ref, x_ref, out_refs, result_ref)
+
+
+def near_modes_kernel(fold, me_ref, geo_ref, last_ref, partial_ref, x_ref, *refs):
     out_refs, result_ref = [[ref] for ref in refs[:-1]], refs[-1]
-    transform(fold, 0, me_ref, geo_ref, table_ref, (near_ref, far_ref), out_refs, result_ref)
-
-
-def transform(fold, other, me_ref, geo_ref, table_ref, terms, out_refs, result_ref):
+    transform(fold, 0, me_ref, geo_ref, last_ref, partial_ref, x_ref, out_refs, result_ref)
+
+
+def transform(fold, other, me_ref, geo_ref, last_ref, partial_ref, x_ref, out_refs, result_ref):
     count = len(out_refs)
-    half = result_ref.shape[0]
-    planes = half // count
+    planes = result_ref.shape[0] // count
     me = me_ref[0]
-    mine = me // count
     jac = jnp.broadcast_to(geo_ref[0:1, :], (planes, LANES))
-    rows = pl.ds(pl.multiple_of((mine ^ other) * half, 16), half)
-
-    def product(which, data):
-        upper, lower = slice(0, 4 * half), slice(4 * half, 6 * half)
-        return jnp.dot(
-            table_ref[which, rows, upper], data, preferred_element_type=jnp.float32
-        ) + jnp.dot(
-            table_ref[which, rows, lower], data[: 2 * half], preferred_element_type=jnp.float32
-        )
-
+    table = last_ref[rows_of(me, count, planes, other), :]
     for pair in range(fold.slots // 2):
-        result_ref[...] = product(mine, terms[0][pair]) + product(1 - mine, terms[1][pair])
+        result_ref[...] = partial_ref[pair] + product(table, x_ref[pair])
         for k in range(2):
             slot = 2 * pair + k
             jp, ip = slot // fold.count_i, slot % fold.count_i
             scale = jac * np.float32(WEIGHTS[jp] * WEIGHTS[ip])
+            lanes = slice(k * LANES, (k + 1) * LANES)
             for number, pieces in enumerate(out_refs):
                 start = (me ^ number) % count * planes
                 for out_ref in pieces:
                     size = out_ref.shape[1]
                     here = pl.ds(pl.multiple_of(start, 8), size)
-                    value = result_ref[here, k * LANES : (k + 1) * LANES]
-                    out_ref[slot] = value * scale[:size]
+                    out_ref[slot] = result_ref[here, lanes] * scale[:size]
                     start = start + size
 
 
@@ -334,17 +355,17 @@
     return [pl.BlockSpec(memory_space=pltpu.VMEM)] * count
 
 
-def some_terms(me, geo, fields, fold, first, count):
+def some_terms(me, geo, fields, fold, first, count, clear=False):
     slots, planes, _ = fields[0].shape
     size = len(fields) * fields[0].size
     return pl.pallas_call(
-        functools.partial(terms_kernel, fold, first, count),
+        functools.partial(terms_kernel, fold, first, count, clear),
         in_specs=[smem()] + vmem(1 + len(fields)),
         out_specs=vmem(1)[0],
         out_shape=jax.ShapeDtypeStruct(
             (slots // 2, 4 * count * planes, 2 * LANES), jnp.bfloat16
         ),
-        scratch_shapes=[pltpu.VMEM((slots, 16, LANES), jnp.float32)],
+        scratch_shapes=[pltpu.VMEM((3, slots, 16, LANES), jnp.float32)],
         compiler_params=pltpu.CompilerParams(vmem_limit_bytes=16 * MIB),
         cost_estimate=pl.CostEstimate(
             flops=80 * size, bytes_accessed=12 * size, transcendentals=0
@@ -352,44 +373,57 @@
     )(me, geo, *fields)
 
 
-def transform_tables(total):
+def transform_tables(total, planes):
     table = fourier_table(total).astype(np.float32).astype(np.float64)
     wave = ((np.arange(total) + 1) // 2).astype(np.float64)
     upper, lower = two_parts(table)
     upper_b, lower_b = two_parts(-axial_mobility * (wave * wave)[:, None] * table)
-    kinds = [upper, upper_b, upper, upper_b, lower, lower_b]
-    halves = np.split(np.stack(kinds), 2, axis=2)
-    return jnp.asarray(np.stack([np.concatenate(list(half), axis=1) for half in halves]))
-
-
-def far_modes(me, geo, tables, near, far, field, fold, count, sizes):
+    kinds = np.stack([upper, upper_b, upper, upper_b, lower, lower_b])
+
+    def cut(pieces):
+        parts = np.split(kinds, pieces, axis=2)
+        return jnp.asarray(np.stack([np.concatenate(list(part), axis=1) for part in parts]))
+
+    return cut(2), cut(total // planes)
+
+
+def partial_modes(me, tables, near, far, count, planes, other):
+    half = count * planes
+    shape = (near.shape[0], half, 2 * LANES)
+    return pl.pallas_call(
+        functools.partial(partial_kernel, count, planes, other),
+        in_specs=[smem()] + vmem(3),
+        out_specs=vmem(1)[0],
+        out_shape=jax.ShapeDtypeStruct(shape, jnp.float32),
+        compiler_params=pltpu.CompilerParams(vmem_limit_bytes=16 * MIB),
+        cost_estimate=small_cost(),
+    )(me, tables, near, far)
+
+
+def far_modes(me, geo, last, partial, field, fold, count, sizes):
     slots, planes, _ = field.shape
-    size = count * field.size
     chunks = len(sizes)
     pieces = [jax.ShapeDtypeStruct((slots, k, LANES), jnp.float32) for k in sizes]
-    *outs, far = pl.pallas_call(
+    *outs, terms = pl.pallas_call(
         functools.partial(far_kernel, fold, count, sizes),
-        in_specs=[smem()] + vmem(5),
+        in_specs=[smem()] + vmem(4),
         out_specs=vmem(chunks * count + 1),
-        input_output_aliases={4: chunks * count},
-        out_shape=pieces * count + [jax.ShapeDtypeStruct(near.shape, jnp.bfloat16)],
+        out_shape=pieces * count
+        + [jax.ShapeDtypeStruct((slots // 2, 4 * planes, 2 * LANES), jnp.bfloat16)],
         scratch_shapes=[
-            pltpu.VMEM((slots, 16, LANES), jnp.float32),
+            pltpu.VMEM((3, slots, 16, LANES), jnp.float32),
             pltpu.VMEM((count * planes, 2 * LANES), jnp.float32),
         ],
-        compiler_params=pltpu.CompilerParams(vmem_limit_bytes=24 * MIB),
+        compiler_params=pltpu.CompilerParams(vmem_limit_bytes=16 * MIB),
         cost_estimate=pl.CostEstimate(
-            flops=12 * count * planes * size, bytes_accessed=8 * size, transcendentals=0
+            flops=80 * field.size, bytes_accessed=8 * field.size, transcendentals=0
         ),
-    )(me, geo, tables, near, far, field)
-    return [outs[k::chunks] for k in range(chunks)], far
-
-
-def near_modes(me, geo, tables, near, far, fold, planes):
-    slots = fold.slots
-    count = near.shape[1] // (4 * planes)
-    size = count * slots * planes * LANES
-    slot = jax.ShapeDtypeStruct((slots, planes, LANES), jnp.float32)
+    )(me, geo, last, partial, field)
+    return [outs[k::chunks] for k in range(chunks)], terms
+
+
+def near_modes(me, geo, last, partial, terms, fold, count, planes):
+    slot = jax.ShapeDtypeStruct((fold.slots, planes, LANES), jnp.float32)
     return pl.pallas_call(
         functools.partial(near_modes_kernel, fold),
         in_specs=[smem()] + vmem(4),
@@ -398,9 +432,9 @@
         scratch_shapes=[pltpu.VMEM((count * planes, 2 * LANES), jnp.float32)],
         compiler_params=pltpu.CompilerParams(vmem_limit_bytes=16 * MIB),
         cost_estimate=pl.CostEstimate(
-            flops=12 * count * planes * size, bytes_accessed=8 * size, transcendentals=0
+            flops=80 * slot.size, bytes_accessed=8 * slot.size, transcendentals=0
         ),
-    )(me, geo, tables, near, far)
+    )(me, geo, last, partial, terms)
 
 
 def edge_send(mask_ref, edge, write):
@@ -550,8 +584,8 @@
             target_ref[pl.ds(row, 2 * total), lanes] = pieces[part]
 
 
-def gathered(trace_ref, table, parts):
-    value = jnp.dot(trace_ref[...], table, preferred_element_type=jnp.float32)
+def gathered(trace, table, parts):
+    value = jnp.dot(trace, table, preferred_element_type=jnp.float32)
     if parts == 2:
         half = value.shape[0] // 2
         value = value[:half] + value[half:]
@@ -568,9 +602,15 @@
 
         fill_pairs(trace_ref, 0, 0, pl.ds(a * elems, elems), value_of, parts)
     for edge in range(4):
-        val_ref[...] = gathered(
-            trace_ref, local_ref[:, edge * elems : (edge + 1) * elems], parts
-        )
+        mine = slice(edge * elems, (edge + 1) * elems)
+        if parts == 2:
+            val_ref[...] = gathered(trace_ref[...], local_ref[:, mine], parts)
+        else:
+            value = gathered(trace_ref[:, mine], local_ref[mine, mine], parts)
+            if edge:
+                left = slice(0, edge * elems)
+                value = value + 2.0 * gathered(trace_ref[:, left], local_ref[left, mine], parts)
+            val_ref[...] = value
         for block in range(elems // LANES):
             lanes = pl.ds(block * LANES, LANES)
             wall = edges_ref[8 * edge : 8 * edge + 1, lanes]
@@ -599,7 +639,7 @@
 
     fill_pairs(trace_ref, 0, modes, pl.ds(0, LANES), value_of, 2)
     for edge in range(4):
-        values = gathered(trace_ref, far_ref[:, edge * LANES : (edge + 1) * LANES], 2)
+        values = gathered(trace_ref[...], far_ref[:, edge * LANES : (edge + 1) * LANES], 2)
         flips = edges_ref[8 * edge + 1 : 8 * edge + 2, :]
         flip = jnp.where(lane < ROWS, flips[:, :LANES], flips[:, elems - LANES :])
         for t in range(8):
@@ -898,19 +938,20 @@
     near_field = exchanged(near_sent)
     near_field[2], far_sent[-1] = lax.optimization_barrier((near_field[2], far_sent[-1]))
     far_field = exchanged(far_sent, half)
-    near_field, geo, mine, mass, flag, tables = lax.optimization_barrier(
-        (near_field, geo, mine, mass, flag, tables)
+    halves, pieces = transform_tables(planes * groups, planes)
+    last = lax.dynamic_index_in_dim(pieces, me ^ (groups - 1), 0, keepdims=False)
+    near_field, geo, mine, mass, flag, tables, last = lax.optimization_barrier(
+        (near_field, geo, mine, mass, flag, tables, last)
     )
     local, far, mask, edges = tables
     near = some_terms(index, mine, near_field, fold, 0, half)
-    far_terms = some_terms(index, mine, far_field[:-1], fold, half, half)
+    far_terms = some_terms(index, mine, far_field[:-1], fold, half, half, clear=True)
     sizes = [planes - 8, 8] if planes > 16 else [planes]
-    tables = transform_tables(planes * groups)
-    sent, far_terms = far_modes(
-        index, mine, tables, near, far_terms, far_field[-1], fold, half, sizes
-    )
-    far_parts = [exchanged(piece, groups // 2) for piece in sent]
-    near_parts = exchanged(near_modes(index, mine, tables, near, far_terms, fold, planes))
+    partial = partial_modes(index, halves, near, far_terms, half, planes, 1)
+    sent, terms = far_modes(index, mine, last, partial, far_field[-1], fold, half, sizes)
+    far_parts = [exchanged(piece, half) for piece in sent]
+    partial = partial_modes(index, halves, near, far_terms, half, planes, 0)
+    near_parts = exchanged(near_modes(index, mine, last, partial, terms, fold, half, planes))
     fields, images, sums, sends, inner = [], [], [], [], []
     start = 0
     for piece, size in enumerate(sizes):

time: 214 us -> 213 us (level)
  waiting for transfers between devices: 136 us -> 133 us
    ppermute x18, waiting for transfers between devices: 132 us -> 129 us  [exchanged(): lax.ppermute(value, 'gz', [(i, i ^ d) for i in range(size)])]
    pallas_call x2 -> x4, Pallas kernels: 9.33 us -> 12.1 us  [the longest x2 8.52 us: some_terms(): pl.pallas_call(functools.partial(terms_kernel, fold, first, count, clear)...]
  transfers between devices with their start and end apart: 25 -> 25, of which waited for: 16 -> 16; matrix products, arithmetic and copies ran while one was open for 4% -> 4% of each run, Pallas kernels for 16% -> 17%
where the time goes in v7:
time: 213 us; the launch traced here: 212 us
  waiting for transfers between devices  133 us (62%)
  Pallas kernels  44.6 us (21%)
  starting transfers between devices  25.7 us (12%)
  other arithmetic  7.66 us (4%)
    ppermute x18, waiting for transfers between devices, exchanged(): lax.ppermute(value, 'gz', [(i, i ^ d) for i in range(size)])  129 us
    ppermute x18, starting transfers between devices, exchanged(): lax.ppermute(value, 'gz', [(i, i ^ d) for i in range(size)])  20.1 us
    pallas_call x3, Pallas kernels, apply_local(): pl.pallas_call(functools.partial(apply_kernel, want_image, len(fields), f...  14.2 us
    pallas_call x3, Pallas kernels, pack(): pl.pallas_call(functools.partial(pack_kernel, fold), grid_spec=pltpu.Pref...  8.59 us
    pallas_call x2, Pallas kernels, some_terms(): pl.pallas_call(functools.partial(terms_kernel, fold, first, count, clear)...  8.52 us
    convert_element_type x1, other arithmetic, edge_tables(): local = (source == place[None, :]).astype(jnp.bfloat16)  7.47 us
    ppermute x7, starting transfers between devices, shifted(): lax.ppermute(value, axis, [(i, (i + steps) % size) for i in range(size)])  5.54 us
  transfers between devices with their start and end apart: 25, of which 16 were waited for; matrix products, arithmetic and copies ran while one was open for 4% of the time, Pallas kernels for 17%

profile of v7, /device:TPU:8, one launch (start us, length us, event | category | flops | bytes accessed | tf_op | source)
XLA Modules:
  0.0 212.3 jit_solution(13341168838564130543)
XLA Ops:
  0.0 2.6 %shard_map.76 = (f32[32,32,128]{2,1,0:T(8,128)}, f32[32,32,128]{2,1,0:T(8,128)}) custom-call(s32[1]{0:T(128)} %bitcast.me_ref, f32[32,64,512]{2,1,0:T(8,128)} %c_ref.5), custom_call_target="tpu_custom_call" | custom-call | flops 1048576 | bytes 4194304 | tf_op jit(solution)/shard_map/pallas_call | solution.py:204
  2.6 2.6 %collective-permute-start.3 = (f32[32,32,128]{2,1,0:T(8,128)}, f32[32,32,128]{2,1,0:T(8,128)S(1)}, u32[]{:S(2)}, u32[]{:S(2)}) collective-permute-start(f32[32,32,128]{2,1,0:T(8,128)} %get-tuple-element.68), channel_id=1, source_target_pairs={{0,4},{1,5},{2,6},{3,7},{4,0},{5,1},{6,2},{7,3},{8,12},{9,13},{10,... | collective-permute-start | bytes 1572872 | tf_op jit(solution)/shard_map/ppermute | solution.py:878
  6.5 2.6 %shard_map.74 = (f32[32,32,128]{2,1,0:T(8,128)}, f32[32,32,128]{2,1,0:T(8,128)}) custom-call(s32[1]{0:T(128)} %bitcast.me_ref, f32[32,64,512]{2,1,0:T(8,128)} %c_ref.5), custom_call_target="tpu_custom_call" | custom-call | flops 1048576 | bytes 4194304 | tf_op jit(solution)/shard_map/pallas_call | solution.py:204
  10.7 3.4 %shard_map.73 = (f32[32,32,128]{2,1,0:T(8,128)}, f32[32,32,128]{2,1,0:T(8,128)}, f32[32,32,128]{2,1,0:T(8,128)}, f32[32,32,128]{2,1,0:T(8,128)}) custom-call(s32[1]{0:T(128)} %bitcast.me_ref, f32[32,64,512]{2,1,0:T(8,128)} %c_ref.5), custom_call_target="tpu_custom_call" | custom-call | flops 1048576 | bytes 4194304 | tf_op jit(solution)/shard_map/pallas_call | solution.py:204
  14.6 2.5 %collective-permute-start.1 = (f32[32,32,128]{2,1,0:T(8,128)}, f32[32,32,128]{2,1,0:T(8,128)S(1)}, u32[]{:S(2)}, u32[]{:S(2)}) collective-permute-start(f32[32,32,128]{2,1,0:T(8,128)} %get-tuple-element.57), channel_id=1, source_target_pairs={{0,2},{1,3},{2,0},{3,1},{4,6},{5,7},{6,4},{7,5},{8,10},{9,11},{10,... | collective-permute-start | bytes 1572872 | tf_op jit(solution)/shard_map/ppermute | solution.py:878
  17.5 7.5 %fusion.refs_4_.refs_6_ = bf16[2048,2048]{1,0:T(8,128)(2,1)} fusion(s32[2048]{0:T(1024)S(1)} %bitcast.22), kind=kLoop, calls=%fused_computation.1 | loop fusion | flops 8388608 | bytes 8396800 | tf_op jit(solution)/shard_map/convert_element_type | solution.py:901
  25.1 26.2 %collective-permute-done.1.refs_2_ = f32[32,32,128]{2,1,0:T(8,128)S(1)} collective-permute-done((f32[32,32,128]{2,1,0:T(8,128)}, f32[32,32,128]{2,1,0:T(8,128)S(1)}, u32[]{:S(2)}, u32[]{:S(2)}) %collective-permute-start.1) | collective-permute-done | bytes 524320 | tf_op jit(solution)/shard_map/ppermute | solution.py:878
  53.7 29.1 %collective-permute-done.2.refs_3_ = f32[32,32,128]{2,1,0:T(8,128)S(1)} collective-permute-done((f32[32,32,128]{2,1,0:T(8,128)}, f32[32,32,128]{2,1,0:T(8,128)S(1)}, u32[]{:S(2)}, u32[]{:S(2)}) %collective-permute-start.2) | collective-permute-done | bytes 524320 | tf_op jit(solution)/shard_map/ppermute | solution.py:878
  84.6 3.7 %shard_map.77.far_ref = bf16[16,512,256]{2,1,0:T(8,128)(2,1)S(1)} custom-call(s32[1]{0:T(128)} %bitcast.me_ref, f32[8,128]{1,0:T(8,128)S(1)} %tile.10.geo_ref, f32[32,32,128]{2,1,0:T(8,128)S(1)} %collective-permute-done.3.refs_0_, f32[32,32,128]{2,1,0:T(8,128)S(1)} %collective-permute-done.4.refs_1_, f32[32,32,128]{2,1,0:T(8,128)S(1)} %collective-permute-done.5.refs_2_), custom_call_target="tpu_custom_call" | custom-call | flops 31457280 | bytes 4718592 | tf_op jit(solution)/shard_map/pallas_call | solution.py:361
  88.3 4.8 %shard_map.75.near_ref = bf16[16,512,256]{2,1,0:T(8,128)(2,1)S(1)} custom-call(s32[1]{0:T(128)} %bitcast.me_ref, f32[8,128]{1,0:T(8,128)S(1)} %tile.10.geo_ref, f32[32,32,128]{2,1,0:T(8,128)S(1)} %copy-done.1, f32[32,32,128]{2,1,0:T(8,128)S(1)} %collective-permute-done.refs_1_, f32[32,32,128]{2,1,0:T(8,128)S(1)} %collective-permute-done.1.refs_2_, ...), custom_call_target="tpu_custom_call" | custom-call | flops 41943040 | bytes 6291456 | tf_op jit(solution)/shard_map/pallas_call | solution.py:361
  93.2 1.8 shard_map.79.partial_ref
  96.0 2.2 %shard_map.80 = (f32[32,24,128]{2,1,0:T(8,128)S(1)}, f32[32,8,128]{2,1,0:T(8,128)S(1)}, f32[32,24,128]{2,1,0:T(8,128)S(1)}, f32[32,8,128]{2,1,0:T(8,128)S(1)}, f...) custom-call(s32[1]{0:T(128)} %bitcast.me_ref, ...), custom_call_target="tpu_custom_call" | custom-call | flops 10485760 | bytes 1048576 | tf_op jit(solution)/shard_map/pallas_call | solution.py:407
  98.2 2.8 %collective-permute-start.10 = (f32[32,24,128]{2,1,0:T(8,128)S(1)}, f32[32,24,128]{2,1,0:T(8,128)S(1)}, u32[]{:S(2)}, u32[]{:S(2)}) collective-permute-start(f32[32,24,128]{2,1,0:T(8,128)S(1)} %get-tuple-element.77), channel_id=1, source_target_pairs={{0,4},{1,5},{2,6},{3,7},{4,0},{5,1},{6,2},{7,3},{8,12},{9,13},{10,... | collective-permute-start | bytes 1179656 | tf_op jit(solution)/shard_map/ppermute | solution.py:878
  107.7 19.6 %collective-permute-done.10.refs_4_ = f32[32,24,128]{2,1,0:T(8,128)S(1)} collective-permute-done((f32[32,24,128]{2,1,0:T(8,128)S(1)}, f32[32,24,128]{2,1,0:T(8,128)S(1)}, u32[]{:S(2)}, u32[]{:S(2)}) %collective-permute-start.10) | collective-permute-done | bytes 393248 | tf_op jit(solution)/shard_map/ppermute | solution.py:878
  127.3 8.4 %collective-permute-done.11.refs_5_ = f32[32,24,128]{2,1,0:T(8,128)S(1)} collective-permute-done((f32[32,24,128]{2,1,0:T(8,128)S(1)}, f32[32,24,128]{2,1,0:T(8,128)S(1)}, u32[]{:S(2)}, u32[]{:S(2)}) %collective-permute-start.11) | collective-permute-done | bytes 393248 | tf_op jit(solution)/shard_map/ppermute | solution.py:878
  135.7 25.3 %collective-permute-done.12.refs_6_ = f32[32,24,128]{2,1,0:T(8,128)S(1)} collective-permute-done((f32[32,24,128]{2,1,0:T(8,128)S(1)}, f32[32,24,128]{2,1,0:T(8,128)S(1)}, u32[]{:S(2)}, u32[]{:S(2)}) %collective-permute-start.12) | collective-permute-done | bytes 393248 | tf_op jit(solution)/shard_map/ppermute | solution.py:878
  161.0 11.3 %collective-permute-done.13.refs_7_ = f32[32,24,128]{2,1,0:T(8,128)S(1)} collective-permute-done((f32[32,24,128]{2,1,0:T(8,128)S(1)}, f32[32,24,128]{2,1,0:T(8,128)S(1)}, u32[]{:S(2)}, u32[]{:S(2)}) %collective-permute-start.13) | collective-permute-done | bytes 393248 | tf_op jit(solution)/shard_map/ppermute | solution.py:878
  172.3 2.4 %collective-permute-start.16 = (f32[32,8,128]{2,1,0:T(8,128)S(1)}, f32[32,8,128]{2,1,0:T(8,128)S(1)}, u32[]{:S(2)}, u32[]{:S(2)}) collective-permute-start(f32[32,8,128]{2,1,0:T(8,128)S(1)} %get-tuple-element.91), channel_id=1, source_target_pairs={{0,6},{1,7},{2,4},{3,5},{4,2},{5,3},{6,0},{7,1},{8,14},{9,15},{10,... | collective-permute-start | bytes 393224 | tf_op jit(solution)/shard_map/ppermute | solution.py:878
  176.8 7.1 %shard_map.83 = (f32[64,24,512]{2,1,0:T(8,128)S(1)}, f32[2,24,128]{2,1,0:T(8,128)S(1)}) custom-call(f32[64,24,512]{2,1,0:T(8,128)S(1)} %get-tuple-element.81.refs_0_.refs_2_, f32[8,512]{1,0:T(8,128)S(1)} %select_maximum_fusion.refs_1_.geo_ref.refs_3_, f32[32,128]{1,0:T(8,128)S(1)} %broadcast_in_dim.25.refs_2_.mass_ref.refs_4_, ...), custom_call_target="tpu_custom_call" | custom-call | flops 1 | bytes 1 | tf_op jit(solution)/shard_map/pallas_call | solution.py:692
  186.3 4.0 %collective-permute-done.16.refs_6_ = f32[32,8,128]{2,1,0:T(8,128)S(1)} collective-permute-done((f32[32,8,128]{2,1,0:T(8,128)S(1)}, f32[32,8,128]{2,1,0:T(8,128)S(1)}, u32[]{:S(2)}, u32[]{:S(2)}) %collective-permute-start.16) | collective-permute-done | bytes 131104 | tf_op jit(solution)/shard_map/ppermute | solution.py:878
  194.0 2.5 %shard_map.86 = (f32[64,8,512]{2,1,0:T(8,128)S(1)}, f32[2,8,128]{2,1,0:T(8,128)S(1)}) custom-call(f32[64,8,512]{2,1,0:T(8,128)S(1)} %get-tuple-element.94.refs_0_.refs_3_.refs_2_, f32[8,512]{1,0:T(8,128)S(1)} %select_maximum_fusion.refs_1_.geo_ref.refs_3_, f32[32,128]{1,0:T(8,128)S(1)} %broadcast_in_dim.25.refs_2_.mass_ref.refs_4_, ...), custom_call_target="tpu_custom_call" | custom-call | flops 1 | bytes 1 | tf_op jit(solution)/shard_map/pallas_call | solution.py:692
  199.7 4.7 %shard_map.88.refs_7_ = f32[2,32,128]{2,1,0:T(8,128)S(1)} custom-call(f32[64,24,512]{2,1,0:T(8,128)S(1)} %get-tuple-element.100.refs_0_.refs_1_, f32[64,8,512]{2,1,0:T(8,128)S(1)} %get-tuple-element.101.refs_1_.refs_3_, f32[2,24,128]{2,1,0:T(8,128)S(1)} %shard_map.84.refs_2_, f32[8,512]{1,0:T(8,128)S(1)} %select_maximum_fusion.refs_1_.geo_ref.refs_3_, ...), custom_call_target="tpu_custom_call" | custom-call | flops 1 | bytes 1 | tf_op jit(solution)/shard_map/pallas_call | solution.py:692
  206.7 2.3 %collective-permute-done.23.refs_6_ = f32[32,128]{1,0:T(8,128)S(1)} collective-permute-done((f32[32,128]{1,0:T(8,128)S(1)}, f32[32,128]{1,0:T(8,128)S(1)}, u32[]{:S(2)}, u32[]{:S(2)}) %collective-permute-start.23) | collective-permute-done | bytes 16416 | tf_op jit(solution)/shard_map/ppermute | solution.py:870
  209.5 2.6 %shard_map.90 = f32[32,64,512]{2,1,0:T(8,128)} custom-call(f32[64,24,512]{2,1,0:T(8,128)S(1)} %get-tuple-element.81.refs_0_.refs_2_, f32[64,24,512]{2,1,0:T(8,128)S(1)} %get-tuple-element.100.refs_0_.refs_1_, f32[64,8,512]{2,1,0:T(8,128)S(1)} %get-tuple-element.94.refs_0_.refs_3_.refs_2_, f32[64,8,512]{2,1,0:T(8,128)S(1)} %get-tuple-element.101.refs_1_.refs_3_, ...), custom_call_target="tpu_custom_call" | custom-call | tf_op jit(solution)/shard_map/pallas_call | solution.py:855
  (85 shorter events, 29.9 us)
Async XLA Ops:
  2.6 80.3 %collective-permute-start.3 = (f32[32,32,128]{2,1,0:T(8,128)}, f32[32,32,128]{2,1,0:T(8,128)S(1)}, u32[]{:S(2)}, u32[]{:S(2)}) collective-permute-start(f32[32,32,128]{2,1,0:T(8,128)} %get-tuple-element.68), channel_id=1, source_target_pairs={{0,4},{1,5},{2,6},{3,7},{4,0},{5,1},{6,2},{7,3},{8,12},{9,13},{10,... | collective-permute-start | bytes 1572872 | tf_op jit(solution)/shard_map/ppermute | solution.py:878
  5.2 77.8 %collective-permute-start.4 = (f32[32,32,128]{2,1,0:T(8,128)}, f32[32,32,128]{2,1,0:T(8,128)S(1)}, u32[]{:S(2)}, u32[]{:S(2)}) collective-permute-start(f32[32,32,128]{2,1,0:T(8,128)} %get-tuple-element.69), channel_id=1, source_target_pairs={{0,5},{1,4},{2,7},{3,6},{4,1},{5,0},{6,3},{7,2},{8,13},{9,12},{10,... | collective-permute-start | bytes 1572872 | tf_op jit(solution)/shard_map/ppermute | solution.py:878
  9.1 75.5 %collective-permute-start.5 = (f32[32,32,128]{2,1,0:T(8,128)}, f32[32,32,128]{2,1,0:T(8,128)S(1)}, u32[]{:S(2)}, u32[]{:S(2)}) collective-permute-start(f32[32,32,128]{2,1,0:T(8,128)} %get-tuple-element.70), channel_id=1, source_target_pairs={{0,6},{1,7},{2,4},{3,5},{4,2},{5,3},{6,0},{7,1},{8,14},{9,15},{10,... | collective-permute-start | bytes 1572872 | tf_op jit(solution)/shard_map/ppermute | solution.py:878
  14.1 37.8 %collective-permute-start = (f32[32,32,128]{2,1,0:T(8,128)}, f32[32,32,128]{2,1,0:T(8,128)S(1)}, u32[]{:S(2)}, u32[]{:S(2)}) collective-permute-start(f32[32,32,128]{2,1,0:T(8,128)} %get-tuple-element.56), channel_id=1, source_target_pairs={{0,1},{1,0},{2,3},{3,2},{4,5},{5,4},{6,7},{7,6},{8,9},{9,8},{10,11... | collective-permute-start | bytes 1572872 | tf_op jit(solution)/shard_map/ppermute | solution.py:878
  14.6 36.7 %collective-permute-start.1 = (f32[32,32,128]{2,1,0:T(8,128)}, f32[32,32,128]{2,1,0:T(8,128)S(1)}, u32[]{:S(2)}, u32[]{:S(2)}) collective-permute-start(f32[32,32,128]{2,1,0:T(8,128)} %get-tuple-element.57), channel_id=1, source_target_pairs={{0,2},{1,3},{2,0},{3,1},{4,6},{5,7},{6,4},{7,5},{8,10},{9,11},{10,... | collective-permute-start | bytes 1572872 | tf_op jit(solution)/shard_map/ppermute | solution.py:878
  51.3 31.5 %collective-permute-start.2 = (f32[32,32,128]{2,1,0:T(8,128)}, f32[32,32,128]{2,1,0:T(8,128)S(1)}, u32[]{:S(2)}, u32[]{:S(2)}) collective-permute-start(f32[32,32,128]{2,1,0:T(8,128)} %get-tuple-element.60), channel_id=1, source_target_pairs={{0,3},{1,2},{2,1},{3,0},{4,7},{5,6},{6,5},{7,4},{8,11},{9,10},{10,... | collective-permute-start | bytes 1572872 | tf_op jit(solution)/shard_map/ppermute | solution.py:878
  51.9 44.1 %collective-permute-start.6 = (f32[32,32,128]{2,1,0:T(8,128)}, f32[32,32,128]{2,1,0:T(8,128)S(1)}, u32[]{:S(2)}, u32[]{:S(2)}) collective-permute-start(f32[32,32,128]{2,1,0:T(8,128)} %get-tuple-element.71), channel_id=1, source_target_pairs={{0,7},{1,6},{2,5},{3,4},{4,3},{5,2},{6,1},{7,0},{8,15},{9,14},{10,... | collective-permute-start | bytes 1572872 | tf_op jit(solution)/shard_map/ppermute | solution.py:878
  98.2 29.1 %collective-permute-start.10 = (f32[32,24,128]{2,1,0:T(8,128)S(1)}, f32[32,24,128]{2,1,0:T(8,128)S(1)}, u32[]{:S(2)}, u32[]{:S(2)}) collective-permute-start(f32[32,24,128]{2,1,0:T(8,128)S(1)} %get-tuple-element.77), channel_id=1, source_target_pairs={{0,4},{1,5},{2,6},{3,7},{4,0},{5,1},{6,2},{7,3},{8,12},{9,13},{10,... | collective-permute-start | bytes 1179656 | tf_op jit(solution)/shard_map/ppermute | solution.py:878
  101.0 34.7 %collective-permute-start.11 = (f32[32,24,128]{2,1,0:T(8,128)S(1)}, f32[32,24,128]{2,1,0:T(8,128)S(1)}, u32[]{:S(2)}, u32[]{:S(2)}) collective-permute-start(f32[32,24,128]{2,1,0:T(8,128)S(1)} %get-tuple-element.78), channel_id=1, source_target_pairs={{0,5},{1,4},{2,7},{3,6},{4,1},{5,0},{6,3},{7,2},{8,13},{9,12},{10,... | collective-permute-start | bytes 1179656 | tf_op jit(solution)/shard_map/ppermute | solution.py:878
  104.1 68.2 %collective-permute-start.7 = (f32[32,32,128]{2,1,0:T(8,128)S(1)}, f32[32,32,128]{2,1,0:T(8,128)S(1)}, u32[]{:S(2)}, u32[]{:S(2)}) collective-permute-start(f32[32,32,128]{2,1,0:T(8,128)S(1)} %get-tuple-element.74), channel_id=1, source_target_pairs={{0,1},{1,0},{2,3},{3,2},{4,5},{5,4},{6,7},{7,6},{8,9},{9,8},{10,11... | collective-permute-start | bytes 1572872 | tf_op jit(solution)/shard_map/ppermute | solution.py:878
  105.4 69.3 %collective-permute-start.8 = (f32[32,32,128]{2,1,0:T(8,128)S(1)}, f32[32,32,128]{2,1,0:T(8,128)S(1)}, u32[]{:S(2)}, u32[]{:S(2)}) collective-permute-start(f32[32,32,128]{2,1,0:T(8,128)S(1)} %get-tuple-element.75), channel_id=1, source_target_pairs={{0,2},{1,3},{2,0},{3,1},{4,6},{5,7},{6,4},{7,5},{8,10},{9,11},{10,... | collective-permute-start | bytes 1572872 | tf_op jit(solution)/shard_map/ppermute | solution.py:878
  106.6 69.1 %collective-permute-start.9 = (f32[32,32,128]{2,1,0:T(8,128)S(1)}, f32[32,32,128]{2,1,0:T(8,128)S(1)}, u32[]{:S(2)}, u32[]{:S(2)}) collective-permute-start(f32[32,32,128]{2,1,0:T(8,128)S(1)} %get-tuple-element.76), channel_id=1, source_target_pairs={{0,3},{1,2},{2,1},{3,0},{4,7},{5,6},{6,5},{7,4},{8,11},{9,10},{10,... | collective-permute-start | bytes 1572872 | tf_op jit(solution)/shard_map/ppermute | solution.py:878
  127.3 33.7 %collective-permute-start.12 = (f32[32,24,128]{2,1,0:T(8,128)S(1)}, f32[32,24,128]{2,1,0:T(8,128)S(1)}, u32[]{:S(2)}, u32[]{:S(2)}) collective-permute-start(f32[32,24,128]{2,1,0:T(8,128)S(1)} %get-tuple-element.79), channel_id=1, source_target_pairs={{0,6},{1,7},{2,4},{3,5},{4,2},{5,3},{6,0},{7,1},{8,14},{9,15},{10,... | collective-permute-start | bytes 1179656 | tf_op jit(solution)/shard_map/ppermute | solution.py:878
  135.7 36.6 %collective-permute-start.13 = (f32[32,24,128]{2,1,0:T(8,128)S(1)}, f32[32,24,128]{2,1,0:T(8,128)S(1)}, u32[]{:S(2)}, u32[]{:S(2)}) collective-permute-start(f32[32,24,128]{2,1,0:T(8,128)S(1)} %get-tuple-element.80), channel_id=1, source_target_pairs={{0,7},{1,6},{2,5},{3,4},{4,3},{5,2},{6,1},{7,0},{8,15},{9,14},{10,... | collective-permute-start | bytes 1179656 | tf_op jit(solution)/shard_map/ppermute | solution.py:878
  161.0 24.4 %collective-permute-start.14 = (f32[32,8,128]{2,1,0:T(8,128)S(1)}, f32[32,8,128]{2,1,0:T(8,128)S(1)}, u32[]{:S(2)}, u32[]{:S(2)}) collective-permute-start(f32[32,8,128]{2,1,0:T(8,128)S(1)} %get-tuple-element.89), channel_id=1, source_target_pairs={{0,4},{1,5},{2,6},{3,7},{4,0},{5,1},{6,2},{7,3},{8,12},{9,13},{10,... | collective-permute-start | bytes 393224 | tf_op jit(solution)/shard_map/ppermute | solution.py:878
  172.3 14.0 %collective-permute-start.15 = (f32[32,8,128]{2,1,0:T(8,128)S(1)}, f32[32,8,128]{2,1,0:T(8,128)S(1)}, u32[]{:S(2)}, u32[]{:S(2)}) collective-permute-start(f32[32,8,128]{2,1,0:T(8,128)S(1)} %get-tuple-element.90), channel_id=1, source_target_pairs={{0,5},{1,4},{2,7},{3,6},{4,1},{5,0},{6,3},{7,2},{8,13},{9,12},{10,... | collective-permute-start | bytes 393224 | tf_op jit(solution)/shard_map/ppermute | solution.py:878
  172.3 17.9 %collective-permute-start.16 = (f32[32,8,128]{2,1,0:T(8,128)S(1)}, f32[32,8,128]{2,1,0:T(8,128)S(1)}, u32[]{:S(2)}, u32[]{:S(2)}) collective-permute-start(f32[32,8,128]{2,1,0:T(8,128)S(1)} %get-tuple-element.91), channel_id=1, source_target_pairs={{0,6},{1,7},{2,4},{3,5},{4,2},{5,3},{6,0},{7,1},{8,14},{9,15},{10,... | collective-permute-start | bytes 393224 | tf_op jit(solution)/shard_map/ppermute | solution.py:878
  174.7 17.1 %collective-permute-start.17 = (f32[32,8,128]{2,1,0:T(8,128)S(1)}, f32[32,8,128]{2,1,0:T(8,128)S(1)}, u32[]{:S(2)}, u32[]{:S(2)}) collective-permute-start(f32[32,8,128]{2,1,0:T(8,128)S(1)} %get-tuple-element.92), channel_id=1, source_target_pairs={{0,7},{1,6},{2,5},{3,4},{4,3},{5,2},{6,1},{7,0},{8,15},{9,14},{10,... | collective-permute-start | bytes 393224 | tf_op jit(solution)/shard_map/ppermute | solution.py:878
  192.2 4.4 %collective-permute-start.19 = (f32[8,32,128]{2,1,0:T(8,128)S(1)}, f32[8,32,128]{2,1,0:T(8,128)S(1)}, u32[]{:S(2)}, u32[]{:S(2)}) collective-permute-start(f32[8,32,128]{2,1,0:T(8,128)S(1)} %get-tuple-element.98), channel_id=1, source_target_pairs={{0,8},{8,16},{16,24},{24,0},{1,9},{9,17},{17,25},{25,1},{2,10},{10... | collective-permute-start | bytes 393224 | tf_op jit(solution)/shard_map/ppermute | solution.py:870
  192.3 4.8 %collective-permute-start.18 = (f32[8,32,128]{2,1,0:T(8,128)S(1)}, f32[8,32,128]{2,1,0:T(8,128)S(1)}, u32[]{:S(2)}, u32[]{:S(2)}) collective-permute-start(f32[8,32,128]{2,1,0:T(8,128)S(1)} %get-tuple-element.98), channel_id=1, source_target_pairs={{0,24},{8,0},{16,8},{24,16},{1,25},{9,1},{17,9},{25,17},{2,26},{10... | collective-permute-start | bytes 393224 | tf_op jit(solution)/shard_map/ppermute | solution.py:870
  197.7 6.7 %collective-permute-start.21 = (f32[8,32,128]{2,1,0:T(8,128)S(1)}, f32[8,32,128]{2,1,0:T(8,128)S(1)}, u32[]{:S(2)}, u32[]{:S(2)}) collective-permute-start(f32[8,32,128]{2,1,0:T(8,128)S(1)} %get-tuple-element.102), channel_id=1, source_target_pairs={{0,8},{8,16},{16,24},{24,0},{1,9},{9,17},{17,25},{25,1},{2,10},{10... | collective-permute-start | bytes 393224 | tf_op jit(solution)/shard_map/ppermute | solution.py:870
  198.9 5.5 %collective-permute-start.20 = (f32[8,32,128]{2,1,0:T(8,128)S(1)}, f32[8,32,128]{2,1,0:T(8,128)S(1)}, u32[]{:S(2)}, u32[]{:S(2)}) collective-permute-start(f32[8,32,128]{2,1,0:T(8,128)S(1)} %get-tuple-element.102), channel_id=1, source_target_pairs={{0,24},{8,0},{16,8},{24,16},{1,25},{9,1},{17,9},{25,17},{2,26},{10... | collective-permute-start | bytes 393224 | tf_op jit(solution)/shard_map/ppermute | solution.py:870
  205.2 3.7 %collective-permute-start.23 = (f32[32,128]{1,0:T(8,128)S(1)}, f32[32,128]{1,0:T(8,128)S(1)}, u32[]{:S(2)}, u32[]{:S(2)}) collective-permute-start(f32[32,128]{1,0:T(8,128)S(1)} %shard_map.89.refs_4_), channel_id=1, source_target_pairs={{0,16},{8,24},{16,0},{24,8},{1,17},{9,25},{17,1},{25,9},{2,18},{10... | collective-permute-start | bytes 49160 | tf_op jit(solution)/shard_map/ppermute | solution.py:870
  206.4 3.2 %collective-permute-start.22 = (f32[32,128]{1,0:T(8,128)S(1)}, f32[32,128]{1,0:T(8,128)S(1)}, u32[]{:S(2)}, u32[]{:S(2)}) collective-permute-start(f32[32,128]{1,0:T(8,128)S(1)} %shard_map.89.refs_4_), channel_id=1, source_target_pairs={{0,8},{8,16},{16,24},{24,0},{1,9},{9,17},{17,25},{25,1},{2,10},{10... | collective-permute-start | bytes 49160 | tf_op jit(solution)/shard_map/ppermute | solution.py:870
  (9 other events, 269.6 us)

commit v8 on v7

--- a/solution.py
+++ b/solution.py
@@ -937,6 +937,7 @@
     near_sent = pack(index, concentration, fold, groups, 0, half)
     near_field = exchanged(near_sent)
     near_field[2], far_sent[-1] = lax.optimization_barrier((near_field[2], far_sent[-1]))
+    near_field[1], far_sent[2] = lax.optimization_barrier((near_field[1], far_sent[2]))
     far_field = exchanged(far_sent, half)
     halves, pieces = transform_tables(planes * groups, planes)
     last = lax.dynamic_index_in_dim(pieces, me ^ (groups - 1), 0, keepdims=False)
@@ -945,7 +946,8 @@
     )
     local, far, mask, edges = tables
     near = some_terms(index, mine, near_field, fold, 0, half)
-    far_terms = some_terms(index, mine, far_field[:-1], fold, half, half, clear=True)
+    near, *some_far = lax.optimization_barrier((near, *far_field[:-1]))
+    far_terms = some_terms(index, mine, some_far, fold, half, half, clear=True)
     sizes = [planes - 8, 8] if planes > 16 else [planes]
     partial = partial_modes(index, halves, near, far_terms, half, planes, 1)
     sent, terms = far_modes(index, mine, last, partial, far_field[-1], fold, half, sizes)

time: 213 us -> 212 us (level)
  waiting for transfers between devices: 133 us -> 130 us
  starting transfers between devices: 25.7 us -> 28 us
    ppermute x18, waiting for transfers between devices: 129 us -> 126 us  [exchanged(): lax.ppermute(value, 'gz', [(i, i ^ d) for i in range(size)])]
    ppermute x18, starting transfers between devices: 20.1 us -> 22.5 us  [exchanged(): lax.ppermute(value, 'gz', [(i, i ^ d) for i in range(size)])]
where the time goes in v8:
time: 212 us
  waiting for transfers between devices  130 us (61%)
  Pallas kernels  44.5 us (21%)
  starting transfers between devices  28 us (13%)
  other arithmetic  7.66 us (4%)
    ppermute x18, waiting for transfers between devices, exchanged(): lax.ppermute(value, 'gz', [(i, i ^ d) for i in range(size)])  126 us
    ppermute x18, starting transfers between devices, exchanged(): lax.ppermute(value, 'gz', [(i, i ^ d) for i in range(size)])  22.5 us
    pallas_call x3, Pallas kernels, apply_local(): pl.pallas_call(functools.partial(apply_kernel, want_image, len(fields), f...  14.2 us
    pallas_call x3, Pallas kernels, pack(): pl.pallas_call(functools.partial(pack_kernel, fold), grid_spec=pltpu.Pref...  8.69 us
    pallas_call x2, Pallas kernels, some_terms(): pl.pallas_call(functools.partial(terms_kernel, fold, first, count, clear)...  8.53 us
    convert_element_type x1, other arithmetic, edge_tables(): local = (source == place[None, :]).astype(jnp.bfloat16)  7.47 us
    ppermute x7, starting transfers between devices, shifted(): lax.ppermute(value, axis, [(i, (i + steps) % size) for i in range(size)])  5.54 us
  transfers between devices with their start and end apart: 25, of which 16 were waited for; matrix products, arithmetic and copies ran while one was open for 4% of the time, Pallas kernels for 17%

profile of v8, /device:TPU:8, one launch (start us, length us, event | category | flops | bytes accessed | tf_op | source)
XLA Modules:
  0.0 212.0 jit_solution(11514764876624005681)
XLA Ops:
  0.0 2.6 %shard_map.76 = (f32[32,32,128]{2,1,0:T(8,128)}, f32[32,32,128]{2,1,0:T(8,128)}) custom-call(s32[1]{0:T(128)} %bitcast.me_ref, f32[32,64,512]{2,1,0:T(8,128)} %c_ref.5), custom_call_target="tpu_custom_call" | custom-call | flops 1048576 | bytes 4194304 | tf_op jit(solution)/shard_map/pallas_call | solution.py:204
  2.7 2.6 %collective-permute-start.3 = (f32[32,32,128]{2,1,0:T(8,128)}, f32[32,32,128]{2,1,0:T(8,128)S(1)}, u32[]{:S(2)}, u32[]{:S(2)}) collective-permute-start(f32[32,32,128]{2,1,0:T(8,128)} %get-tuple-element.76), channel_id=1, source_target_pairs={{0,4},{1,5},{2,6},{3,7},{4,0},{5,1},{6,2},{7,3},{8,12},{9,13},{10,... | collective-permute-start | bytes 1572872 | tf_op jit(solution)/shard_map/ppermute | solution.py:878
  6.5 3.4 %shard_map.73 = (f32[32,32,128]{2,1,0:T(8,128)}, f32[32,32,128]{2,1,0:T(8,128)}, f32[32,32,128]{2,1,0:T(8,128)}, f32[32,32,128]{2,1,0:T(8,128)}) custom-call(s32[1]{0:T(128)} %bitcast.me_ref, f32[32,64,512]{2,1,0:T(8,128)} %c_ref.5), custom_call_target="tpu_custom_call" | custom-call | flops 1048576 | bytes 4194304 | tf_op jit(solution)/shard_map/pallas_call | solution.py:204
  10.6 2.8 %collective-permute-start.2 = (f32[32,32,128]{2,1,0:T(8,128)}, f32[32,32,128]{2,1,0:T(8,128)S(1)}, u32[]{:S(2)}, u32[]{:S(2)}) collective-permute-start(f32[32,32,128]{2,1,0:T(8,128)} %get-tuple-element.68), channel_id=1, source_target_pairs={{0,3},{1,2},{2,1},{3,0},{4,7},{5,6},{6,5},{7,4},{8,11},{9,10},{10,... | collective-permute-start | bytes 1572872 | tf_op jit(solution)/shard_map/ppermute | solution.py:878
  13.8 7.5 %fusion.refs_4_.refs_6_ = bf16[2048,2048]{1,0:T(8,128)(2,1)} fusion(s32[2048]{0:T(1024)S(1)} %bitcast.22), kind=kLoop, calls=%fused_computation.1 | loop fusion | flops 8388608 | bytes 8396800 | tf_op jit(solution)/shard_map/convert_element_type | solution.py:901
  21.3 2.6 %shard_map.74 = (f32[32,32,128]{2,1,0:T(8,128)}, f32[32,32,128]{2,1,0:T(8,128)}) custom-call(s32[1]{0:T(128)} %bitcast.me_ref, f32[32,64,512]{2,1,0:T(8,128)} %c_ref.5), custom_call_target="tpu_custom_call" | custom-call | flops 1048576 | bytes 4194304 | tf_op jit(solution)/shard_map/pallas_call | solution.py:204
  24.0 10.5 %collective-permute-done.refs_1_ = f32[32,32,128]{2,1,0:T(8,128)S(1)} collective-permute-done((f32[32,32,128]{2,1,0:T(8,128)}, f32[32,32,128]{2,1,0:T(8,128)S(1)}, u32[]{:S(2)}, u32[]{:S(2)}) %collective-permute-start) | collective-permute-done | bytes 524320 | tf_op jit(solution)/shard_map/ppermute | solution.py:878
  36.0 5.2 %collective-permute-done.1.refs_2_ = f32[32,32,128]{2,1,0:T(8,128)S(1)} collective-permute-done((f32[32,32,128]{2,1,0:T(8,128)}, f32[32,32,128]{2,1,0:T(8,128)S(1)}, u32[]{:S(2)}, u32[]{:S(2)}) %collective-permute-start.1) | collective-permute-done | bytes 524320 | tf_op jit(solution)/shard_map/ppermute | solution.py:878
  43.6 33.0 %collective-permute-done.2.refs_3_ = f32[32,32,128]{2,1,0:T(8,128)S(1)} collective-permute-done((f32[32,32,128]{2,1,0:T(8,128)}, f32[32,32,128]{2,1,0:T(8,128)S(1)}, u32[]{:S(2)}, u32[]{:S(2)}) %collective-permute-start.2) | collective-permute-done | bytes 524320 | tf_op jit(solution)/shard_map/ppermute | solution.py:878
  76.7 4.8 %shard_map.75.near_ref = bf16[16,512,256]{2,1,0:T(8,128)(2,1)S(1)} custom-call(s32[1]{0:T(128)} %bitcast.me_ref, f32[8,128]{1,0:T(8,128)S(1)} %tile.10.geo_ref, f32[32,32,128]{2,1,0:T(8,128)S(1)} %copy-done.1, f32[32,32,128]{2,1,0:T(8,128)S(1)} %collective-permute-done.refs_1_, f32[32,32,128]{2,1,0:T(8,128)S(1)} %collective-permute-done.1.refs_2_, ...), custom_call_target="tpu_custom_call" | custom-call | flops 41943040 | bytes 6291456 | tf_op jit(solution)/shard_map/pallas_call | solution.py:361
  81.6 3.1 %collective-permute-done.5.refs_2_ = f32[32,32,128]{2,1,0:T(8,128)S(1)} collective-permute-done((f32[32,32,128]{2,1,0:T(8,128)}, f32[32,32,128]{2,1,0:T(8,128)S(1)}, u32[]{:S(2)}, u32[]{:S(2)}) %collective-permute-start.5) | collective-permute-done | bytes 524320 | tf_op jit(solution)/shard_map/ppermute | solution.py:878
  84.7 3.7 %shard_map.77.far_ref = bf16[16,512,256]{2,1,0:T(8,128)(2,1)S(1)} custom-call(s32[1]{0:T(128)} %bitcast.me_ref, f32[8,128]{1,0:T(8,128)S(1)} %tile.10.geo_ref, f32[32,32,128]{2,1,0:T(8,128)S(1)} %collective-permute-done.3.refs_0_, f32[32,32,128]{2,1,0:T(8,128)S(1)} %collective-permute-done.4.refs_1_, f32[32,32,128]{2,1,0:T(8,128)S(1)} %collective-permute-done.5.refs_2_), custom_call_target="tpu_custom_call" | custom-call | flops 31457280 | bytes 4718592 | tf_op jit(solution)/shard_map/pallas_call | solution.py:361
  90.2 5.9 %collective-permute-done.6.y_ref = f32[32,32,128]{2,1,0:T(8,128)S(1)} collective-permute-done((f32[32,32,128]{2,1,0:T(8,128)}, f32[32,32,128]{2,1,0:T(8,128)S(1)}, u32[]{:S(2)}, u32[]{:S(2)}) %collective-permute-start.6) | collective-permute-done | bytes 524320 | tf_op jit(solution)/shard_map/ppermute | solution.py:878
  98.2 3.1 %collective-permute-start.11 = (f32[32,24,128]{2,1,0:T(8,128)S(1)}, f32[32,24,128]{2,1,0:T(8,128)S(1)}, u32[]{:S(2)}, u32[]{:S(2)}) collective-permute-start(f32[32,24,128]{2,1,0:T(8,128)S(1)} %get-tuple-element.90), channel_id=1, source_target_pairs={{0,5},{1,4},{2,7},{3,6},{4,1},{5,0},{6,3},{7,2},{8,13},{9,12},{10,... | collective-permute-start | bytes 1179656 | tf_op jit(solution)/shard_map/ppermute | solution.py:878
  107.5 17.1 %collective-permute-done.10.refs_4_ = f32[32,24,128]{2,1,0:T(8,128)S(1)} collective-permute-done((f32[32,24,128]{2,1,0:T(8,128)S(1)}, f32[32,24,128]{2,1,0:T(8,128)S(1)}, u32[]{:S(2)}, u32[]{:S(2)}) %collective-permute-start.10) | collective-permute-done | bytes 393248 | tf_op jit(solution)/shard_map/ppermute | solution.py:878
  125.9 7.2 %collective-permute-done.11.refs_5_ = f32[32,24,128]{2,1,0:T(8,128)S(1)} collective-permute-done((f32[32,24,128]{2,1,0:T(8,128)S(1)}, f32[32,24,128]{2,1,0:T(8,128)S(1)}, u32[]{:S(2)}, u32[]{:S(2)}) %collective-permute-start.11) | collective-permute-done | bytes 393248 | tf_op jit(solution)/shard_map/ppermute | solution.py:878
  135.2 24.8 %collective-permute-done.12.refs_6_ = f32[32,24,128]{2,1,0:T(8,128)S(1)} collective-permute-done((f32[32,24,128]{2,1,0:T(8,128)S(1)}, f32[32,24,128]{2,1,0:T(8,128)S(1)}, u32[]{:S(2)}, u32[]{:S(2)}) %collective-permute-start.12) | collective-permute-done | bytes 393248 | tf_op jit(solution)/shard_map/ppermute | solution.py:878
  160.0 12.2 %collective-permute-done.13.refs_7_ = f32[32,24,128]{2,1,0:T(8,128)S(1)} collective-permute-done((f32[32,24,128]{2,1,0:T(8,128)S(1)}, f32[32,24,128]{2,1,0:T(8,128)S(1)}, u32[]{:S(2)}, u32[]{:S(2)}) %collective-permute-start.13) | collective-permute-done | bytes 393248 | tf_op jit(solution)/shard_map/ppermute | solution.py:878
  175.4 7.1 %shard_map.83 = (f32[64,24,512]{2,1,0:T(8,128)S(1)}, f32[2,24,128]{2,1,0:T(8,128)S(1)}) custom-call(f32[64,24,512]{2,1,0:T(8,128)S(1)} %get-tuple-element.93.refs_0_.refs_2_, f32[8,512]{1,0:T(8,128)S(1)} %select_maximum_fusion.refs_1_.geo_ref.refs_3_, f32[32,128]{1,0:T(8,128)S(1)} %broadcast_in_dim.25.refs_2_.mass_ref.refs_4_, ...), custom_call_target="tpu_custom_call" | custom-call | flops 1 | bytes 1 | tf_op jit(solution)/shard_map/pallas_call | solution.py:692
  184.0 4.1 %collective-permute-done.16.refs_6_ = f32[32,8,128]{2,1,0:T(8,128)S(1)} collective-permute-done((f32[32,8,128]{2,1,0:T(8,128)S(1)}, f32[32,8,128]{2,1,0:T(8,128)S(1)}, u32[]{:S(2)}, u32[]{:S(2)}) %collective-permute-start.16) | collective-permute-done | bytes 131104 | tf_op jit(solution)/shard_map/ppermute | solution.py:878
  188.1 3.4 %collective-permute-done.17.refs_7_ = f32[32,8,128]{2,1,0:T(8,128)S(1)} collective-permute-done((f32[32,8,128]{2,1,0:T(8,128)S(1)}, f32[32,8,128]{2,1,0:T(8,128)S(1)}, u32[]{:S(2)}, u32[]{:S(2)}) %collective-permute-start.17) | collective-permute-done | bytes 131104 | tf_op jit(solution)/shard_map/ppermute | solution.py:878
  193.7 2.5 %shard_map.86 = (f32[64,8,512]{2,1,0:T(8,128)S(1)}, f32[2,8,128]{2,1,0:T(8,128)S(1)}) custom-call(f32[64,8,512]{2,1,0:T(8,128)S(1)} %get-tuple-element.106.refs_0_.refs_3_.refs_2_, f32[8,512]{1,0:T(8,128)S(1)} %select_maximum_fusion.refs_1_.geo_ref.refs_3_, f32[32,128]{1,0:T(8,128)S(1)} %broadcast_in_dim.25.refs_2_.mass_ref.refs_4_, ...), custom_call_target="tpu_custom_call" | custom-call | flops 1 | bytes 1 | tf_op jit(solution)/shard_map/pallas_call | solution.py:692
  199.4 4.7 %shard_map.88.refs_7_ = f32[2,32,128]{2,1,0:T(8,128)S(1)} custom-call(f32[64,24,512]{2,1,0:T(8,128)S(1)} %get-tuple-element.112.refs_0_.refs_1_, f32[64,8,512]{2,1,0:T(8,128)S(1)} %get-tuple-element.113.refs_1_.refs_3_, f32[2,24,128]{2,1,0:T(8,128)S(1)} %shard_map.84.refs_2_, f32[8,512]{1,0:T(8,128)S(1)} %select_maximum_fusion.refs_1_.geo_ref.refs_3_, ...), custom_call_target="tpu_custom_call" | custom-call | flops 1 | bytes 1 | tf_op jit(solution)/shard_map/pallas_call | solution.py:692
  209.2 2.6 %shard_map.90 = f32[32,64,512]{2,1,0:T(8,128)} custom-call(f32[64,24,512]{2,1,0:T(8,128)S(1)} %get-tuple-element.93.refs_0_.refs_2_, f32[64,24,512]{2,1,0:T(8,128)S(1)} %get-tuple-element.112.refs_0_.refs_1_, f32[64,8,512]{2,1,0:T(8,128)S(1)} %get-tuple-element.106.refs_0_.refs_3_.refs_2_, f32[64,8,512]{2,1,0:T(8,128)S(1)} %get-tuple-element.113.refs_1_.refs_3_, ...), custom_call_target="tpu_custom_call" | custom-call | tf_op jit(solution)/shard_map/pallas_call | solution.py:855
  (85 shorter events, 35.1 us)
Async XLA Ops:
  2.7 78.9 %collective-permute-start.3 = (f32[32,32,128]{2,1,0:T(8,128)}, f32[32,32,128]{2,1,0:T(8,128)S(1)}, u32[]{:S(2)}, u32[]{:S(2)}) collective-permute-start(f32[32,32,128]{2,1,0:T(8,128)} %get-tuple-element.76), channel_id=1, source_target_pairs={{0,4},{1,5},{2,6},{3,7},{4,0},{5,1},{6,2},{7,3},{8,12},{9,13},{10,... | collective-permute-start | bytes 1572872 | tf_op jit(solution)/shard_map/ppermute | solution.py:878
  5.3 76.3 %collective-permute-start.4 = (f32[32,32,128]{2,1,0:T(8,128)}, f32[32,32,128]{2,1,0:T(8,128)S(1)}, u32[]{:S(2)}, u32[]{:S(2)}) collective-permute-start(f32[32,32,128]{2,1,0:T(8,128)} %get-tuple-element.77), channel_id=1, source_target_pairs={{0,5},{1,4},{2,7},{3,6},{4,1},{5,0},{6,3},{7,2},{8,13},{9,12},{10,... | collective-permute-start | bytes 1572872 | tf_op jit(solution)/shard_map/ppermute | solution.py:878
  9.9 24.5 %collective-permute-start = (f32[32,32,128]{2,1,0:T(8,128)}, f32[32,32,128]{2,1,0:T(8,128)S(1)}, u32[]{:S(2)}, u32[]{:S(2)}) collective-permute-start(f32[32,32,128]{2,1,0:T(8,128)} %get-tuple-element.62), channel_id=1, source_target_pairs={{0,1},{1,0},{2,3},{3,2},{4,5},{5,4},{6,7},{7,6},{8,9},{9,8},{10,11... | collective-permute-start | bytes 1572872 | tf_op jit(solution)/shard_map/ppermute | solution.py:878
  10.4 30.8 %collective-permute-start.1 = (f32[32,32,128]{2,1,0:T(8,128)}, f32[32,32,128]{2,1,0:T(8,128)S(1)}, u32[]{:S(2)}, u32[]{:S(2)}) collective-permute-start(f32[32,32,128]{2,1,0:T(8,128)} %get-tuple-element.65), channel_id=1, source_target_pairs={{0,2},{1,3},{2,0},{3,1},{4,6},{5,7},{6,4},{7,5},{8,10},{9,11},{10,... | collective-permute-start | bytes 1572872 | tf_op jit(solution)/shard_map/ppermute | solution.py:878
  10.6 65.9 %collective-permute-start.2 = (f32[32,32,128]{2,1,0:T(8,128)}, f32[32,32,128]{2,1,0:T(8,128)S(1)}, u32[]{:S(2)}, u32[]{:S(2)}) collective-permute-start(f32[32,32,128]{2,1,0:T(8,128)} %get-tuple-element.68), channel_id=1, source_target_pairs={{0,3},{1,2},{2,1},{3,0},{4,7},{5,6},{6,5},{7,4},{8,11},{9,10},{10,... | collective-permute-start | bytes 1572872 | tf_op jit(solution)/shard_map/ppermute | solution.py:878
  34.5 50.2 %collective-permute-start.5 = (f32[32,32,128]{2,1,0:T(8,128)}, f32[32,32,128]{2,1,0:T(8,128)S(1)}, u32[]{:S(2)}, u32[]{:S(2)}) collective-permute-start(f32[32,32,128]{2,1,0:T(8,128)} %get-tuple-element.78), channel_id=1, source_target_pairs={{0,6},{1,7},{2,4},{3,5},{4,2},{5,3},{6,0},{7,1},{8,14},{9,15},{10,... | collective-permute-start | bytes 1572872 | tf_op jit(solution)/shard_map/ppermute | solution.py:878
  41.3 54.8 %collective-permute-start.6 = (f32[32,32,128]{2,1,0:T(8,128)}, f32[32,32,128]{2,1,0:T(8,128)S(1)}, u32[]{:S(2)}, u32[]{:S(2)}) collective-permute-start(f32[32,32,128]{2,1,0:T(8,128)} %get-tuple-element.83), channel_id=1, source_target_pairs={{0,7},{1,6},{2,5},{3,4},{4,3},{5,2},{6,1},{7,0},{8,15},{9,14},{10,... | collective-permute-start | bytes 1572872 | tf_op jit(solution)/shard_map/ppermute | solution.py:878
  98.1 26.5 %collective-permute-start.10 = (f32[32,24,128]{2,1,0:T(8,128)S(1)}, f32[32,24,128]{2,1,0:T(8,128)S(1)}, u32[]{:S(2)}, u32[]{:S(2)}) collective-permute-start(f32[32,24,128]{2,1,0:T(8,128)S(1)} %get-tuple-element.89), channel_id=1, source_target_pairs={{0,4},{1,5},{2,6},{3,7},{4,0},{5,1},{6,2},{7,3},{8,12},{9,13},{10,... | collective-permute-start | bytes 1179656 | tf_op jit(solution)/shard_map/ppermute | solution.py:878
  98.2 34.9 %collective-permute-start.11 = (f32[32,24,128]{2,1,0:T(8,128)S(1)}, f32[32,24,128]{2,1,0:T(8,128)S(1)}, u32[]{:S(2)}, u32[]{:S(2)}) collective-permute-start(f32[32,24,128]{2,1,0:T(8,128)S(1)} %get-tuple-element.90), channel_id=1, source_target_pairs={{0,5},{1,4},{2,7},{3,6},{4,1},{5,0},{6,3},{7,2},{8,13},{9,12},{10,... | collective-permute-start | bytes 1179656 | tf_op jit(solution)/shard_map/ppermute | solution.py:878
  104.0 68.2 %collective-permute-start.7 = (f32[32,32,128]{2,1,0:T(8,128)S(1)}, f32[32,32,128]{2,1,0:T(8,128)S(1)}, u32[]{:S(2)}, u32[]{:S(2)}) collective-permute-start(f32[32,32,128]{2,1,0:T(8,128)S(1)} %get-tuple-element.86), channel_id=1, source_target_pairs={{0,1},{1,0},{2,3},{3,2},{4,5},{5,4},{6,7},{7,6},{8,9},{9,8},{10,11... | collective-permute-start | bytes 1572872 | tf_op jit(solution)/shard_map/ppermute | solution.py:878
  105.3 66.9 %collective-permute-start.8 = (f32[32,32,128]{2,1,0:T(8,128)S(1)}, f32[32,32,128]{2,1,0:T(8,128)S(1)}, u32[]{:S(2)}, u32[]{:S(2)}) collective-permute-start(f32[32,32,128]{2,1,0:T(8,128)S(1)} %get-tuple-element.87), channel_id=1, source_target_pairs={{0,2},{1,3},{2,0},{3,1},{4,6},{5,7},{6,4},{7,5},{8,10},{9,11},{10,... | collective-permute-start | bytes 1572872 | tf_op jit(solution)/shard_map/ppermute | solution.py:878
  106.5 67.7 %collective-permute-start.9 = (f32[32,32,128]{2,1,0:T(8,128)S(1)}, f32[32,32,128]{2,1,0:T(8,128)S(1)}, u32[]{:S(2)}, u32[]{:S(2)}) collective-permute-start(f32[32,32,128]{2,1,0:T(8,128)S(1)} %get-tuple-element.88), channel_id=1, source_target_pairs={{0,3},{1,2},{2,1},{3,0},{4,7},{5,6},{6,5},{7,4},{8,11},{9,10},{10,... | collective-permute-start | bytes 1572872 | tf_op jit(solution)/shard_map/ppermute | solution.py:878
  124.6 35.4 %collective-permute-start.12 = (f32[32,24,128]{2,1,0:T(8,128)S(1)}, f32[32,24,128]{2,1,0:T(8,128)S(1)}, u32[]{:S(2)}, u32[]{:S(2)}) collective-permute-start(f32[32,24,128]{2,1,0:T(8,128)S(1)} %get-tuple-element.91), channel_id=1, source_target_pairs={{0,6},{1,7},{2,4},{3,5},{4,2},{5,3},{6,0},{7,1},{8,14},{9,15},{10,... | collective-permute-start | bytes 1179656 | tf_op jit(solution)/shard_map/ppermute | solution.py:878
  133.0 39.2 %collective-permute-start.13 = (f32[32,24,128]{2,1,0:T(8,128)S(1)}, f32[32,24,128]{2,1,0:T(8,128)S(1)}, u32[]{:S(2)}, u32[]{:S(2)}) collective-permute-start(f32[32,24,128]{2,1,0:T(8,128)S(1)} %get-tuple-element.92), channel_id=1, source_target_pairs={{0,7},{1,6},{2,5},{3,4},{4,3},{5,2},{6,1},{7,0},{8,15},{9,14},{10,... | collective-permute-start | bytes 1179656 | tf_op jit(solution)/shard_map/ppermute | solution.py:878
  160.0 23.9 %collective-permute-start.14 = (f32[32,8,128]{2,1,0:T(8,128)S(1)}, f32[32,8,128]{2,1,0:T(8,128)S(1)}, u32[]{:S(2)}, u32[]{:S(2)}) collective-permute-start(f32[32,8,128]{2,1,0:T(8,128)S(1)} %get-tuple-element.101), channel_id=1, source_target_pairs={{0,4},{1,5},{2,6},{3,7},{4,0},{5,1},{6,2},{7,3},{8,12},{9,13},{10,... | collective-permute-start | bytes 393224 | tf_op jit(solution)/shard_map/ppermute | solution.py:878
  172.2 11.8 %collective-permute-start.15 = (f32[32,8,128]{2,1,0:T(8,128)S(1)}, f32[32,8,128]{2,1,0:T(8,128)S(1)}, u32[]{:S(2)}, u32[]{:S(2)}) collective-permute-start(f32[32,8,128]{2,1,0:T(8,128)S(1)} %get-tuple-element.102), channel_id=1, source_target_pairs={{0,5},{1,4},{2,7},{3,6},{4,1},{5,0},{6,3},{7,2},{8,13},{9,12},{10,... | collective-permute-start | bytes 393224 | tf_op jit(solution)/shard_map/ppermute | solution.py:878
  172.2 15.9 %collective-permute-start.16 = (f32[32,8,128]{2,1,0:T(8,128)S(1)}, f32[32,8,128]{2,1,0:T(8,128)S(1)}, u32[]{:S(2)}, u32[]{:S(2)}) collective-permute-start(f32[32,8,128]{2,1,0:T(8,128)S(1)} %get-tuple-element.103), channel_id=1, source_target_pairs={{0,6},{1,7},{2,4},{3,5},{4,2},{5,3},{6,0},{7,1},{8,14},{9,15},{10,... | collective-permute-start | bytes 393224 | tf_op jit(solution)/shard_map/ppermute | solution.py:878
  172.2 19.3 %collective-permute-start.17 = (f32[32,8,128]{2,1,0:T(8,128)S(1)}, f32[32,8,128]{2,1,0:T(8,128)S(1)}, u32[]{:S(2)}, u32[]{:S(2)}) collective-permute-start(f32[32,8,128]{2,1,0:T(8,128)S(1)} %get-tuple-element.104), channel_id=1, source_target_pairs={{0,7},{1,6},{2,5},{3,4},{4,3},{5,2},{6,1},{7,0},{8,15},{9,14},{10,... | collective-permute-start | bytes 393224 | tf_op jit(solution)/shard_map/ppermute | solution.py:878
  191.9 4.4 %collective-permute-start.19 = (f32[8,32,128]{2,1,0:T(8,128)S(1)}, f32[8,32,128]{2,1,0:T(8,128)S(1)}, u32[]{:S(2)}, u32[]{:S(2)}) collective-permute-start(f32[8,32,128]{2,1,0:T(8,128)S(1)} %get-tuple-element.110), channel_id=1, source_target_pairs={{0,8},{8,16},{16,24},{24,0},{1,9},{9,17},{17,25},{25,1},{2,10},{10... | collective-permute-start | bytes 393224 | tf_op jit(solution)/shard_map/ppermute | solution.py:870
  192.0 4.8 %collective-permute-start.18 = (f32[8,32,128]{2,1,0:T(8,128)S(1)}, f32[8,32,128]{2,1,0:T(8,128)S(1)}, u32[]{:S(2)}, u32[]{:S(2)}) collective-permute-start(f32[8,32,128]{2,1,0:T(8,128)S(1)} %get-tuple-element.110), channel_id=1, source_target_pairs={{0,24},{8,0},{16,8},{24,16},{1,25},{9,1},{17,9},{25,17},{2,26},{10... | collective-permute-start | bytes 393224 | tf_op jit(solution)/shard_map/ppermute | solution.py:870
  197.3 6.7 %collective-permute-start.21 = (f32[8,32,128]{2,1,0:T(8,128)S(1)}, f32[8,32,128]{2,1,0:T(8,128)S(1)}, u32[]{:S(2)}, u32[]{:S(2)}) collective-permute-start(f32[8,32,128]{2,1,0:T(8,128)S(1)} %get-tuple-element.114), channel_id=1, source_target_pairs={{0,8},{8,16},{16,24},{24,0},{1,9},{9,17},{17,25},{25,1},{2,10},{10... | collective-permute-start | bytes 393224 | tf_op jit(solution)/shard_map/ppermute | solution.py:870
  198.6 5.5 %collective-permute-start.20 = (f32[8,32,128]{2,1,0:T(8,128)S(1)}, f32[8,32,128]{2,1,0:T(8,128)S(1)}, u32[]{:S(2)}, u32[]{:S(2)}) collective-permute-start(f32[8,32,128]{2,1,0:T(8,128)S(1)} %get-tuple-element.114), channel_id=1, source_target_pairs={{0,24},{8,0},{16,8},{24,16},{1,25},{9,1},{17,9},{25,17},{2,26},{10... | collective-permute-start | bytes 393224 | tf_op jit(solution)/shard_map/ppermute | solution.py:870
  204.9 3.7 %collective-permute-start.23 = (f32[32,128]{1,0:T(8,128)S(1)}, f32[32,128]{1,0:T(8,128)S(1)}, u32[]{:S(2)}, u32[]{:S(2)}) collective-permute-start(f32[32,128]{1,0:T(8,128)S(1)} %shard_map.89.refs_4_), channel_id=1, source_target_pairs={{0,16},{8,24},{16,0},{24,8},{1,17},{9,25},{17,1},{25,9},{2,18},{10... | collective-permute-start | bytes 49160 | tf_op jit(solution)/shard_map/ppermute | solution.py:870
  206.0 3.2 %collective-permute-start.22 = (f32[32,128]{1,0:T(8,128)S(1)}, f32[32,128]{1,0:T(8,128)S(1)}, u32[]{:S(2)}, u32[]{:S(2)}) collective-permute-start(f32[32,128]{1,0:T(8,128)S(1)} %shard_map.89.refs_4_), channel_id=1, source_target_pairs={{0,8},{8,16},{16,24},{24,0},{1,9},{9,17},{17,25},{25,1},{2,10},{10... | collective-permute-start | bytes 49160 | tf_op jit(solution)/shard_map/ppermute | solution.py:870
  (9 other events, 272.4 us)
